TPU v7x, 32 devices: a whole 2x2x4 slice. The times are simulated.
32 devices in a mesh: cells: 8 (over z, x), bands: 4 (over y, core).
Axes of the slice: x: 2, y: 2, z: 4, core: 2. Of those that a mesh axis runs over, the one named last changes fastest.
Arguments:
- wavefunctions: bfloat16 [5832, 512], P('cells', 'bands'), may hold values from -6 to 6
- hamiltonians: bfloat16 [8, 729, 729], P('cells'), may hold values from -0.21875 to 0.21875
- connectivity: int32 [8, 729], P('cells'), may hold values from 0 to 728, as said below
- face_nodes: int32 [16, 81], P('cells'), may hold values from 0 to 728, as said below
Outputs:
- filtered: float32 [5832, 512], P('cells', 'bands')
- correlation: float32 [512, 512], P(None, 'bands')
Inputs may be any that keep to these rules, and one draw needn't show every extreme that they name: `connectivity`: within each partition the values are a permutation of the local node numbers laid on a lattice: cell c's node (i, j, k), 0 <= i, j, k <= 8, is lattice point (8 c + i, j, k) of the partition, so consecutive cells of a partition share 81 nodes and every local node belongs to some cell. `face_nodes`: row 0 of a partition lists the local numbers of its lattice points with first coordinate 0, row 1 those with first coordinate 8, in the order of the other two coordinates; neighbouring partitions list the same physical face nodes in the same order.
All inputs are finite; a program needn't handle non-finite values.
Results may differ from a plain program's by a relative error of at most 0.0039.
Values may be sent and summed in bfloat16 or wider, within the bound.
No kernel may reach another device: no remote copies, remote signals or barrier semaphores. Data moves between devices by JAX's collectives and lax.ppermute only.
A program may use at most 64 MiB of HBM per device.

v0:
```python
import jax
import jax.numpy as jnp
from jax import lax
from jax.sharding import PartitionSpec as P

NODES_DEV = 729


def with_halo(cells, sides, width):
    for axis, dim in sides:
        count = lax.axis_size(axis)
        ends = count - 1
        head = lax.slice_in_dim(cells, 0, width, axis=dim)
        tail = lax.slice_in_dim(cells, cells.shape[dim] - width, cells.shape[dim], axis=dim)
        cells = jnp.concatenate(
            [
                lax.ppermute(tail, axis, [(i, (i + 1) % count) for i in range(ends)]),
                cells,
                lax.ppermute(head, axis, [((i + 1) % count, i) for i in range(ends)]),
            ],
            axis=dim,
        )
    return cells


def body(wavefunctions, hamiltonians, connectivity, face_nodes):
    node_count = wavefunctions.shape[0]
    band_width = wavefunctions.shape[1]

    def operate(vector):
        cell_rows = vector.astype(jnp.bfloat16)[connectivity]
        cell_terms = jnp.einsum(
            "cij,cjb->cib", hamiltonians, cell_rows, preferred_element_type=jnp.float32
        )
        assembled = jnp.zeros((node_count, band_width), jnp.float32)
        assembled = assembled.at[connectivity.reshape(-1)].add(cell_terms.reshape(-1, band_width))
        face_rows = assembled[face_nodes]
        face_halo = with_halo(face_rows, (("cells", 0),), 1)
        return assembled.at[face_nodes[0]].add(face_halo[0]).at[face_nodes[1]].add(face_halo[3])

    older = wavefunctions.astype(jnp.float32)
    newer = 0.5 * operate(older)
    following = operate(newer) - older
    first_part = lax.axis_index("cells") == 0
    keep_value = jnp.where(first_part, jnp.float32(1.0), jnp.float32(0.0))
    keep_rows = jnp.ones((node_count,), jnp.float32).at[face_nodes[0]].set(keep_value)
    masked = following * keep_rows[:, None]
    high_word = masked.astype(jnp.bfloat16)
    group_count = lax.axis_size("bands")
    pad_rows = -node_count % group_count
    padded_words = jnp.pad(high_word, ((0, pad_rows), (0, 0)))
    node_share = lax.all_to_all(padded_words, "bands", split_axis=0, concat_axis=1, tiled=True)
    full_gram = jnp.dot(node_share.T, node_share, preferred_element_type=jnp.float32)
    partial_gram = lax.psum_scatter(
        full_gram.astype(jnp.bfloat16), "bands", scatter_dimension=1, tiled=True
    ).astype(jnp.float32)
    gram = lax.psum(partial_gram, "cells")
    correlation = gram / (lax.axis_size("cells") * NODES_DEV)
    return (following, correlation)


def solution(mesh):
    placed = (P("cells", "bands"), P("cells", None, None), P("cells", None), P("cells", None))
    return jax.shard_map(
        body,
        mesh=mesh,
        in_specs=placed,
        out_specs=(P("cells", "bands"), P(None, "bands")),
        check_vma=False,
    )
```

profile of v0, /device:TPU:0, one launch (start us, length us, event | category | flops | bytes accessed | tf_op | source)
XLA Modules:
  0.0 134.3 jit_solution(9295224358395896304)
XLA Ops:
  7.2 0.0 copy-start
  7.2 0.0 reduce-scatter.4.cloned.1.call-start
  7.2 0.8 fusion.14
  8.0 0.7 fusion.15
  8.7 0.7 compare_select_fusion.2
  9.4 0.1 reshape.126
  9.5 2.7 %gather_fusion = bf16[729,128]{1,0:T(8,128)(2,1)S(1)} fusion(bf16[729,128]{1,0:T(8,128)(2,1)} %param.4, s32[1024]{0:T(1024)S(1)} %pad_clamp_fusion.1), kind=kCustom, calls=%fused_computation | custom fusion | bytes 376164 | tf_op jit(solution)/shard_map/gather | solution.py:31
  12.2 0.0 copy-done
  12.2 0.0 copy-start.2
  12.2 0.5 convolution_bitcast_fusion.1
  12.7 6.1 %scatter_custom_fusion = f32[729,128]{1,0:T(8,128)S(1)} fusion(s32[729]{0:T(1024)S(1)} %fusion.14, f32[729,128]{1,0:T(8,128)S(1)} %convolution_bitcast_fusion.1, f32[]{:T(128)} %constant.9.clone.1), kind=kCustom, calls=%fused_computation.21 | custom fusion | flops 93312 | bytes 373252 | tf_op jit(solution)/shard_map/scatter-add | solution.py:36
  18.8 0.7 gather_fusion.1
  19.5 1.3 collective-permute-start.1
  20.8 5.5 %collective-permute-start = (f32[1,81,128]{2,1,0:T(8,128)S(1)}, f32[1,81,128]{2,1,0:T(8,128)S(1)}, u32[]{:S(2)}, u32[]{:S(2)}) collective-permute-start(f32[1,81,128]{2,1,0:T(8,128)S(1)} %get-tuple-element.7), channel_id=1, source_target_pairs={{0,4},{4,8},{8,12},{12,16},{16,20},{20,24},{24,28},{1,5},{5,9},{9,... | collective-permute-start | bytes 124424 | tf_op jit(solution)/shard_map/ppermute | solution.py:17
  26.3 0.0 copy-done.2
  26.3 1.7 %collective-permute-done = f32[1,81,128]{2,1,0:T(8,128)S(1)} collective-permute-done((f32[1,81,128]{2,1,0:T(8,128)S(1)}, f32[1,81,128]{2,1,0:T(8,128)S(1)}, u32[]{:S(2)}, u32[]{:S(2)}) %collective-permute-start) | collective-permute-done | bytes 41504 | tf_op jit(solution)/shard_map/ppermute | solution.py:17
  28.0 1.1 scatter_custom_fusion.1
  29.1 0.0 collective-permute-done.1
  29.1 1.1 scatter_custom_fusion.2
  30.3 2.0 %gather_fusion.2 = bf16[729,128]{1,0:T(8,128)(2,1)S(1)} fusion(bf16[729,128]{1,0:T(8,128)(2,1)S(1)} %multiply_convert_fusion.1, s32[1024]{0:T(1024)S(1)} %pad_clamp_fusion.1), kind=kCustom, calls=%fused_computation.2 | custom fusion | bytes 376164 | tf_op jit(solution)/shard_map/gather | solution.py:31
  32.4 0.5 convolution_bitcast_fusion
  32.8 0.0 copy-start.1
  32.8 6.1 %scatter_custom_fusion.3 = f32[729,128]{1,0:T(8,128)S(1)} fusion(s32[729]{0:T(1024)S(1)} %fusion.14, f32[729,128]{1,0:T(8,128)S(1)} %convolution_bitcast_fusion, f32[]{:T(128)} %constant.9.clone.1), kind=kCustom, calls=%fused_computation.19 | custom fusion | flops 93312 | bytes 373252 | tf_op jit(solution)/shard_map/scatter-add | solution.py:36
  39.0 0.7 gather_fusion.3
  39.6 4.8 %collective-permute-start.2 = (f32[1,81,128]{2,1,0:T(8,128)S(1)}, f32[1,81,128]{2,1,0:T(8,128)S(1)}, u32[]{:S(2)}, u32[]{:S(2)}) collective-permute-start(f32[1,81,128]{2,1,0:T(8,128)S(1)} %get-tuple-element.5), channel_id=1, source_target_pairs={{0,4},{4,8},{8,12},{12,16},{16,20},{20,24},{24,28},{1,5},{5,9},{9,... | collective-permute-start | bytes 124424 | tf_op jit(solution)/shard_map/ppermute | solution.py:17
  44.5 1.3 collective-permute-start.3
  45.8 0.8 scatter_custom_fusion.6
  46.6 0.0 collective-permute-done.2
  46.6 1.1 scatter_custom_fusion.4
  47.8 3.9 %collective-permute-done.3 = f32[1,81,128]{2,1,0:T(8,128)S(1)} collective-permute-done((f32[1,81,128]{2,1,0:T(8,128)S(1)}, f32[1,81,128]{2,1,0:T(8,128)S(1)}, u32[]{:S(2)}, u32[]{:S(2)}) %collective-permute-start.3) | collective-permute-done | bytes 41504 | tf_op jit(solution)/shard_map/ppermute | solution.py:19
  51.6 1.1 scatter_custom_fusion.5
  52.8 0.0 copy-done.1
  52.8 0.8 multiply_convert_fusion
  53.6 0.1 all_to_all.14
  53.7 7.8 %all_to_all.19 = bf16[4,183,128]{2,1,0:T(8,128)(2,1)S(1)} all-to-all(bf16[4,183,128]{2,1,0:T(8,128)(2,1)S(1)} %all_to_all.14), channel_id=1, replica_groups=mesh['cells'=8,'bands'=4] {'bands'}, dimensions={0} | all-to-all | bytes 374784 | tf_op jit(solution)/shard_map/all_to_all | solution.py:52
  61.5 0.1 copy.7
  61.6 0.1 pad.9
  61.7 0.3 convolution_convert_fusion
  62.1 1.0 copy.8
  63.1 0.0 reduce-scatter.4.cloned.1.call-update
  63.1 22.5 %reduce-scatter.4.cloned.1.call-done = bf16[128,512]{1,0:T(8,128)(2,1)} async-done(((bf16[512,512]{1,0:T(8,128)(2,1)}), bf16[128,512]{1,0:T(8,128)(2,1)}) %reduce-scatter.4.cloned.1.call-update) | async-done | bytes 131088
  85.6 1.0 copy.9
  86.6 40.1 %all-reduce.2 = f32[512,128]{1,0:T(8,128)S(1)} all-reduce(bf16[512,128]{1,0:T(8,128)(2,1)S(1)} %copy.9), channel_id=1, replica_groups=mesh['cells'=8,'bands'=4] {'cells'}, use_global_device_ids=true, to_apply=%region_8.9 | all-reduce | flops 65536 | bytes 393216 | tf_op jit(solution)/shard_map/psum | solution.py:57
  126.7 0.7 broadcast_multiply_fusion
  (9 shorter events, 0.1 us)
Async XLA Ops:
  7.2 5.1 %copy-start = (bf16[1,729,729]{2,1,0:T(8,128)(2,1)S(1)}, bf16[1,729,729]{2,1,0:T(8,128)(2,1)}, u32[]{:S(2)}) copy-start(bf16[1,729,729]{2,1,0:T(8,128)(2,1)} %param.5) | copy-start | bytes 3188650
  7.2 78.4 %reduce-scatter.4.cloned.1.call-start = ((), (), s32[]{:S(2)}) async-start(), calls=%async_computation.2 | async-start | bytes 655360
  12.2 14.1 %copy-start.2 = (s32[2,81]{1,0:T(2,128)S(1)}, s32[2,81]{1,0:T(2,128)}, u32[]{:S(2)}) copy-start(s32[2,81]{1,0:T(2,128)} %param.7) | copy-start | bytes 1948
  19.5 9.6 %collective-permute-start.1 = (f32[1,81,128]{2,1,0:T(8,128)S(1)}, f32[1,81,128]{2,1,0:T(8,128)S(1)}, u32[]{:S(2)}, u32[]{:S(2)}) collective-permute-start(f32[1,81,128]{2,1,0:T(8,128)S(1)} %get-tuple-element.6), channel_id=1, source_target_pairs={{4,0},{8,4},{12,8},{16,12},{20,16},{24,20},{28,24},{5,1},{9,5},{13... | collective-permute-start | bytes 124424 | tf_op jit(solution)/shard_map/ppermute | solution.py:19
  20.8 7.2 %collective-permute-start = (f32[1,81,128]{2,1,0:T(8,128)S(1)}, f32[1,81,128]{2,1,0:T(8,128)S(1)}, u32[]{:S(2)}, u32[]{:S(2)}) collective-permute-start(f32[1,81,128]{2,1,0:T(8,128)S(1)} %get-tuple-element.7), channel_id=1, source_target_pairs={{0,4},{4,8},{8,12},{12,16},{16,20},{20,24},{24,28},{1,5},{5,9},{9,... | collective-permute-start | bytes 124424 | tf_op jit(solution)/shard_map/ppermute | solution.py:17
  32.8 19.9 %copy-start.1 = (bf16[729,128]{1,0:T(8,128)(2,1)S(1)}, bf16[729,128]{1,0:T(8,128)(2,1)}, u32[]{:S(2)}) copy-start(bf16[729,128]{1,0:T(8,128)(2,1)} %param.4) | copy-start | bytes 559876
  39.6 7.0 %collective-permute-start.2 = (f32[1,81,128]{2,1,0:T(8,128)S(1)}, f32[1,81,128]{2,1,0:T(8,128)S(1)}, u32[]{:S(2)}, u32[]{:S(2)}) collective-permute-start(f32[1,81,128]{2,1,0:T(8,128)S(1)} %get-tuple-element.5), channel_id=1, source_target_pairs={{0,4},{4,8},{8,12},{12,16},{16,20},{20,24},{24,28},{1,5},{5,9},{9,... | collective-permute-start | bytes 124424 | tf_op jit(solution)/shard_map/ppermute | solution.py:17
  44.5 7.2 %collective-permute-start.3 = (f32[1,81,128]{2,1,0:T(8,128)S(1)}, f32[1,81,128]{2,1,0:T(8,128)S(1)}, u32[]{:S(2)}, u32[]{:S(2)}) collective-permute-start(f32[1,81,128]{2,1,0:T(8,128)S(1)} %get-tuple-element.4), channel_id=1, source_target_pairs={{4,0},{8,4},{12,8},{16,12},{20,16},{24,20},{28,24},{5,1},{9,5},{13... | collective-permute-start | bytes 124424 | tf_op jit(solution)/shard_map/ppermute | solution.py:19
Sparse Core Ops, SparseCore 0:
  63.2 22.3 reduce-scatter.3
where the time goes:
time: 135 us; the launch traced here: 134 us
  blocking collectives  47.9 us (35%)
  waiting for transfers between devices  28 us (21%)
  other arithmetic  20.5 us (15%)
  between operations  14.3 us (11%)
  starting transfers between devices  12.9 us (10%)
  local copies, waits for them, and re-layouts  9.35 us (7%)
    psum x1, blocking collectives, body(): gram = lax.psum(partial_gram, 'cells')  40.1 us
    unnamed x2, waiting for transfers between devices  22.5 us
    scatter-add x2, other arithmetic, operate(): assembled.at[connectivity.reshape(-1)]  12.2 us
    ppermute x2, starting transfers between devices, with_halo(): lax.ppermute(tail, axis, [(i, (i + 1) % count) for i in range(ends)])  10.3 us
    all_to_all x1, blocking collectives, body(): lax.all_to_all(padded_words, 'bands', split_axis=0, concat_axis=1, tiled=...  7.84 us
    gather x2, local copies, waits for them, and re-layouts, operate(): cell_rows = vector.astype(jnp.bfloat16)[connectivity]  4.76 us
    scatter-add x4, other arithmetic, operate(): assembled.at[face_nodes[0]].add(face_halo[0]).at[face_nodes[1]]  4.49 us
    ppermute x2, waiting for transfers between devices, with_halo(): lax.ppermute(head, axis, [((i + 1) % count, i) for i in range(ends)])  3.86 us
  transfers between devices with their start and end apart: 5, of which 3 were waited for; matrix products, arithmetic and copies ran while one was open for 2% of the time, Pallas kernels for 0%

commit v1 on v0

v1 whole, which is shorter than its diff:
```python
import jax
import jax.numpy as jnp
from jax import lax
from jax.sharding import PartitionSpec as P

BF16 = jnp.bfloat16
F32 = jnp.float32


def digits(count):
    stride, left, out = 1, count, []
    for radix in range(2, count + 1):
        while left % radix == 0:
            out.append((stride, radix))
            stride *= radix
            left //= radix
    return out


def turned(count, stride, radix, by):
    pairs = []
    for source in range(count):
        digit = source // stride % radix
        pairs.append((source, source + ((digit + by) % radix - digit) * stride))
    return pairs


def sum_over(axis, value):
    count = lax.axis_size(axis)
    for stride, radix in digits(count):
        word = value.astype(BF16)
        value = word.astype(F32)
        for by in range(1, radix):
            value = value + lax.ppermute(word, axis, turned(count, stride, radix, by)).astype(F32)
    return value


def gather_over(axis, own):
    count = lax.axis_size(axis)
    blocks = {0: own}
    for stride, radix in reversed(digits(count)):
        for at, block in list(blocks.items()):
            for by in range(1, radix):
                blocks[at + by * stride] = lax.ppermute(block, axis, turned(count, stride, radix, radix - by))
    return blocks


def one_hot_t(flags, values):
    return lax.dot_general(flags, values, (((0,), (0,)), ((), ())), preferred_element_type=F32)


def body(wavefunctions, hamiltonians, connectivity, face_nodes):
    node_count, width = wavefunctions.shape
    shared = face_nodes.shape[1]
    place = lax.axis_index("cells")
    parts = lax.axis_size("cells")
    hamiltonian = hamiltonians[0]
    cell = connectivity[0]
    place_of = (lax.broadcasted_iota(jnp.int32, (node_count, node_count), 0) == cell[None, :]).astype(BF16)
    face = (face_nodes.reshape(-1)[:, None] == cell[None, :]).astype(BF16)
    start = one_hot_t(place_of, wavefunctions)
    ahead = [(i, (i + 1) % parts) for i in range(parts)]
    back = [((i + 1) % parts, i) for i in range(parts)]

    def halo(sums):
        rows = jnp.dot(face, sums.astype(BF16), preferred_element_type=F32).astype(BF16)
        before = lax.ppermute(rows[shared:], "cells", ahead)
        after = lax.ppermute(rows[:shared], "cells", back)
        before = jnp.where(place > 0, before, jnp.zeros_like(before))
        after = jnp.where(place < parts - 1, after, jnp.zeros_like(after))
        return one_hot_t(face, jnp.concatenate([before, after]))

    local = jnp.dot(hamiltonian, start.astype(BF16), preferred_element_type=F32)
    newer = 0.5 * (local + halo(local))
    local = jnp.dot(hamiltonian, newer.astype(BF16), preferred_element_type=F32)
    following = local + halo(local) - start

    top = following.astype(BF16)
    rest = following - top.astype(F32)
    middle = rest.astype(BF16)
    low = (rest - middle.astype(F32)).astype(BF16)
    filtered = sum(jnp.dot(place_of, word, preferred_element_type=F32) for word in (low, middle, top))

    first_face = jnp.sum(face[:shared].astype(F32), axis=0)
    keep = jnp.where(place > 0, 1.0 - first_face, jnp.ones_like(first_face))
    word = (following * keep[:, None]).astype(BF16)
    groups = lax.axis_size("bands")
    blocks = gather_over("bands", word)
    gram = jnp.stack([one_hot_t(blocks[turn], word) for turn in range(groups)])
    total = sum_over("cells", gram)
    group = lax.axis_index("bands")
    order = jnp.zeros((groups,), jnp.int32)
    for stride, radix in digits(groups):
        at = jnp.arange(groups, dtype=jnp.int32) // stride % radix
        order = order + (at - group // stride % radix) % radix * stride
    correlation = total[order].reshape(groups * width, width) / (parts * node_count)
    return filtered, correlation


def solution(mesh):
    placed = (P("cells", "bands"), P("cells", None, None), P("cells", None), P("cells", None))
    return jax.shard_map(
        body,
        mesh=mesh,
        in_specs=placed,
        out_specs=(P("cells", "bands"), P(None, "bands")),
        check_vma=False,
    )
```

time: 135 us -> 48.6 us (0.36)
  blocking collectives: 47.9 us -> 0 us
  other arithmetic: 20.5 us -> 1.82 us
  between operations: 14.3 us -> 0.89 us
  local copies, waits for them, and re-layouts: 9.35 us -> 1.45 us
  waiting for transfers between devices: 28 us -> 20.9 us
  matrix products: 1.28 us -> 7.45 us
  starting transfers between devices: 12.9 us -> 15.9 us
    psum x1 -> x0, blocking collectives: 40.1 us -> none  [body(): gram = lax.psum(partial_gram, 'cells')]
    unnamed x2 -> x0, waiting for transfers between devices: 22.5 us -> none
    scatter-add x6 -> x0, other arithmetic: 16.7 us -> none  [the longest x2 12.2 us: operate(): assembled.at[connectivity.reshape(-1)]]
    ppermute x4 -> x10, waiting for transfers between devices: 5.53 us -> 20.9 us  [the longest x3 13.2 us: sum_over(): lax.ppermute(word, axis, turned(count, stride, radix, by)).astype(F32)]
    all_to_all x1 -> x0, blocking collectives: 7.84 us -> none  [body(): lax.all_to_all(padded_words, 'bands', split_axis=0, concat_axis=1, tiled=...]
    dot_general x3 -> x13, matrix products: 1.28 us -> 7.45 us  [the longest x6 3.24 us: one_hot_t(): lax.dot_general(flags, values, (((0,), (0,)), ((), ())), preferred_elemen...]
    gather x4 -> x1, local copies, waits for them, and re-layouts: 6.11 us -> 0.57 us  [body(): total[order].reshape(groups * width, width) / (parts * node_count)]
    ppermute x4 -> x10, starting transfers between devices: 12.9 us -> 15.9 us  [the longest x2 6.52 us: halo(): after = lax.ppermute(rows[:shared], 'cells', back)]
  transfers between devices with their start and end apart: 5 -> 10, of which waited for: 3 -> 7; matrix products, arithmetic and copies ran while one was open for 2% -> 7% of each run, Pallas kernels for 0% -> 0%
where the time goes in v1:
time: 48.6 us; the launch traced here: 48.4 us
  waiting for transfers between devices  20.9 us (43%)
  starting transfers between devices  15.9 us (33%)
  matrix products  7.45 us (15%)
  other arithmetic  1.82 us (4%)
  local copies, waits for them, and re-layouts  1.45 us (3%)
  between operations  0.89 us (2%)
    ppermute x3, waiting for transfers between devices, sum_over(): lax.ppermute(word, axis, turned(count, stride, radix, by)).astype(F32)  13.2 us
    ppermute x2, starting transfers between devices, halo(): after = lax.ppermute(rows[:shared], 'cells', back)  6.52 us
    ppermute x3, waiting for transfers between devices, gather_over(): lax.ppermute(block, axis, turned(count, stride, radix, radix - by))  4.54 us
    ppermute x2, starting transfers between devices, halo(): before = lax.ppermute(rows[shared:], 'cells', ahead)  4.45 us
    dot_general x6, matrix products, one_hot_t(): lax.dot_general(flags, values, (((0,), (0,)), ((), ())), preferred_elemen...  3.24 us
    ppermute x3, starting transfers between devices, sum_over(): lax.ppermute(word, axis, turned(count, stride, radix, by)).astype(F32)  3.19 us
    ppermute x2, waiting for transfers between devices, halo(): before = lax.ppermute(rows[shared:], 'cells', ahead)  3.16 us
    dot_general x3, matrix products, body(): jnp.dot(place_of, word, preferred_element_type=F32)  2.29 us
  transfers between devices with their start and end apart: 10, of which 7 were waited for; matrix products, arithmetic and copies ran while one was open for 7% of the time, Pallas kernels for 0%

profile of v1, /device:TPU:0, one launch (start us, length us, event | category | flops | bytes accessed | tf_op | source)
XLA Modules:
  0.0 48.4 jit_solution(13105099006583969070)
XLA Ops:
  0.6 0.0 copy-start
  0.6 0.9 %eq.36 = s32[162]{0:T(256)S(1)} reshape(s32[2,81]{1,0:T(2,128)} %param.7) | data formatting | bytes 1296 | tf_op jit(solution)/shard_map/eq | solution.py:60
  1.5 0.7 %reduce = s32[729]{0:T(1024)S(1)} reduce(s32[1,729]{1,0:T(1,128)} %param.6, s32[]{:T(128)} %constant.94.clone.1), dimensions={0}, to_apply=%param.6.reduce_sub_computation | reduce | bytes 5836 | tf_op args[2]
  2.2 1.8 %fusion.3 = f32[729,128]{1,0:T(8,128)S(1)} fusion(bf16[729,128]{1,0:T(8,128)(2,1)} %param.4, s32[729]{0:T(1024)S(1)} %reduce), kind=kOutput, calls=%fused_computation.5 | convolution fusion | flops 136580336 | bytes 562788 | tf_op jit(solution)/shard_map/dot_general | solution.py:49
  4.0 0.0 copy-done
  4.0 0.5 convolution_bitcast_fusion.1
  4.4 0.3 convolution_convert_fusion.1
  4.7 3.0 %collective-permute-start = (bf16[81,128]{1,0:T(8,128)(2,1)S(1)}, bf16[81,128]{1,0:T(8,128)(2,1)S(1)}, u32[]{:S(2)}, u32[]{:S(2)}) collective-permute-start(bf16[81,128]{1,0:T(8,128)(2,1)S(1)} %get-tuple-element.4), channel_id=1, source_target_pairs={{0,4},{4,8},{8,12},{12,16},{16,20},{20,24},{24,28},{28,0},{1,5},{5... | collective-permute-start | bytes 62216 | tf_op jit(solution)/shard_map/ppermute | solution.py:67
  7.7 3.1 %collective-permute-start.1 = (bf16[81,128]{1,0:T(8,128)(2,1)S(1)}, bf16[81,128]{1,0:T(8,128)(2,1)S(1)}, u32[]{:S(2)}, u32[]{:S(2)}) collective-permute-start(bf16[81,128]{1,0:T(8,128)(2,1)S(1)} %get-tuple-element.5), channel_id=1, source_target_pairs={{4,0},{8,4},{12,8},{16,12},{20,16},{24,20},{28,24},{0,28},{5,1},{9... | collective-permute-start | bytes 62216 | tf_op jit(solution)/shard_map/ppermute | solution.py:68
  10.8 0.1 broadcast_compare_fusion
  11.1 1.5 %collective-permute-done = bf16[81,128]{1,0:T(8,128)(2,1)S(1)} collective-permute-done((bf16[81,128]{1,0:T(8,128)(2,1)S(1)}, bf16[81,128]{1,0:T(8,128)(2,1)S(1)}, u32[]{:S(2)}, u32[]{:S(2)}) %collective-permute-start) | collective-permute-done | bytes 20768 | tf_op jit(solution)/shard_map/ppermute | solution.py:67
  12.6 0.0 collective-permute-done.1
  12.6 0.9 %convolution_bitcast_fusion = f32[729,128]{1,0:T(8,128)S(1)} fusion(f32[729,128]{1,0:T(8,128)S(1)} %convolution_bitcast_fusion.1, bf16[1,729,729]{2,1,0:T(8,128)(2,1)S(1)} %copy-done, s32[729]{0:T(1024)S(1)} %reduce, s32[162]{0:T(256)S(1)} %eq.36, bf16[81,128]{1,0:T(8,128)(2,1)S(1)} %broadcast_select_fusion.1, bf16[81,128]{1,0:T(8,128)(2,1)S(1)} %broadcast_select_fusion.3), kind=kOutput, calls=%fused_computation.7 | convolution fusion | flops 166762960 | bytes 1854414 | tf_op jit(solution)/shard_map/dot_general | solution.py:75
  13.5 0.3 convolution_convert_fusion
  13.8 1.5 %collective-permute-start.2 = (bf16[81,128]{1,0:T(8,128)(2,1)S(1)}, bf16[81,128]{1,0:T(8,128)(2,1)S(1)}, u32[]{:S(2)}, u32[]{:S(2)}) collective-permute-start(bf16[81,128]{1,0:T(8,128)(2,1)S(1)} %get-tuple-element.2), channel_id=1, source_target_pairs={{0,4},{4,8},{8,12},{12,16},{16,20},{20,24},{24,28},{28,0},{1,5},{5... | collective-permute-start | bytes 62216 | tf_op jit(solution)/shard_map/ppermute | solution.py:67
  15.3 3.4 %collective-permute-start.3 = (bf16[81,128]{1,0:T(8,128)(2,1)S(1)}, bf16[81,128]{1,0:T(8,128)(2,1)S(1)}, u32[]{:S(2)}, u32[]{:S(2)}) collective-permute-start(bf16[81,128]{1,0:T(8,128)(2,1)S(1)} %get-tuple-element.3), channel_id=1, source_target_pairs={{4,0},{8,4},{12,8},{16,12},{20,16},{24,20},{28,24},{0,28},{5,1},{9... | collective-permute-start | bytes 62216 | tf_op jit(solution)/shard_map/ppermute | solution.py:68
  18.7 1.7 %collective-permute-done.2 = bf16[81,128]{1,0:T(8,128)(2,1)S(1)} collective-permute-done((bf16[81,128]{1,0:T(8,128)(2,1)S(1)}, bf16[81,128]{1,0:T(8,128)(2,1)S(1)}, u32[]{:S(2)}, u32[]{:S(2)}) %collective-permute-start.2) | collective-permute-done | bytes 20768 | tf_op jit(solution)/shard_map/ppermute | solution.py:67
  20.4 0.0 collective-permute-done.3
  20.4 0.5 multiply_convert_fusion
  20.9 1.7 %collective-permute-start.5 = (bf16[729,128]{1,0:T(8,128)(2,1)S(1)}, bf16[729,128]{1,0:T(8,128)(2,1)S(1)}, u32[]{:S(2)}, u32[]{:S(2)}) collective-permute-start(bf16[729,128]{1,0:T(8,128)(2,1)S(1)} %get-tuple-element.6), channel_id=1, source_target_pairs={{0,2},{1,3},{2,0},{3,1},{4,6},{5,7},{6,4},{7,5},{8,10},{9,11},{10,... | collective-permute-start | bytes 559880 | tf_op jit(solution)/shard_map/ppermute | solution.py:44
  22.6 0.0 collective-permute-start.4
  22.7 0.3 fusion.15
  22.9 3.6 %collective-permute-done.5 = bf16[729,128]{1,0:T(8,128)(2,1)S(1)} collective-permute-done((bf16[729,128]{1,0:T(8,128)(2,1)S(1)}, bf16[729,128]{1,0:T(8,128)(2,1)S(1)}, u32[]{:S(2)}, u32[]{:S(2)}) %collective-permute-start.5) | collective-permute-done | bytes 186656 | tf_op jit(solution)/shard_map/ppermute | solution.py:44
  26.6 0.0 collective-permute-start.6
  26.6 0.3 fusion.17
  26.8 0.0 collective-permute-done.4
  26.8 0.3 fusion.16
  27.1 0.9 %collective-permute-done.6 = bf16[729,128]{1,0:T(8,128)(2,1)S(1)} collective-permute-done((bf16[729,128]{1,0:T(8,128)(2,1)S(1)}, bf16[729,128]{1,0:T(8,128)(2,1)S(1)}, u32[]{:S(2)}, u32[]{:S(2)}) %collective-permute-start.6) | collective-permute-done | bytes 186656 | tf_op jit(solution)/shard_map/ppermute | solution.py:44
  28.0 0.3 fusion.18
  28.3 0.3 collective-permute-start.7
  28.5 0.5 %fusion.1 = f32[729,128]{1,0:T(8,128)S(1)} fusion(s32[729]{0:T(1024)S(1)} %reduce, f32[729,128]{1,0:T(8,128)S(1)} %get-tuple-element.7), kind=kOutput, calls=%fused_computation.3 | convolution fusion | flops 136953584 | bytes 749412 | tf_op jit(solution)/shard_map/dot_general | solution.py:82
  29.0 4.8 %collective-permute-done.7 = bf16[4,128,128]{2,1,0:T(8,128)(2,1)S(1)} collective-permute-done((bf16[4,128,128]{2,1,0:T(8,128)(2,1)S(1)}, bf16[4,128,128]{2,1,0:T(8,128)(2,1)S(1)}, u32[]{:S(2)}, u32[]{:S(2)}) %collective-permute-start.7) | collective-permute-done | bytes 131104 | tf_op jit(solution)/shard_map/ppermute | solution.py:34
  33.9 0.4 collective-permute-start.8
  34.3 0.5 %fusion.6 = f32[729,128]{1,0:T(8,128)S(1)} fusion(f32[729,128]{1,0:T(8,128)S(1)} %fusion.1, s32[729]{0:T(1024)S(1)} %reduce, f32[729,128]{1,0:T(8,128)S(1)} %get-tuple-element.7), kind=kOutput, calls=%fused_computation.12 | convolution fusion | flops 137326832 | bytes 1122660 | tf_op jit(solution)/shard_map/dot_general | solution.py:82
  34.8 4.1 %collective-permute-done.8 = bf16[4,128,128]{2,1,0:T(8,128)(2,1)S(1)} collective-permute-done((bf16[4,128,128]{2,1,0:T(8,128)(2,1)S(1)}, bf16[4,128,128]{2,1,0:T(8,128)(2,1)S(1)}, u32[]{:S(2)}, u32[]{:S(2)}) %collective-permute-start.8) | collective-permute-done | bytes 131104 | tf_op jit(solution)/shard_map/ppermute | solution.py:34
  39.0 0.1 add_convert_fusion
  39.0 2.6 %collective-permute-start.9 = (bf16[4,128,128]{2,1,0:T(8,128)(2,1)S(1)}, bf16[4,128,128]{2,1,0:T(8,128)(2,1)S(1)}, u32[]{:S(2)}, u32[]{:S(2)}) collective-permute-start(bf16[4,128,128]{2,1,0:T(8,128)(2,1)S(1)} %add_convert_fusion), channel_id=1, source_target_pairs={{0,16},{4,20},{8,24},{12,28},{16,0},{20,4},{24,8},{28,12},{1,17},{... | collective-permute-start | bytes 393224 | tf_op jit(solution)/shard_map/ppermute | solution.py:34
  41.6 1.3 %fusion.7 = f32[729,128]{1,0:T(8,128)} fusion(f32[729,128]{1,0:T(8,128)S(1)} %fusion.6, s32[729]{0:T(1024)S(1)} %reduce, f32[729,128]{1,0:T(8,128)S(1)} %get-tuple-element.7), kind=kOutput, calls=%fused_computation.13 | convolution fusion | flops 136766960 | bytes 1122660 | tf_op jit(solution)/shard_map/dot_general | solution.py:82
  42.8 4.2 %collective-permute-done.9 = bf16[4,128,128]{2,1,0:T(8,128)(2,1)S(1)} collective-permute-done((bf16[4,128,128]{2,1,0:T(8,128)(2,1)S(1)}, bf16[4,128,128]{2,1,0:T(8,128)(2,1)S(1)}, u32[]{:S(2)}, u32[]{:S(2)}) %collective-permute-start.9) | collective-permute-done | bytes 131104 | tf_op jit(solution)/shard_map/ppermute | solution.py:34
  47.1 0.6 %gather_fusion = f32[4,128,128]{2,1,0:T(8,128)S(1)} fusion(f32[4,128,128]{2,1,0:T(8,128)S(1)} %convert_add_fusion, s32[1024]{0:T(1024)S(1)} %pad_clamp_fusion), kind=kCustom, calls=%fused_computation | custom fusion | bytes 524304 | tf_op jit(solution)/shard_map/gather | solution.py:96
  47.7 0.7 %broadcast_multiply_fusion = f32[4,128,128]{2,1,0:T(8,128)} fusion(f32[4,128,128]{2,1,0:T(8,128)S(1)} %gather_fusion), kind=kLoop, calls=%fused_computation.59 | loop fusion | flops 65536 | bytes 524288 | tf_op jit(solution)/shard_map/div | solution.py:96
  (13 shorter events, 0.2 us)
Async XLA Ops:
  0.6 3.3 %copy-start = (bf16[1,729,729]{2,1,0:T(8,128)(2,1)S(1)}, bf16[1,729,729]{2,1,0:T(8,128)(2,1)}, u32[]{:S(2)}) copy-start(bf16[1,729,729]{2,1,0:T(8,128)(2,1)} %param.5) | copy-start | bytes 3188650
  4.7 7.8 %collective-permute-start = (bf16[81,128]{1,0:T(8,128)(2,1)S(1)}, bf16[81,128]{1,0:T(8,128)(2,1)S(1)}, u32[]{:S(2)}, u32[]{:S(2)}) collective-permute-start(bf16[81,128]{1,0:T(8,128)(2,1)S(1)} %get-tuple-element.4), channel_id=1, source_target_pairs={{0,4},{4,8},{8,12},{12,16},{16,20},{20,24},{24,28},{28,0},{1,5},{5... | collective-permute-start | bytes 62216 | tf_op jit(solution)/shard_map/ppermute | solution.py:67
  7.7 4.8 %collective-permute-start.1 = (bf16[81,128]{1,0:T(8,128)(2,1)S(1)}, bf16[81,128]{1,0:T(8,128)(2,1)S(1)}, u32[]{:S(2)}, u32[]{:S(2)}) collective-permute-start(bf16[81,128]{1,0:T(8,128)(2,1)S(1)} %get-tuple-element.5), channel_id=1, source_target_pairs={{4,0},{8,4},{12,8},{16,12},{20,16},{24,20},{28,24},{0,28},{5,1},{9... | collective-permute-start | bytes 62216 | tf_op jit(solution)/shard_map/ppermute | solution.py:68
  13.8 6.6 %collective-permute-start.2 = (bf16[81,128]{1,0:T(8,128)(2,1)S(1)}, bf16[81,128]{1,0:T(8,128)(2,1)S(1)}, u32[]{:S(2)}, u32[]{:S(2)}) collective-permute-start(bf16[81,128]{1,0:T(8,128)(2,1)S(1)} %get-tuple-element.2), channel_id=1, source_target_pairs={{0,4},{4,8},{8,12},{12,16},{16,20},{20,24},{24,28},{28,0},{1,5},{5... | collective-permute-start | bytes 62216 | tf_op jit(solution)/shard_map/ppermute | solution.py:67
  15.3 5.1 %collective-permute-start.3 = (bf16[81,128]{1,0:T(8,128)(2,1)S(1)}, bf16[81,128]{1,0:T(8,128)(2,1)S(1)}, u32[]{:S(2)}, u32[]{:S(2)}) collective-permute-start(bf16[81,128]{1,0:T(8,128)(2,1)S(1)} %get-tuple-element.3), channel_id=1, source_target_pairs={{4,0},{8,4},{12,8},{16,12},{20,16},{24,20},{28,24},{0,28},{5,1},{9... | collective-permute-start | bytes 62216 | tf_op jit(solution)/shard_map/ppermute | solution.py:68
  20.9 5.6 %collective-permute-start.5 = (bf16[729,128]{1,0:T(8,128)(2,1)S(1)}, bf16[729,128]{1,0:T(8,128)(2,1)S(1)}, u32[]{:S(2)}, u32[]{:S(2)}) collective-permute-start(bf16[729,128]{1,0:T(8,128)(2,1)S(1)} %get-tuple-element.6), channel_id=1, source_target_pairs={{0,2},{1,3},{2,0},{3,1},{4,6},{5,7},{6,4},{7,5},{8,10},{9,11},{10,... | collective-permute-start | bytes 559880 | tf_op jit(solution)/shard_map/ppermute | solution.py:44
  22.6 4.2 %collective-permute-start.4 = (bf16[729,128]{1,0:T(8,128)(2,1)S(1)}, bf16[729,128]{1,0:T(8,128)(2,1)S(1)}, u32[]{:S(2)}, u32[]{:S(2)}) collective-permute-start(bf16[729,128]{1,0:T(8,128)(2,1)S(1)} %get-tuple-element.6), channel_id=1, source_target_pairs={{0,1},{1,0},{2,3},{3,2},{4,5},{5,4},{6,7},{7,6},{8,9},{9,8},{10,11... | collective-permute-start | bytes 559880 | tf_op jit(solution)/shard_map/ppermute | solution.py:44
  26.6 1.4 %collective-permute-start.6 = (bf16[729,128]{1,0:T(8,128)(2,1)S(1)}, bf16[729,128]{1,0:T(8,128)(2,1)S(1)}, u32[]{:S(2)}, u32[]{:S(2)}) collective-permute-start(bf16[729,128]{1,0:T(8,128)(2,1)S(1)} %collective-permute-done.5), channel_id=1, source_target_pairs={{0,1},{1,0},{2,3},{3,2},{4,5},{5,4},{6,7},{7,6},{8,9},{9,8},{10,11... | collective-permute-start | bytes 559880 | tf_op jit(solution)/shard_map/ppermute | solution.py:44
  28.3 5.6 %collective-permute-start.7 = (bf16[4,128,128]{2,1,0:T(8,128)(2,1)S(1)}, bf16[4,128,128]{2,1,0:T(8,128)(2,1)S(1)}, u32[]{:S(2)}, u32[]{:S(2)}) collective-permute-start(bf16[4,128,128]{2,1,0:T(8,128)(2,1)S(1)} %pad_maximum_fusion), channel_id=1, source_target_pairs={{0,4},{4,0},{8,12},{12,8},{16,20},{20,16},{24,28},{28,24},{1,5},{5... | collective-permute-start | bytes 393224 | tf_op jit(solution)/shard_map/ppermute | solution.py:34
  33.9 5.0 %collective-permute-start.8 = (bf16[4,128,128]{2,1,0:T(8,128)(2,1)S(1)}, bf16[4,128,128]{2,1,0:T(8,128)(2,1)S(1)}, u32[]{:S(2)}, u32[]{:S(2)}) collective-permute-start(bf16[4,128,128]{2,1,0:T(8,128)(2,1)S(1)} %add_convert_fusion.1), channel_id=1, source_target_pairs={{0,8},{4,12},{8,0},{12,4},{16,24},{20,28},{24,16},{28,20},{1,9},{5... | collective-permute-start | bytes 393224 | tf_op jit(solution)/shard_map/ppermute | solution.py:34
  39.0 8.1 %collective-permute-start.9 = (bf16[4,128,128]{2,1,0:T(8,128)(2,1)S(1)}, bf16[4,128,128]{2,1,0:T(8,128)(2,1)S(1)}, u32[]{:S(2)}, u32[]{:S(2)}) collective-permute-start(bf16[4,128,128]{2,1,0:T(8,128)(2,1)S(1)} %add_convert_fusion), channel_id=1, source_target_pairs={{0,16},{4,20},{8,24},{12,28},{16,0},{20,4},{24,8},{28,12},{1,17},{... | collective-permute-start | bytes 393224 | tf_op jit(solution)/shard_map/ppermute | solution.py:34

commit v2 on v1

v2 whole, which is shorter than its diff:
```python
import jax
import jax.numpy as jnp
from jax import lax
from jax.experimental import pallas as pl
from jax.experimental.pallas import tpu as pltpu
from jax.sharding import PartitionSpec as P

BF16 = jnp.bfloat16
F32 = jnp.float32


def digits(count):
    stride, left, out = 1, count, []
    for radix in range(2, count + 1):
        while left % radix == 0:
            out.append((stride, radix))
            stride *= radix
            left //= radix
    return out


def turn(index, stride, radix, by):
    digit = index // stride % radix
    return index + ((digit + by) % radix - digit) * stride


def turned(count, stride, radix, by):
    return [(source, turn(source, stride, radix, by)) for source in range(count)]


def sum_over(axis, value):
    count = lax.axis_size(axis)
    for stride, radix in digits(count):
        word = value.astype(BF16)
        value = word.astype(F32)
        for by in range(1, radix):
            value = value + lax.ppermute(word, axis, turned(count, stride, radix, by)).astype(F32)
    return value


def dot(a, b):
    return jnp.dot(a, b, preferred_element_type=F32)


def dot_t(a, b):
    return lax.dot_general(a, b, (((0,), (0,)), ((), ())), preferred_element_type=F32)


def one_hot(flags):
    return jnp.where(flags, jnp.float32(1), jnp.float32(0)).astype(BF16)


def first_kernel(waves_hbm, cell_hbm, faces_hbm, ham_hbm, start, local, sums, ham, one, columns, waves, cell, faces, rows, sems):
    pairs = ((cell_hbm, cell), (faces_hbm, faces), (waves_hbm, waves), (ham_hbm.at[0], ham))
    copies = [pltpu.make_async_copy(source, target, sems.at[at]) for at, (source, target) in enumerate(pairs)]
    for copy in copies:
        copy.start()
    count = waves.shape[0]
    shared = faces.shape[1]
    padded = one.shape[0] // 2
    rows[...] = jnp.full(rows.shape, -1, F32)
    copies[0].wait()
    copies[1].wait()
    row = cell[...].astype(F32)
    rows[0:1, :count] = row
    rows[1:3, :shared] = faces[...].astype(F32)
    turned_rows = jnp.transpose(rows[...])
    columns[...] = turned_rows
    nodes = lax.broadcasted_iota(jnp.int32, (count, count), 1).astype(F32)
    place = one_hot(turned_rows[:count, 0:1] == nodes)
    pick = one_hot(jnp.concatenate([turned_rows[:padded, 1:2], turned_rows[:padded, 2:3]], axis=0) == row)
    one[...] = pick
    copies[2].wait()
    begin = dot(place, waves[...]).astype(BF16)
    start[...] = begin
    copies[3].wait()
    result = dot(ham[...], begin)
    local[...] = result
    sums[...] = dot(pick, result.astype(BF16)).astype(BF16)


def middle_kernel(ends, columns, faces, one_t, keep):
    count = one_t.shape[0]
    shared = faces.shape[1]
    padded = one_t.shape[1] // 2
    col = columns[:count, 0:1]
    row = faces[...].astype(F32)
    has_before = jnp.where(ends[0] > 0, jnp.float32(1), jnp.float32(0))
    has_after = jnp.where(ends[1] > 0, jnp.float32(1), jnp.float32(0))
    first = jnp.where(col == row[0:1], jnp.float32(1), jnp.float32(0))
    second = jnp.where(col == row[1:2], jnp.float32(1), jnp.float32(0))
    one_t[...] = jnp.zeros(one_t.shape, BF16)
    one_t[:, :shared] = (first * has_before).astype(BF16)
    one_t[:, padded : padded + shared] = (second * has_after).astype(BF16)
    on_first = jnp.sum(first, axis=1, keepdims=True) * has_before
    on_second = jnp.sum(second, axis=1, keepdims=True)
    keep[...] = jnp.broadcast_to(1.0 - on_first - on_second, keep.shape)


def second_kernel(local, before, after, ham, start, one, one_t, keep, partial, block, sums):
    count = local.shape[0]
    padded = before.shape[0]
    head = block.shape[0] - padded
    halo = jnp.concatenate([before[...], after[...]], axis=0)
    newer = 0.5 * (local[...] + dot(one_t[...], halo))
    result = dot(ham[...], newer.astype(BF16))
    rest = result - start[...].astype(F32)
    partial[...] = rest
    sums[...] = dot(one[...], result.astype(BF16)).astype(BF16)
    block[count:head, :] = jnp.zeros((head - count, block.shape[1]), BF16)
    block[:count, :] = (rest * keep[...]).astype(BF16)
    block[head:, :] = dot(one[padded:, :], rest.astype(BF16)).astype(BF16)


def vmem(count):
    return [pl.BlockSpec(memory_space=pltpu.VMEM)] * count


def body(wavefunctions, hamiltonians, connectivity, face_nodes):
    node_count, width = wavefunctions.shape
    shared = face_nodes.shape[1]
    padded = -(-shared // 32) * 32
    head = -(-node_count // 16) * 16
    lanes = -(-node_count // 128) * 128
    parts = lax.axis_size("cells")
    groups = lax.axis_size("bands")
    place = lax.axis_index("cells")
    group = lax.axis_index("bands")
    nodal = (node_count, width)
    shape = jax.ShapeDtypeStruct
    params = pltpu.CompilerParams(vmem_limit_bytes=24 * 2**20)

    start, local, sums, ham, one, columns = pl.pallas_call(
        first_kernel,
        out_shape=(
            shape(nodal, BF16),
            shape(nodal, F32),
            shape((2 * padded, width), BF16),
            shape(hamiltonians.shape[1:], BF16),
            shape((2 * padded, node_count), BF16),
            shape((lanes, 8), F32),
        ),
        in_specs=[pl.BlockSpec(memory_space=pltpu.HBM)] * 4,
        out_specs=tuple(vmem(6)),
        scratch_shapes=[
            pltpu.VMEM(nodal, BF16),
            pltpu.VMEM(connectivity.shape, jnp.int32),
            pltpu.VMEM(face_nodes.shape, jnp.int32),
            pltpu.VMEM((8, lanes), F32),
            pltpu.SemaphoreType.DMA((4,)),
        ],
        compiler_params=params,
    )(*(pltpu.with_memory_space_constraint(x, pltpu.HBM) for x in (wavefunctions, connectivity, face_nodes, hamiltonians)))

    both = ("cells", "bands")
    stride, radix = digits(groups)[-1] if groups > 1 else (1, 1)

    def pair_swap(first):
        pairs = []
        for part in range(parts):
            other = first + ((part - first) ^ 1)
            for band in range(groups):
                if part >= first and other < parts:
                    pairs.append((part * groups + band, other * groups + band))
                else:
                    pairs.append((part * groups + band, part * groups + turn(band, stride, radix, 1)))
        return pairs

    odd = place % 2 == 1

    def neighbours(sums):
        low, high = sums[:padded], sums[padded:]
        even_odd = lax.ppermute(jnp.where(odd, low, high), both, pair_swap(0))
        odd_even = lax.ppermute(jnp.where(odd, high, low), both, pair_swap(1))
        return jnp.where(odd, even_odd, odd_even), jnp.where(odd, odd_even, even_odd)

    before, after = neighbours(sums)
    ends = jnp.stack([place, parts - 1 - place]).astype(jnp.int32)
    one_t, keep = pl.pallas_call(
        middle_kernel,
        out_shape=(shape((node_count, 2 * padded), BF16), shape(nodal, F32)),
        in_specs=[pl.BlockSpec(memory_space=pltpu.SMEM)] + vmem(2),
        out_specs=tuple(vmem(2)),
        compiler_params=params,
    )(ends, columns, face_nodes)
    partial, block, sums = pl.pallas_call(
        second_kernel,
        out_shape=(shape(nodal, F32), shape((head + padded, width), BF16), shape((2 * padded, width), BF16)),
        in_specs=vmem(8),
        out_specs=tuple(vmem(3)),
        compiler_params=params,
    )(local, before, after, ham, start, one, one_t, keep)

    blocks = {0: block}
    tails = {}
    for stride, radix in digits(groups)[1:]:
        for at in list(blocks):
            for by in range(1, radix):
                blocks[at + by * stride] = lax.ppermute(blocks[at], "bands", turned(groups, stride, radix, radix - by))
    before, after = neighbours(sums)
    has_after = place < parts - 1
    tails[0] = after
    for at in list(blocks)[1:]:
        pairs = []
        for part in range(parts):
            for band in range(groups):
                target = band
                for stride, radix in digits(groups)[1:]:
                    target = turn(target, stride, radix, radix - at // stride % radix)
                pairs.append((part * groups + band, (part - 1) % parts * groups + target))
        tails[at] = lax.ppermute(sums[:padded], both, pairs)
    for at in list(blocks):
        tail = jnp.where(has_after, tails[at], jnp.zeros_like(tails[at]))
        blocks[at] = blocks[at].at[head:].add(tail)
    for stride, radix in digits(groups)[:1]:
        for at in list(blocks):
            for by in range(1, radix):
                blocks[at + by * stride] = lax.ppermute(blocks[at], "bands", turned(groups, stride, radix, radix - by))
    gram = jnp.stack([dot_t(blocks[at], blocks[0]) for at in range(groups)])
    gram, partial, before, after = lax.optimization_barrier((gram, partial, before, after))
    total = sum_over("cells", gram) * (1.0 / (parts * node_count))
    radices = digits(groups)
    total = total.reshape(tuple(radix for _, radix in reversed(radices)) + (width, width))
    for at, (stride, radix) in enumerate(radices):
        digit = group // stride % radix
        moved = total
        for by in range(1, radix):
            moved = jnp.where(digit == by, jnp.roll(total, by, axis=len(radices) - 1 - at), moved)
        total = moved
    correlation = total.reshape(groups * width, width)

    before = jnp.where(place > 0, before, jnp.zeros_like(before))[:shared]
    after = jnp.where(has_after, after, jnp.zeros_like(after))[:shared]
    nodes = lax.broadcasted_iota(jnp.int32, (node_count, node_count), 0)
    place_of = (nodes == connectivity).astype(BF16)
    face_of = (face_nodes.reshape(-1)[None, :] == nodes[:, :1]).astype(BF16)
    top = partial.astype(BF16)
    rest = partial - top.astype(F32)
    middle = rest.astype(BF16)
    small = (rest - middle.astype(F32)).astype(BF16)
    halo = jnp.concatenate([before, after])
    filtered = dot(place_of, small) + dot(place_of, middle) + dot(face_of, halo) + dot(place_of, top)
    return filtered, correlation


def solution(mesh):
    placed = (P("cells", "bands"), P("cells", None, None), P("cells", None), P("cells", None))
    return jax.shard_map(
        body,
        mesh=mesh,
        in_specs=placed,
        out_specs=(P("cells", "bands"), P(None, "bands")),
        check_vma=False,
    )
```

time: 48.6 us -> 43.9 us (0.903)
  waiting for transfers between devices: 20.9 us -> 14.9 us
  Pallas kernels: 0 us -> 4.9 us
  matrix products: 7.45 us -> 3.6 us
  starting transfers between devices: 15.9 us -> 18.2 us
  local copies, waits for them, and re-layouts: 1.45 us -> 0.15 us
  other arithmetic: 1.82 us -> 1.12 us
    pallas_call x0 -> x3, Pallas kernels: none -> 4.9 us  [the longest x1 2.79 us: body(): pl.pallas_call(first_kernel, out_shape=(shape(nodal, BF16), shape(nodal,...]
    dot_general x13 -> x8, matrix products: 7.45 us -> 3.6 us  [the longest x4 2.57 us: dot(): return jnp.dot(a, b, preferred_element_type=F32)]
    ppermute x7 -> x8, waiting for transfers between devices: 7.7 us -> 4.06 us  [the longest x1 2.21 us: body(): tails[at] = lax.ppermute(sums[:padded], both, pairs)]
    ppermute x3, waiting for transfers between devices: 13.2 us -> 10.8 us  [sum_over(): lax.ppermute(word, axis, turned(count, stride, radix, by)).astype(F32)]
    ppermute x3, starting transfers between devices: 3.19 us -> 5.52 us  [sum_over(): lax.ppermute(word, axis, turned(count, stride, radix, by)).astype(F32)]
    eq x1, local copies, waits for them, and re-layouts: 0.85 us -> 0.08 us  [body(): face_of = (face_nodes.reshape(-1)[None, :] == nodes[:, :1]).astype(BF16)]
    select_n x6, other arithmetic: 0.07 us -> 0.82 us  [the longest x2 0.78 us: body(): jnp.where(digit == by, jnp.roll(total, by, axis=len(radices) - 1 - at), m...]
    div x1 -> x0, other arithmetic: 0.73 us -> none  [body(): total[order].reshape(groups * width, width) / (parts * node_count)]
  transfers between devices with their start and end apart: 10 -> 11, of which waited for: 7 -> 6; matrix products, arithmetic and copies ran while one was open for 7% -> 8% of each run, Pallas kernels for 0% -> 2%
where the time goes in v2:
time: 43.9 us; the launch traced here: 43.7 us
  starting transfers between devices  18.2 us (41%)
  waiting for transfers between devices  14.9 us (34%)
  Pallas kernels  4.9 us (11%)
  matrix products  3.6 us (8%)
  other arithmetic  1.12 us (3%)
  between operations  0.84 us (2%)
    ppermute x3, waiting for transfers between devices, sum_over(): lax.ppermute(word, axis, turned(count, stride, radix, by)).astype(F32)  10.8 us
    ppermute x2, starting transfers between devices, neighbours(): even_odd = lax.ppermute(jnp.where(odd, low, high), both, pair_swap(0))  6.44 us
    ppermute x3, starting transfers between devices, sum_over(): lax.ppermute(word, axis, turned(count, stride, radix, by)).astype(F32)  5.52 us
    pallas_call x1, Pallas kernels, body(): pl.pallas_call(first_kernel, out_shape=(shape(nodal, BF16), shape(nodal,...  2.79 us
    dot_general x4, matrix products, dot(): return jnp.dot(a, b, preferred_element_type=F32)  2.57 us
    ppermute x1, starting transfers between devices, body(): tails[at] = lax.ppermute(sums[:padded], both, pairs)  2.44 us
    ppermute x1, waiting for transfers between devices, body(): tails[at] = lax.ppermute(sums[:padded], both, pairs)  2.21 us
    ppermute x2, starting transfers between devices, neighbours(): odd_even = lax.ppermute(jnp.where(odd, high, low), both, pair_swap(1))  2.09 us
  transfers between devices with their start and end apart: 11, of which 6 were waited for; matrix products, arithmetic and copies ran while one was open for 8% of the time, Pallas kernels for 2%

profile of v2, /device:TPU:0, one launch (start us, length us, event | category | flops | bytes accessed | tf_op | source)
XLA Modules:
  0.0 43.7 jit_solution(5497766139831096576)
XLA Ops:
  0.6 0.0 copy-start
  0.7 2.8 %shard_map.59 = (bf16[729,128]{1,0:T(8,128)(2,1)S(1)}, f32[729,128]{1,0:T(8,128)S(1)}, bf16[192,128]{1,0:T(8,128)(2,1)S(1)}, bf16[729,729]{1,0:T(8,128)(2,1)S(1)...) custom-call(bf16[729,128]{1,0:T(8,128)(2,1)} %waves_hbm.1, s32[1,729]{1,0:T(1,128)} %cell_hbm.1, s32[2,81]{1,0:T(2,128)} %faces.1, ...), custom_call_target="tpu_custom_call" | custom-call | tf_op jit(solution)/shard_map/pallas_call | solution.py:133
  3.5 3.0 %collective-permute-start = (bf16[96,128]{1,0:T(8,128)(2,1)S(1)}, bf16[96,128]{1,0:T(8,128)(2,1)S(1)}, u32[]{:S(2)}, u32[]{:S(2)}) collective-permute-start(bf16[96,128]{1,0:T(8,128)(2,1)S(1)} %get-tuple-element.71), channel_id=1, source_target_pairs={{0,4},{1,5},{2,6},{3,7},{4,0},{5,1},{6,2},{7,3},{8,12},{9,13},{10,... | collective-permute-start | bytes 73736 | tf_op jit(solution)/shard_map/ppermute | solution.py:173
  6.5 1.5 %collective-permute-start.1 = (bf16[96,128]{1,0:T(8,128)(2,1)S(1)}, bf16[96,128]{1,0:T(8,128)(2,1)S(1)}, u32[]{:S(2)}, u32[]{:S(2)}) collective-permute-start(bf16[96,128]{1,0:T(8,128)(2,1)S(1)} %get-tuple-element.70), channel_id=1, source_target_pairs={{0,2},{1,3},{2,0},{3,1},{4,8},{5,9},{6,10},{7,11},{8,4},{9,5},{10,... | collective-permute-start | bytes 73736 | tf_op jit(solution)/shard_map/ppermute | solution.py:174
  8.0 0.1 pad_add_fusion.ends
  8.1 0.0 copy-done
  8.1 1.0 %shard_map.60 = (bf16[729,192]{1,0:T(8,128)(2,1)S(1)}, f32[729,128]{1,0:T(8,128)S(1)}) custom-call(s32[2]{0:T(128)S(1)} %pad_add_fusion.ends, f32[768,8]{1,0:T(8,128)S(1)} %get-tuple-element.46.columns, s32[2,81]{1,0:T(2,128)S(1)} %copy-done), custom_call_target="tpu_custom_call" | custom-call | tf_op jit(solution)/shard_map/pallas_call | solution.py:179
  9.1 0.0 collective-permute-done
  9.1 1.2 %collective-permute-done.1 = bf16[96,128]{1,0:T(8,128)(2,1)S(1)} collective-permute-done((bf16[96,128]{1,0:T(8,128)(2,1)S(1)}, bf16[96,128]{1,0:T(8,128)(2,1)S(1)}, u32[]{:S(2)}, u32[]{:S(2)}) %collective-permute-start.1) | collective-permute-done | bytes 24608 | tf_op jit(solution)/shard_map/ppermute | solution.py:174
  10.3 0.0 copy-start.1
  10.3 1.1 %shard_map.61 = (f32[729,128]{1,0:T(8,128)S(1)}, bf16[832,128]{1,0:T(8,128)(2,1)S(1)}, bf16[192,128]{1,0:T(8,128)(2,1)S(1)}) custom-call(f32[729,128]{1,0:T(8,128)S(1)} %get-tuple-element.41.local, bf16[96,128]{1,0:T(8,128)(2,1)S(1)} %get-tuple-element.69.before, bf16[96,128]{1,0:T(8,128)(2,1)S(1)} %get-tuple-element.68.after, ...), custom_call_target="tpu_custom_call" | custom-call | tf_op jit(solution)/shard_map/pallas_call | solution.py:186
  11.4 1.6 %collective-permute-start.5 = (bf16[832,128]{1,0:T(8,128)(2,1)S(1)}, bf16[832,128]{1,0:T(8,128)(2,1)S(1)}, u32[]{:S(2)}, u32[]{:S(2)}) collective-permute-start(bf16[832,128]{1,0:T(8,128)(2,1)S(1)} %get-tuple-element.49), channel_id=1, source_target_pairs={{0,2},{1,3},{2,0},{3,1},{4,6},{5,7},{6,4},{7,5},{8,10},{9,11},{10,... | collective-permute-start | bytes 638984 | tf_op jit(solution)/shard_map/ppermute | solution.py:199
  13.0 0.6 %collective-permute-start.2 = (bf16[96,128]{1,0:T(8,128)(2,1)S(1)}, bf16[96,128]{1,0:T(8,128)(2,1)S(1)}, u32[]{:S(2)}, u32[]{:S(2)}) collective-permute-start(bf16[96,128]{1,0:T(8,128)(2,1)S(1)} %get-tuple-element.67), channel_id=1, source_target_pairs={{0,2},{1,3},{2,0},{3,1},{4,8},{5,9},{6,10},{7,11},{8,4},{9,5},{10,... | collective-permute-start | bytes 73736 | tf_op jit(solution)/shard_map/ppermute | solution.py:174
  13.6 3.4 %collective-permute-start.3 = (bf16[96,128]{1,0:T(8,128)(2,1)S(1)}, bf16[96,128]{1,0:T(8,128)(2,1)S(1)}, u32[]{:S(2)}, u32[]{:S(2)}) collective-permute-start(bf16[96,128]{1,0:T(8,128)(2,1)S(1)} %get-tuple-element.65), channel_id=1, source_target_pairs={{0,4},{1,5},{2,6},{3,7},{4,0},{5,1},{6,2},{7,3},{8,12},{9,13},{10,... | collective-permute-start | bytes 73736 | tf_op jit(solution)/shard_map/ppermute | solution.py:173
  17.0 0.0 copy-done.1
  17.0 0.1 eq.44
  17.1 2.4 %collective-permute-start.6 = (bf16[96,128]{1,0:T(8,128)(2,1)S(1)}, bf16[96,128]{1,0:T(8,128)(2,1)S(1)}, u32[]{:S(2)}, u32[]{:S(2)}) collective-permute-start(bf16[96,128]{1,0:T(8,128)(2,1)S(1)} %get-tuple-element.66), channel_id=1, source_target_pairs={{0,30},{1,31},{2,28},{3,29},{4,2},{5,3},{6,0},{7,1},{8,6},{9,7},{1... | collective-permute-start | bytes 73736 | tf_op jit(solution)/shard_map/ppermute | solution.py:211
  19.6 0.0 collective-permute-done.2
  19.6 0.0 collective-permute-done.3
  19.6 0.0 collective-permute-done.5
  19.6 0.1 collective-permute-start.4
  19.7 2.2 %collective-permute-done.6 = bf16[96,128]{1,0:T(8,128)(2,1)S(1)} collective-permute-done((bf16[96,128]{1,0:T(8,128)(2,1)S(1)}, bf16[96,128]{1,0:T(8,128)(2,1)S(1)}, u32[]{:S(2)}, u32[]{:S(2)}) %collective-permute-start.6) | collective-permute-done | bytes 24608 | tf_op jit(solution)/shard_map/ppermute | solution.py:211
  21.9 0.1 collective-permute-start.7
  22.0 0.3 convolution_bitcast_fusion.1
  22.3 0.3 convolution_bitcast_fusion.3
  22.6 0.0 collective-permute-done.4
  22.6 0.3 convolution_bitcast_fusion.2
  22.8 0.6 %collective-permute-done.7 = bf16[832,128]{1,0:T(8,128)(2,1)S(1)} collective-permute-done((bf16[832,128]{1,0:T(8,128)(2,1)S(1)}, bf16[832,128]{1,0:T(8,128)(2,1)S(1)}, u32[]{:S(2)}, u32[]{:S(2)}) %collective-permute-start.7) | collective-permute-done | bytes 213024 | tf_op jit(solution)/shard_map/ppermute | solution.py:218
  23.5 0.3 convolution_bitcast_fusion
  23.8 1.0 %collective-permute-start.8 = (bf16[4,128,128]{2,1,0:T(8,128)(2,1)S(1)}, bf16[4,128,128]{2,1,0:T(8,128)(2,1)S(1)}, u32[]{:S(2)}, u32[]{:S(2)}) collective-permute-start(bf16[4,128,128]{2,1,0:T(8,128)(2,1)S(1)} %pad_maximum_fusion), channel_id=1, source_target_pairs={{0,4},{4,0},{8,12},{12,8},{16,20},{20,16},{24,28},{28,24},{1,5},{5... | collective-permute-start | bytes 393224 | tf_op jit(solution)/shard_map/ppermute | solution.py:37
  24.7 0.5 %fusion.1 = f32[729,128]{1,0:T(8,128)S(1)} fusion(s32[729]{0:T(1024)S(1)} %reduce.4, f32[729,128]{1,0:T(8,128)S(1)} %get-tuple-element.52), kind=kOutput, calls=%fused_computation.2 | convolution fusion | flops 136953584 | bytes 749412 | tf_op jit(solution)/shard_map/dot_general | solution.py:42
  25.2 0.5 %fusion.4 = f32[729,128]{1,0:T(8,128)S(1)} fusion(f32[729,128]{1,0:T(8,128)S(1)} %fusion.1, s32[729]{0:T(1024)S(1)} %reduce.4, f32[729,128]{1,0:T(8,128)S(1)} %get-tuple-element.52), kind=kOutput, calls=%fused_computation.6 | convolution fusion | flops 137326832 | bytes 1122660 | tf_op jit(solution)/shard_map/dot_general | solution.py:42
  25.8 0.5 %fusion = f32[729,128]{1,0:T(8,128)S(1)} fusion(s32[729]{0:T(1024)S(1)} %reduce.4, f32[729,128]{1,0:T(8,128)S(1)} %get-tuple-element.52), kind=kOutput, calls=%fused_computation.1 | convolution fusion | flops 136673648 | bytes 749412 | tf_op jit(solution)/shard_map/dot_general | solution.py:42
  26.3 3.1 %collective-permute-done.8 = bf16[4,128,128]{2,1,0:T(8,128)(2,1)S(1)} collective-permute-done((bf16[4,128,128]{2,1,0:T(8,128)(2,1)S(1)}, bf16[4,128,128]{2,1,0:T(8,128)(2,1)S(1)}, u32[]{:S(2)}, u32[]{:S(2)}) %collective-permute-start.8) | collective-permute-done | bytes 131104 | tf_op jit(solution)/shard_map/ppermute | solution.py:37
  29.4 1.6 %collective-permute-start.9 = (bf16[4,128,128]{2,1,0:T(8,128)(2,1)S(1)}, bf16[4,128,128]{2,1,0:T(8,128)(2,1)S(1)}, u32[]{:S(2)}, u32[]{:S(2)}) collective-permute-start(bf16[4,128,128]{2,1,0:T(8,128)(2,1)S(1)} %add_convert_fusion.1), channel_id=1, source_target_pairs={{0,8},{4,12},{8,0},{12,4},{16,24},{20,28},{24,16},{28,20},{1,9},{5... | collective-permute-start | bytes 393224 | tf_op jit(solution)/shard_map/ppermute | solution.py:37
  31.1 3.4 %collective-permute-done.9 = bf16[4,128,128]{2,1,0:T(8,128)(2,1)S(1)} collective-permute-done((bf16[4,128,128]{2,1,0:T(8,128)(2,1)S(1)}, bf16[4,128,128]{2,1,0:T(8,128)(2,1)S(1)}, u32[]{:S(2)}, u32[]{:S(2)}) %collective-permute-start.9) | collective-permute-done | bytes 131104 | tf_op jit(solution)/shard_map/ppermute | solution.py:37
  34.5 2.9 %collective-permute-start.10 = (bf16[4,128,128]{2,1,0:T(8,128)(2,1)S(1)}, bf16[4,128,128]{2,1,0:T(8,128)(2,1)S(1)}, u32[]{:S(2)}, u32[]{:S(2)}) collective-permute-start(bf16[4,128,128]{2,1,0:T(8,128)(2,1)S(1)} %add_convert_fusion), channel_id=1, source_target_pairs={{0,16},{4,20},{8,24},{12,28},{16,0},{20,4},{24,8},{28,12},{1,17},{... | collective-permute-start | bytes 393224 | tf_op jit(solution)/shard_map/ppermute | solution.py:37
  37.4 1.1 %fusion.3 = f32[729,128]{1,0:T(8,128)} fusion(f32[729,128]{1,0:T(8,128)S(1)} %fusion, f32[729,128]{1,0:T(8,128)S(1)} %fusion.4, s32[162]{0:T(256)S(1)} %eq.44, s32[729]{0:T(1024)S(1)} %iota_reduce_fusion, bf16[81,128]{1,0:T(8,128)(2,1)S(1)} %get-tuple-element.72, bf16[81,128]{1,0:T(8,128)(2,1)S(1)} %get-tuple-element.73), kind=kOutput, calls=%fused_computation.5 | convolution fusion | flops 30620754 | bytes 1164780 | tf_op jit(solution)/shard_map/dot_general | solution.py:42
  38.5 4.4 %collective-permute-done.10 = bf16[4,128,128]{2,1,0:T(8,128)(2,1)S(1)} collective-permute-done((bf16[4,128,128]{2,1,0:T(8,128)(2,1)S(1)}, bf16[4,128,128]{2,1,0:T(8,128)(2,1)S(1)}, u32[]{:S(2)}, u32[]{:S(2)}) %collective-permute-start.10) | collective-permute-done | bytes 131104 | tf_op jit(solution)/shard_map/ppermute | solution.py:37
  43.0 0.7 %fusion.11 = f32[512,128]{1,0:T(8,128)} fusion(f32[4,128,128]{2,1,0:T(8,128)S(1)} %add_multiply_fusion, f32[2,2,128,128]{3,2,1,0:T(8,128)S(1)} %get-tuple-element.61, f32[2,2,128,128]{3,2,1,0:T(8,128)S(1)} %pad_maximum_fusion.2, pred[]{:T(512)S(6)} %eq.50, pred[]{:T(512)S(6)} %eq.49), kind=kLoop, calls=%fused_computation.23 | loop fusion | flops 131072 | bytes 1048578 | tf_op jit(solution)/shard_map/jit(_where)/select_n | solution.py:228
  (16 shorter events, 0.4 us)
Async XLA Ops:
  0.6 7.4 %copy-start = (s32[2,81]{1,0:T(2,128)S(1)}, s32[2,81]{1,0:T(2,128)}, u32[]{:S(2)}) copy-start(s32[2,81]{1,0:T(2,128)} %faces.1) | copy-start | bytes 1948
  3.5 5.6 %collective-permute-start = (bf16[96,128]{1,0:T(8,128)(2,1)S(1)}, bf16[96,128]{1,0:T(8,128)(2,1)S(1)}, u32[]{:S(2)}, u32[]{:S(2)}) collective-permute-start(bf16[96,128]{1,0:T(8,128)(2,1)S(1)} %get-tuple-element.71), channel_id=1, source_target_pairs={{0,4},{1,5},{2,6},{3,7},{4,0},{5,1},{6,2},{7,3},{8,12},{9,13},{10,... | collective-permute-start | bytes 73736 | tf_op jit(solution)/shard_map/ppermute | solution.py:173
  6.5 3.8 %collective-permute-start.1 = (bf16[96,128]{1,0:T(8,128)(2,1)S(1)}, bf16[96,128]{1,0:T(8,128)(2,1)S(1)}, u32[]{:S(2)}, u32[]{:S(2)}) collective-permute-start(bf16[96,128]{1,0:T(8,128)(2,1)S(1)} %get-tuple-element.70), channel_id=1, source_target_pairs={{0,2},{1,3},{2,0},{3,1},{4,8},{5,9},{6,10},{7,11},{8,4},{9,5},{10,... | collective-permute-start | bytes 73736 | tf_op jit(solution)/shard_map/ppermute | solution.py:174
  10.3 6.7 %copy-start.1 = (s32[1,729]{1,0:T(1,128)S(1)}, s32[1,729]{1,0:T(1,128)}, u32[]{:S(2)}) copy-start(s32[1,729]{1,0:T(1,128)} %cell_hbm.1) | copy-start | bytes 8752
  11.4 8.2 %collective-permute-start.5 = (bf16[832,128]{1,0:T(8,128)(2,1)S(1)}, bf16[832,128]{1,0:T(8,128)(2,1)S(1)}, u32[]{:S(2)}, u32[]{:S(2)}) collective-permute-start(bf16[832,128]{1,0:T(8,128)(2,1)S(1)} %get-tuple-element.49), channel_id=1, source_target_pairs={{0,2},{1,3},{2,0},{3,1},{4,6},{5,7},{6,4},{7,5},{8,10},{9,11},{10,... | collective-permute-start | bytes 638984 | tf_op jit(solution)/shard_map/ppermute | solution.py:199
  13.0 6.6 %collective-permute-start.2 = (bf16[96,128]{1,0:T(8,128)(2,1)S(1)}, bf16[96,128]{1,0:T(8,128)(2,1)S(1)}, u32[]{:S(2)}, u32[]{:S(2)}) collective-permute-start(bf16[96,128]{1,0:T(8,128)(2,1)S(1)} %get-tuple-element.67), channel_id=1, source_target_pairs={{0,2},{1,3},{2,0},{3,1},{4,8},{5,9},{6,10},{7,11},{8,4},{9,5},{10,... | collective-permute-start | bytes 73736 | tf_op jit(solution)/shard_map/ppermute | solution.py:174
  13.6 6.0 %collective-permute-start.3 = (bf16[96,128]{1,0:T(8,128)(2,1)S(1)}, bf16[96,128]{1,0:T(8,128)(2,1)S(1)}, u32[]{:S(2)}, u32[]{:S(2)}) collective-permute-start(bf16[96,128]{1,0:T(8,128)(2,1)S(1)} %get-tuple-element.65), channel_id=1, source_target_pairs={{0,4},{1,5},{2,6},{3,7},{4,0},{5,1},{6,2},{7,3},{8,12},{9,13},{10,... | collective-permute-start | bytes 73736 | tf_op jit(solution)/shard_map/ppermute | solution.py:173
  17.1 4.8 %collective-permute-start.6 = (bf16[96,128]{1,0:T(8,128)(2,1)S(1)}, bf16[96,128]{1,0:T(8,128)(2,1)S(1)}, u32[]{:S(2)}, u32[]{:S(2)}) collective-permute-start(bf16[96,128]{1,0:T(8,128)(2,1)S(1)} %get-tuple-element.66), channel_id=1, source_target_pairs={{0,30},{1,31},{2,28},{3,29},{4,2},{5,3},{6,0},{7,1},{8,6},{9,7},{1... | collective-permute-start | bytes 73736 | tf_op jit(solution)/shard_map/ppermute | solution.py:211
  19.6 2.9 %collective-permute-start.4 = (bf16[832,128]{1,0:T(8,128)(2,1)S(1)}, bf16[832,128]{1,0:T(8,128)(2,1)S(1)}, u32[]{:S(2)}, u32[]{:S(2)}) collective-permute-start(bf16[832,128]{1,0:T(8,128)(2,1)S(1)} %get-tuple-element.56), channel_id=1, source_target_pairs={{0,1},{1,0},{2,3},{3,2},{4,5},{5,4},{6,7},{7,6},{8,9},{9,8},{10,11... | collective-permute-start | bytes 638984 | tf_op jit(solution)/shard_map/ppermute | solution.py:218
  21.9 1.5 %collective-permute-start.7 = (bf16[832,128]{1,0:T(8,128)(2,1)S(1)}, bf16[832,128]{1,0:T(8,128)(2,1)S(1)}, u32[]{:S(2)}, u32[]{:S(2)}) collective-permute-start(bf16[832,128]{1,0:T(8,128)(2,1)S(1)} %fusion.18), channel_id=1, source_target_pairs={{0,1},{1,0},{2,3},{3,2},{4,5},{5,4},{6,7},{7,6},{8,9},{9,8},{10,11... | collective-permute-start | bytes 638984 | tf_op jit(solution)/shard_map/ppermute | solution.py:218
  23.8 5.6 %collective-permute-start.8 = (bf16[4,128,128]{2,1,0:T(8,128)(2,1)S(1)}, bf16[4,128,128]{2,1,0:T(8,128)(2,1)S(1)}, u32[]{:S(2)}, u32[]{:S(2)}) collective-permute-start(bf16[4,128,128]{2,1,0:T(8,128)(2,1)S(1)} %pad_maximum_fusion), channel_id=1, source_target_pairs={{0,4},{4,0},{8,12},{12,8},{16,20},{20,16},{24,28},{28,24},{1,5},{5... | collective-permute-start | bytes 393224 | tf_op jit(solution)/shard_map/ppermute | solution.py:37
  29.4 5.0 %collective-permute-start.9 = (bf16[4,128,128]{2,1,0:T(8,128)(2,1)S(1)}, bf16[4,128,128]{2,1,0:T(8,128)(2,1)S(1)}, u32[]{:S(2)}, u32[]{:S(2)}) collective-permute-start(bf16[4,128,128]{2,1,0:T(8,128)(2,1)S(1)} %add_convert_fusion.1), channel_id=1, source_target_pairs={{0,8},{4,12},{8,0},{12,4},{16,24},{20,28},{24,16},{28,20},{1,9},{5... | collective-permute-start | bytes 393224 | tf_op jit(solution)/shard_map/ppermute | solution.py:37
  34.5 8.3 %collective-permute-start.10 = (bf16[4,128,128]{2,1,0:T(8,128)(2,1)S(1)}, bf16[4,128,128]{2,1,0:T(8,128)(2,1)S(1)}, u32[]{:S(2)}, u32[]{:S(2)}) collective-permute-start(bf16[4,128,128]{2,1,0:T(8,128)(2,1)S(1)} %add_convert_fusion), channel_id=1, source_target_pairs={{0,16},{4,20},{8,24},{12,28},{16,0},{20,4},{24,8},{28,12},{1,17},{... | collective-permute-start | bytes 393224 | tf_op jit(solution)/shard_map/ppermute | solution.py:37

commit v3 on v2

--- a/solution.py
+++ b/solution.py
@@ -28,13 +28,23 @@
     return [(source, turn(source, stride, radix, by)) for source in range(count)]
 
 
-def sum_over(axis, value):
-    count = lax.axis_size(axis)
-    for stride, radix in digits(count):
+def sum_over_cells(value):
+    parts, groups = lax.axis_size("cells"), lax.axis_size("bands")
+    binary = [stride for stride, radix in digits(parts) if radix == 2]
+    other = [(stride, radix) for stride, radix in digits(parts) if radix != 2]
+    masks = [stride + (stride // 2 if stride > 2 else 0) for stride in binary]
+    steps = [[(mask, masks[at - 1])] for at, mask in enumerate(masks)]
+    steps = [[lambda part, band, m=m: part ^ m[band % 2] for m in step] for step in steps]
+    for stride, radix in other:
+        steps.append([lambda part, band, d=(stride, radix, by): turn(part, *d) for by in range(1, radix)])
+    for step in steps:
         word = value.astype(BF16)
         value = word.astype(F32)
-        for by in range(1, radix):
-            value = value + lax.ppermute(word, axis, turned(count, stride, radix, by)).astype(F32)
+        for move in step:
+            pairs = [
+                (part * groups + band, move(part, band) * groups + band) for part in range(parts) for band in range(groups)
+            ]
+            value = value + lax.ppermute(word, ("cells", "bands"), pairs).astype(F32)
     return value
 
 
@@ -50,14 +60,24 @@
     return jnp.where(flags, jnp.float32(1), jnp.float32(0)).astype(BF16)
 
 
+def row_chunks(count):
+    return [(first, min(first + 256, count)) for first in range(0, count, 256)]
+
+
+def tall_dot(rows_of, values):
+    return jnp.concatenate([dot(rows_of(first, last), values) for first, last in row_chunks(values.shape[0])], axis=0)
+
+
 def first_kernel(waves_hbm, cell_hbm, faces_hbm, ham_hbm, start, local, sums, ham, one, columns, waves, cell, faces, rows, sems):
-    pairs = ((cell_hbm, cell), (faces_hbm, faces), (waves_hbm, waves), (ham_hbm.at[0], ham))
+    count = waves.shape[0]
+    shared = faces.shape[1]
+    padded = one.shape[0] // 2
+    chunks = row_chunks(count)
+    pairs = [(cell_hbm, cell), (faces_hbm, faces), (waves_hbm, waves)]
+    pairs += [(ham_hbm.at[0, first:last], ham.at[first:last]) for first, last in chunks]
     copies = [pltpu.make_async_copy(source, target, sems.at[at]) for at, (source, target) in enumerate(pairs)]
     for copy in copies:
         copy.start()
-    count = waves.shape[0]
-    shared = faces.shape[1]
-    padded = one.shape[0] // 2
     rows[...] = jnp.full(rows.shape, -1, F32)
     copies[0].wait()
     copies[1].wait()
@@ -71,12 +91,12 @@
     pick = one_hot(jnp.concatenate([turned_rows[:padded, 1:2], turned_rows[:padded, 2:3]], axis=0) == row)
     one[...] = pick
     copies[2].wait()
-    begin = dot(place, waves[...]).astype(BF16)
+    begin = tall_dot(lambda first, last: place[first:last], waves[...]).astype(BF16)
     start[...] = begin
-    copies[3].wait()
-    result = dot(ham[...], begin)
-    local[...] = result
-    sums[...] = dot(pick, result.astype(BF16)).astype(BF16)
+    for at, (first, last) in enumerate(chunks):
+        copies[3 + at].wait()
+        local[first:last] = dot(ham[first:last], begin)
+    sums[...] = dot(pick, local[...].astype(BF16)).astype(BF16)
 
 
 def middle_kernel(ends, columns, faces, one_t, keep):
@@ -103,13 +123,15 @@
     head = block.shape[0] - padded
     halo = jnp.concatenate([before[...], after[...]], axis=0)
     newer = 0.5 * (local[...] + dot(one_t[...], halo))
-    result = dot(ham[...], newer.astype(BF16))
+    width = local.shape[1]
+    result = tall_dot(lambda first, last: ham[first:last], newer.astype(BF16))
     rest = result - start[...].astype(F32)
     partial[...] = rest
-    sums[...] = dot(one[...], result.astype(BF16)).astype(BF16)
-    block[count:head, :] = jnp.zeros((head - count, block.shape[1]), BF16)
+    on_faces = dot(one[...], jnp.concatenate([result.astype(BF16), rest.astype(BF16)], axis=1)).astype(BF16)
+    sums[...] = on_faces[:, :width]
+    block[count:head, :] = jnp.zeros((head - count, width), BF16)
     block[:count, :] = (rest * keep[...]).astype(BF16)
-    block[head:, :] = dot(one[padded:, :], rest.astype(BF16)).astype(BF16)
+    block[head:, :] = on_faces[padded:, width:]
 
 
 def vmem(count):
@@ -147,7 +169,7 @@
             pltpu.VMEM(connectivity.shape, jnp.int32),
             pltpu.VMEM(face_nodes.shape, jnp.int32),
             pltpu.VMEM((8, lanes), F32),
-            pltpu.SemaphoreType.DMA((4,)),
+            pltpu.SemaphoreType.DMA((3 + len(row_chunks(node_count)),)),
         ],
         compiler_params=params,
     )(*(pltpu.with_memory_space_constraint(x, pltpu.HBM) for x in (wavefunctions, connectivity, face_nodes, hamiltonians)))
@@ -191,34 +213,47 @@
         compiler_params=params,
     )(local, before, after, ham, start, one, one_t, keep)
 
+    core, chips = digits(groups)[:1], digits(groups)[1:]
+    low = sums[:padded]
+    has_after = place < parts - 1
     blocks = {0: block}
-    tails = {}
-    for stride, radix in digits(groups)[1:]:
+    for stride, radix in chips:
         for at in list(blocks):
             for by in range(1, radix):
                 blocks[at + by * stride] = lax.ppermute(blocks[at], "bands", turned(groups, stride, radix, radix - by))
+    raw = {}
+    for stride, radix in core:
+        for by in range(1, radix):
+            raw[by * stride] = lax.ppermute(block, "bands", turned(groups, stride, radix, radix - by))
     before, after = neighbours(sums)
-    has_after = place < parts - 1
-    tails[0] = after
+    tails = {0: jnp.where(has_after, after, jnp.zeros_like(after))}
+    blocks[0] = blocks[0].at[head:].add(tails[0])
     for at in list(blocks)[1:]:
         pairs = []
         for part in range(parts):
             for band in range(groups):
                 target = band
-                for stride, radix in digits(groups)[1:]:
+                for stride, radix in chips:
                     target = turn(target, stride, radix, radix - at // stride % radix)
                 pairs.append((part * groups + band, (part - 1) % parts * groups + target))
-        tails[at] = lax.ppermute(sums[:padded], both, pairs)
-    for at in list(blocks):
-        tail = jnp.where(has_after, tails[at], jnp.zeros_like(tails[at]))
-        blocks[at] = blocks[at].at[head:].add(tail)
-    for stride, radix in digits(groups)[:1]:
-        for at in list(blocks):
-            for by in range(1, radix):
-                blocks[at + by * stride] = lax.ppermute(blocks[at], "bands", turned(groups, stride, radix, radix - by))
+        tail = lax.ppermute(low, both, pairs)
+        tails[at] = jnp.where(has_after, tail, jnp.zeros_like(tail))
+        blocks[at] = blocks[at].at[head:].add(tails[at])
+    after = tails[0]
+    relayed = jnp.concatenate([after] + [blocks[at] for at in list(blocks)[1:]])
+    for stride, radix in core:
+        for by in range(1, radix):
+            got = lax.ppermute(relayed, "bands", turned(groups, stride, radix, radix - by))
+            raw[by * stride] = raw[by * stride].at[head:].add(got[:padded])
+            for place_at, at in enumerate(list(blocks)[1:]):
+                first = padded + place_at * block.shape[0]
+                raw[at + by * stride] = got[first : first + block.shape[0]]
+    blocks.update(raw)
     gram = jnp.stack([dot_t(blocks[at], blocks[0]) for at in range(groups)])
+
     gram, partial, before, after = lax.optimization_barrier((gram, partial, before, after))
-    total = sum_over("cells", gram) * (1.0 / (parts * node_count))
+    total = sum_over_cells(gram) * (1.0 / (parts * node_count))
+    before = jnp.where(place > 0, before, jnp.zeros_like(before))
     radices = digits(groups)
     total = total.reshape(tuple(radix for _, radix in reversed(radices)) + (width, width))
     for at, (stride, radix) in enumerate(radices):
@@ -229,8 +264,6 @@
         total = moved
     correlation = total.reshape(groups * width, width)
 
-    before = jnp.where(place > 0, before, jnp.zeros_like(before))[:shared]
-    after = jnp.where(has_after, after, jnp.zeros_like(after))[:shared]
     nodes = lax.broadcasted_iota(jnp.int32, (node_count, node_count), 0)
     place_of = (nodes == connectivity).astype(BF16)
     face_of = (face_nodes.reshape(-1)[None, :] == nodes[:, :1]).astype(BF16)
@@ -238,7 +271,7 @@
     rest = partial - top.astype(F32)
     middle = rest.astype(BF16)
     small = (rest - middle.astype(F32)).astype(BF16)
-    halo = jnp.concatenate([before, after])
+    halo = jnp.concatenate([before[:shared], after[:shared]])
     filtered = dot(place_of, small) + dot(place_of, middle) + dot(face_of, halo) + dot(place_of, top)
     return filtered, correlation
 

time: 43.9 us -> 41 us (0.934)
  starting transfers between devices: 18.2 us -> 13 us
  waiting for transfers between devices: 14.9 us -> 17.5 us
    ppermute x2, starting transfers between devices: 6.44 us -> 3.05 us  [neighbours(): even_odd = lax.ppermute(jnp.where(odd, low, high), both, pair_swap(0))]
    ppermute x2, waiting for transfers between devices: 0.01 us -> 2.84 us  [neighbours(): even_odd = lax.ppermute(jnp.where(odd, low, high), both, pair_swap(0))]
    ppermute x4 -> x6, starting transfers between devices: 7.95 us -> 6.38 us  [the longest x1 3.57 us: body(): tail = lax.ppermute(low, both, pairs)]
    ppermute x3 -> x1, waiting for transfers between devices: 0.65 us -> 0.01 us  [body(): lax.ppermute(blocks[at], 'bands', turned(groups, stride, radix, radix - by))]
    ppermute x4 -> x6, waiting for transfers between devices: 13.1 us -> 13.3 us  [the longest x3 11.6 us: sum_over_cells(): value = value + lax.ppermute(word, ('cells', 'bands'), pairs).astype(F32)]
    ppermute x3 -> x1, starting transfers between devices: 1.73 us -> 1.58 us  [body(): lax.ppermute(blocks[at], 'bands', turned(groups, stride, radix, radix - by))]
  transfers between devices with their start and end apart: 11 -> 11, of which waited for: 6 -> 8; matrix products, arithmetic and copies ran while one was open for 8% -> 8% of each run, Pallas kernels for 2% -> 2%
where the time goes in v3:
time: 41 us; the launch traced here: 40.9 us
  waiting for transfers between devices  17.5 us (43%)
  starting transfers between devices  13 us (32%)
  Pallas kernels  4.57 us (11%)
  matrix products  3.61 us (9%)
  other arithmetic  1.15 us (3%)
  between operations  0.86 us (2%)
    ppermute x3, waiting for transfers between devices, sum_over_cells(): value = value + lax.ppermute(word, ('cells', 'bands'), pairs).astype(F32)  11.6 us
    ppermute x1, starting transfers between devices, body(): tail = lax.ppermute(low, both, pairs)  3.57 us
    ppermute x2, starting transfers between devices, neighbours(): even_odd = lax.ppermute(jnp.where(odd, low, high), both, pair_swap(0))  3.05 us
    ppermute x2, waiting for transfers between devices, neighbours(): even_odd = lax.ppermute(jnp.where(odd, low, high), both, pair_swap(0))  2.84 us
    ppermute x3, starting transfers between devices, sum_over_cells(): value = value + lax.ppermute(word, ('cells', 'bands'), pairs).astype(F32)  2.67 us
    pallas_call x1, Pallas kernels, body(): pl.pallas_call(first_kernel, out_shape=(shape(nodal, BF16), shape(nodal,...  2.65 us
    dot_general x4, matrix products, dot(): return jnp.dot(a, b, preferred_element_type=F32)  2.57 us
    ppermute x2, starting transfers between devices, neighbours(): odd_even = lax.ppermute(jnp.where(odd, high, low), both, pair_swap(1))  2.02 us
  transfers between devices with their start and end apart: 11, of which 8 were waited for; matrix products, arithmetic and copies ran while one was open for 8% of the time, Pallas kernels for 2%

profile of v3, /device:TPU:0, one launch (start us, length us, event | category | flops | bytes accessed | tf_op | source)
XLA Modules:
  0.0 40.9 jit_solution(10239944123892596228)
XLA Ops:
  0.6 0.0 copy-start
  0.7 2.6 %shard_map.59 = (bf16[729,128]{1,0:T(8,128)(2,1)S(1)}, f32[729,128]{1,0:T(8,128)S(1)}, bf16[192,128]{1,0:T(8,128)(2,1)S(1)}, bf16[729,729]{1,0:T(8,128)(2,1)S(1)...) custom-call(bf16[729,128]{1,0:T(8,128)(2,1)} %waves_hbm.1, s32[1,729]{1,0:T(1,128)} %cell_hbm.1, s32[2,81]{1,0:T(2,128)} %faces.1, ...), custom_call_target="tpu_custom_call" | custom-call | tf_op jit(solution)/shard_map/pallas_call | solution.py:155
  3.3 3.0 %collective-permute-start = (bf16[96,128]{1,0:T(8,128)(2,1)S(1)}, bf16[96,128]{1,0:T(8,128)(2,1)S(1)}, u32[]{:S(2)}, u32[]{:S(2)}) collective-permute-start(bf16[96,128]{1,0:T(8,128)(2,1)S(1)} %get-tuple-element.83), channel_id=1, source_target_pairs={{0,4},{1,5},{2,6},{3,7},{4,0},{5,1},{6,2},{7,3},{8,12},{9,13},{10,... | collective-permute-start | bytes 73736 | tf_op jit(solution)/shard_map/ppermute | solution.py:195
  6.3 1.5 %collective-permute-start.1 = (bf16[96,128]{1,0:T(8,128)(2,1)S(1)}, bf16[96,128]{1,0:T(8,128)(2,1)S(1)}, u32[]{:S(2)}, u32[]{:S(2)}) collective-permute-start(bf16[96,128]{1,0:T(8,128)(2,1)S(1)} %get-tuple-element.82), channel_id=1, source_target_pairs={{0,2},{1,3},{2,0},{3,1},{4,8},{5,9},{6,10},{7,11},{8,4},{9,5},{10,... | collective-permute-start | bytes 73736 | tf_op jit(solution)/shard_map/ppermute | solution.py:196
  7.8 0.1 pad_add_fusion.ends
  7.9 0.0 copy-done
  7.9 1.0 %shard_map.60 = (bf16[729,192]{1,0:T(8,128)(2,1)S(1)}, f32[729,128]{1,0:T(8,128)S(1)}) custom-call(s32[2]{0:T(128)S(1)} %pad_add_fusion.ends, f32[768,8]{1,0:T(8,128)S(1)} %get-tuple-element.58.columns, s32[2,81]{1,0:T(2,128)S(1)} %copy-done), custom_call_target="tpu_custom_call" | custom-call | tf_op jit(solution)/shard_map/pallas_call | solution.py:201
  8.9 0.0 collective-permute-done
  9.0 1.2 %collective-permute-done.1 = bf16[96,128]{1,0:T(8,128)(2,1)S(1)} collective-permute-done((bf16[96,128]{1,0:T(8,128)(2,1)S(1)}, bf16[96,128]{1,0:T(8,128)(2,1)S(1)}, u32[]{:S(2)}, u32[]{:S(2)}) %collective-permute-start.1) | collective-permute-done | bytes 24608 | tf_op jit(solution)/shard_map/ppermute | solution.py:196
  10.2 0.0 copy-start.1
  10.2 0.9 %shard_map.61 = (f32[729,128]{1,0:T(8,128)S(1)}, bf16[832,128]{1,0:T(8,128)(2,1)S(1)}, bf16[192,128]{1,0:T(8,128)(2,1)S(1)}) custom-call(f32[729,128]{1,0:T(8,128)S(1)} %get-tuple-element.53.local, bf16[96,128]{1,0:T(8,128)(2,1)S(1)} %get-tuple-element.81.before, bf16[96,128]{1,0:T(8,128)(2,1)S(1)} %get-tuple-element.80.after, ...), custom_call_target="tpu_custom_call" | custom-call | tf_op jit(solution)/shard_map/pallas_call | solution.py:208
  11.1 1.6 %collective-permute-start.5 = (bf16[832,128]{1,0:T(8,128)(2,1)S(1)}, bf16[832,128]{1,0:T(8,128)(2,1)S(1)}, u32[]{:S(2)}, u32[]{:S(2)}) collective-permute-start(bf16[832,128]{1,0:T(8,128)(2,1)S(1)} %get-tuple-element.61), channel_id=1, source_target_pairs={{0,2},{1,3},{2,0},{3,1},{4,6},{5,7},{6,4},{7,5},{8,10},{9,11},{10,... | collective-permute-start | bytes 638984 | tf_op jit(solution)/shard_map/ppermute | solution.py:223
  12.7 3.6 %collective-permute-start.6 = (bf16[96,128]{1,0:T(8,128)(2,1)S(1)}, bf16[96,128]{1,0:T(8,128)(2,1)S(1)}, u32[]{:S(2)}, u32[]{:S(2)}) collective-permute-start(bf16[96,128]{1,0:T(8,128)(2,1)S(1)} %get-tuple-element.77), channel_id=1, source_target_pairs={{0,30},{1,31},{2,28},{3,29},{4,2},{5,3},{6,0},{7,1},{8,6},{9,7},{1... | collective-permute-start | bytes 73736 | tf_op jit(solution)/shard_map/ppermute | solution.py:239
  16.3 0.0 copy-done.1
  16.3 0.1 eq.44
  16.4 0.1 collective-permute-start.4
  16.5 0.5 %collective-permute-start.2 = (bf16[96,128]{1,0:T(8,128)(2,1)S(1)}, bf16[96,128]{1,0:T(8,128)(2,1)S(1)}, u32[]{:S(2)}, u32[]{:S(2)}) collective-permute-start(bf16[96,128]{1,0:T(8,128)(2,1)S(1)} %get-tuple-element.79), channel_id=1, source_target_pairs={{0,1},{1,0},{2,3},{3,2},{4,8},{5,9},{6,10},{7,11},{8,4},{9,5},{10,... | collective-permute-start | bytes 73736 | tf_op jit(solution)/shard_map/ppermute | solution.py:196
  17.0 0.1 collective-permute-start.3
  17.0 0.8 %collective-permute-done.6 = bf16[96,128]{1,0:T(8,128)(2,1)S(1)} collective-permute-done((bf16[96,128]{1,0:T(8,128)(2,1)S(1)}, bf16[96,128]{1,0:T(8,128)(2,1)S(1)}, u32[]{:S(2)}, u32[]{:S(2)}) %collective-permute-start.6) | collective-permute-done | bytes 24608 | tf_op jit(solution)/shard_map/ppermute | solution.py:239
  17.8 0.0 collective-permute-done.5
  17.8 0.1 collective-permute-done.2
  17.9 2.8 %collective-permute-done.3 = bf16[96,128]{1,0:T(8,128)(2,1)S(1)} collective-permute-done((bf16[96,128]{1,0:T(8,128)(2,1)S(1)}, bf16[96,128]{1,0:T(8,128)(2,1)S(1)}, u32[]{:S(2)}, u32[]{:S(2)}) %collective-permute-start.3) | collective-permute-done | bytes 24608 | tf_op jit(solution)/shard_map/ppermute | solution.py:195
  20.8 0.0 collective-permute-done.4
  20.8 0.1 collective-permute-start.7
  20.9 0.3 convolution_bitcast_fusion.1
  21.2 0.3 convolution_bitcast_fusion.3
  21.5 1.0 %collective-permute-done.7 = bf16[928,128]{1,0:T(8,128)(2,1)S(1)} collective-permute-done((bf16[928,128]{1,0:T(8,128)(2,1)S(1)}, bf16[928,128]{1,0:T(8,128)(2,1)S(1)}, u32[]{:S(2)}, u32[]{:S(2)}) %collective-permute-start.7) | collective-permute-done | bytes 237600 | tf_op jit(solution)/shard_map/ppermute | solution.py:246
  22.4 0.3 convolution_bitcast_fusion.2
  22.7 0.3 convolution_bitcast_fusion
  23.0 0.1 collective-permute-start.8
  23.1 0.5 %fusion.1 = f32[729,128]{1,0:T(8,128)S(1)} fusion(s32[729]{0:T(1024)S(1)} %reduce.6, f32[729,128]{1,0:T(8,128)S(1)} %get-tuple-element.64), kind=kOutput, calls=%fused_computation.2 | convolution fusion | flops 136953584 | bytes 749412 | tf_op jit(solution)/shard_map/dot_general | solution.py:52
  23.6 0.5 %fusion.4 = f32[729,128]{1,0:T(8,128)S(1)} fusion(f32[729,128]{1,0:T(8,128)S(1)} %fusion.1, s32[729]{0:T(1024)S(1)} %reduce.6, f32[729,128]{1,0:T(8,128)S(1)} %get-tuple-element.64), kind=kOutput, calls=%fused_computation.6 | convolution fusion | flops 137326832 | bytes 1122660 | tf_op jit(solution)/shard_map/dot_general | solution.py:52
  24.1 0.5 %fusion = f32[729,128]{1,0:T(8,128)S(1)} fusion(s32[729]{0:T(1024)S(1)} %reduce.6, f32[729,128]{1,0:T(8,128)S(1)} %get-tuple-element.64), kind=kOutput, calls=%fused_computation.1 | convolution fusion | flops 136673648 | bytes 749412 | tf_op jit(solution)/shard_map/dot_general | solution.py:52
  24.6 3.4 %collective-permute-done.8 = bf16[4,128,128]{2,1,0:T(8,128)(2,1)S(1)} collective-permute-done((bf16[4,128,128]{2,1,0:T(8,128)(2,1)S(1)}, bf16[4,128,128]{2,1,0:T(8,128)(2,1)S(1)}, u32[]{:S(2)}, u32[]{:S(2)}) %collective-permute-start.8) | collective-permute-done | bytes 131104 | tf_op jit(solution)/shard_map/ppermute | solution.py:47
  28.1 0.1 collective-permute-start.9
  28.2 4.9 %collective-permute-done.9 = bf16[4,128,128]{2,1,0:T(8,128)(2,1)S(1)} collective-permute-done((bf16[4,128,128]{2,1,0:T(8,128)(2,1)S(1)}, bf16[4,128,128]{2,1,0:T(8,128)(2,1)S(1)}, u32[]{:S(2)}, u32[]{:S(2)}) %collective-permute-start.9) | collective-permute-done | bytes 131104 | tf_op jit(solution)/shard_map/ppermute | solution.py:47
  33.1 2.5 %collective-permute-start.10 = (bf16[4,128,128]{2,1,0:T(8,128)(2,1)S(1)}, bf16[4,128,128]{2,1,0:T(8,128)(2,1)S(1)}, u32[]{:S(2)}, u32[]{:S(2)}) collective-permute-start(bf16[4,128,128]{2,1,0:T(8,128)(2,1)S(1)} %add_convert_fusion), channel_id=1, source_target_pairs={{0,24},{1,9},{2,26},{3,11},{4,28},{5,13},{6,30},{7,15},{8,16},{9,1... | collective-permute-start | bytes 393224 | tf_op jit(solution)/shard_map/ppermute | solution.py:47
  35.6 1.1 %fusion.3 = f32[729,128]{1,0:T(8,128)} fusion(f32[729,128]{1,0:T(8,128)S(1)} %fusion, f32[729,128]{1,0:T(8,128)S(1)} %fusion.4, s32[162]{0:T(256)S(1)} %eq.44, s32[729]{0:T(1024)S(1)} %iota_reduce_fusion, bf16[81,128]{1,0:T(8,128)(2,1)S(1)} %slice.112, bf16[81,128]{1,0:T(8,128)(2,1)S(1)} %slice_select_fusion), kind=kOutput, calls=%fused_computation.5 | convolution fusion | flops 30620754 | bytes 1164780 | tf_op jit(solution)/shard_map/dot_general | solution.py:52
  36.7 3.3 %collective-permute-done.10 = bf16[4,128,128]{2,1,0:T(8,128)(2,1)S(1)} collective-permute-done((bf16[4,128,128]{2,1,0:T(8,128)(2,1)S(1)}, bf16[4,128,128]{2,1,0:T(8,128)(2,1)S(1)}, u32[]{:S(2)}, u32[]{:S(2)}) %collective-permute-start.10) | collective-permute-done | bytes 131104 | tf_op jit(solution)/shard_map/ppermute | solution.py:47
  40.1 0.7 %fusion.11 = f32[512,128]{1,0:T(8,128)} fusion(f32[4,128,128]{2,1,0:T(8,128)S(1)} %add_multiply_fusion, f32[2,2,128,128]{3,2,1,0:T(8,128)S(1)} %get-tuple-element.73, f32[2,2,128,128]{3,2,1,0:T(8,128)S(1)} %pad_maximum_fusion.2, pred[]{:T(512)S(6)} %eq.50, pred[]{:T(512)S(6)} %eq.49), kind=kLoop, calls=%fused_computation.23 | loop fusion | flops 131072 | bytes 1048578 | tf_op jit(solution)/shard_map/jit(_where)/select_n | solution.py:263
  (19 shorter events, 0.4 us)
Async XLA Ops:
  0.6 7.3 %copy-start = (s32[2,81]{1,0:T(2,128)S(1)}, s32[2,81]{1,0:T(2,128)}, u32[]{:S(2)}) copy-start(s32[2,81]{1,0:T(2,128)} %faces.1) | copy-start | bytes 1948
  3.3 5.6 %collective-permute-start = (bf16[96,128]{1,0:T(8,128)(2,1)S(1)}, bf16[96,128]{1,0:T(8,128)(2,1)S(1)}, u32[]{:S(2)}, u32[]{:S(2)}) collective-permute-start(bf16[96,128]{1,0:T(8,128)(2,1)S(1)} %get-tuple-element.83), channel_id=1, source_target_pairs={{0,4},{1,5},{2,6},{3,7},{4,0},{5,1},{6,2},{7,3},{8,12},{9,13},{10,... | collective-permute-start | bytes 73736 | tf_op jit(solution)/shard_map/ppermute | solution.py:195
  6.3 3.8 %collective-permute-start.1 = (bf16[96,128]{1,0:T(8,128)(2,1)S(1)}, bf16[96,128]{1,0:T(8,128)(2,1)S(1)}, u32[]{:S(2)}, u32[]{:S(2)}) collective-permute-start(bf16[96,128]{1,0:T(8,128)(2,1)S(1)} %get-tuple-element.82), channel_id=1, source_target_pairs={{0,2},{1,3},{2,0},{3,1},{4,8},{5,9},{6,10},{7,11},{8,4},{9,5},{10,... | collective-permute-start | bytes 73736 | tf_op jit(solution)/shard_map/ppermute | solution.py:196
  10.2 6.1 %copy-start.1 = (s32[1,729]{1,0:T(1,128)S(1)}, s32[1,729]{1,0:T(1,128)}, u32[]{:S(2)}) copy-start(s32[1,729]{1,0:T(1,128)} %cell_hbm.1) | copy-start | bytes 8752
  11.1 6.7 %collective-permute-start.5 = (bf16[832,128]{1,0:T(8,128)(2,1)S(1)}, bf16[832,128]{1,0:T(8,128)(2,1)S(1)}, u32[]{:S(2)}, u32[]{:S(2)}) collective-permute-start(bf16[832,128]{1,0:T(8,128)(2,1)S(1)} %get-tuple-element.61), channel_id=1, source_target_pairs={{0,2},{1,3},{2,0},{3,1},{4,6},{5,7},{6,4},{7,5},{8,10},{9,11},{10,... | collective-permute-start | bytes 638984 | tf_op jit(solution)/shard_map/ppermute | solution.py:223
  12.7 5.1 %collective-permute-start.6 = (bf16[96,128]{1,0:T(8,128)(2,1)S(1)}, bf16[96,128]{1,0:T(8,128)(2,1)S(1)}, u32[]{:S(2)}, u32[]{:S(2)}) collective-permute-start(bf16[96,128]{1,0:T(8,128)(2,1)S(1)} %get-tuple-element.77), channel_id=1, source_target_pairs={{0,30},{1,31},{2,28},{3,29},{4,2},{5,3},{6,0},{7,1},{8,6},{9,7},{1... | collective-permute-start | bytes 73736 | tf_op jit(solution)/shard_map/ppermute | solution.py:239
  16.4 4.4 %collective-permute-start.4 = (bf16[832,128]{1,0:T(8,128)(2,1)S(1)}, bf16[832,128]{1,0:T(8,128)(2,1)S(1)}, u32[]{:S(2)}, u32[]{:S(2)}) collective-permute-start(bf16[832,128]{1,0:T(8,128)(2,1)S(1)} %get-tuple-element.61), channel_id=1, source_target_pairs={{0,1},{1,0},{2,3},{3,2},{4,5},{5,4},{6,7},{7,6},{8,9},{9,8},{10,11... | collective-permute-start | bytes 638984 | tf_op jit(solution)/shard_map/ppermute | solution.py:227
  16.5 1.5 %collective-permute-start.2 = (bf16[96,128]{1,0:T(8,128)(2,1)S(1)}, bf16[96,128]{1,0:T(8,128)(2,1)S(1)}, u32[]{:S(2)}, u32[]{:S(2)}) collective-permute-start(bf16[96,128]{1,0:T(8,128)(2,1)S(1)} %get-tuple-element.79), channel_id=1, source_target_pairs={{0,1},{1,0},{2,3},{3,2},{4,8},{5,9},{6,10},{7,11},{8,4},{9,5},{10,... | collective-permute-start | bytes 73736 | tf_op jit(solution)/shard_map/ppermute | solution.py:196
  17.0 3.8 %collective-permute-start.3 = (bf16[96,128]{1,0:T(8,128)(2,1)S(1)}, bf16[96,128]{1,0:T(8,128)(2,1)S(1)}, u32[]{:S(2)}, u32[]{:S(2)}) collective-permute-start(bf16[96,128]{1,0:T(8,128)(2,1)S(1)} %get-tuple-element.78), channel_id=1, source_target_pairs={{0,4},{1,5},{2,6},{3,7},{4,0},{5,1},{6,2},{7,3},{8,12},{9,13},{10,... | collective-permute-start | bytes 73736 | tf_op jit(solution)/shard_map/ppermute | solution.py:195
  20.8 1.6 %collective-permute-start.7 = (bf16[928,128]{1,0:T(8,128)(2,1)S(1)}, bf16[928,128]{1,0:T(8,128)(2,1)S(1)}, u32[]{:S(2)}, u32[]{:S(2)}) collective-permute-start(bf16[928,128]{1,0:T(8,128)(2,1)S(1)} %pad_maximum_fusion.3), channel_id=1, source_target_pairs={{0,1},{1,0},{2,3},{3,2},{4,5},{5,4},{6,7},{7,6},{8,9},{9,8},{10,11... | collective-permute-start | bytes 712712 | tf_op jit(solution)/shard_map/ppermute | solution.py:246
  23.0 5.0 %collective-permute-start.8 = (bf16[4,128,128]{2,1,0:T(8,128)(2,1)S(1)}, bf16[4,128,128]{2,1,0:T(8,128)(2,1)S(1)}, u32[]{:S(2)}, u32[]{:S(2)}) collective-permute-start(bf16[4,128,128]{2,1,0:T(8,128)(2,1)S(1)} %pad_maximum_fusion), channel_id=1, source_target_pairs={{0,4},{1,25},{2,6},{3,27},{4,0},{5,29},{6,2},{7,31},{8,12},{9,17},... | collective-permute-start | bytes 393224 | tf_op jit(solution)/shard_map/ppermute | solution.py:47
  28.1 5.0 %collective-permute-start.9 = (bf16[4,128,128]{2,1,0:T(8,128)(2,1)S(1)}, bf16[4,128,128]{2,1,0:T(8,128)(2,1)S(1)}, u32[]{:S(2)}, u32[]{:S(2)}) collective-permute-start(bf16[4,128,128]{2,1,0:T(8,128)(2,1)S(1)} %add_convert_fusion.1), channel_id=1, source_target_pairs={{0,8},{1,5},{2,10},{3,7},{4,12},{5,1},{6,14},{7,3},{8,0},{9,13},{1... | collective-permute-start | bytes 393224 | tf_op jit(solution)/shard_map/ppermute | solution.py:47
  33.1 6.8 %collective-permute-start.10 = (bf16[4,128,128]{2,1,0:T(8,128)(2,1)S(1)}, bf16[4,128,128]{2,1,0:T(8,128)(2,1)S(1)}, u32[]{:S(2)}, u32[]{:S(2)}) collective-permute-start(bf16[4,128,128]{2,1,0:T(8,128)(2,1)S(1)} %add_convert_fusion), channel_id=1, source_target_pairs={{0,24},{1,9},{2,26},{3,11},{4,28},{5,13},{6,30},{7,15},{8,16},{9,1... | collective-permute-start | bytes 393224 | tf_op jit(solution)/shard_map/ppermute | solution.py:47

commit v4 on v3

--- a/solution.py
+++ b/solution.py
@@ -93,9 +93,9 @@
     copies[2].wait()
     begin = tall_dot(lambda first, last: place[first:last], waves[...]).astype(BF16)
     start[...] = begin
-    for at, (first, last) in enumerate(chunks):
-        copies[3 + at].wait()
-        local[first:last] = dot(ham[first:last], begin)
+    for copy in copies[3:]:
+        copy.wait()
+    local[...] = tall_dot(lambda first, last: ham[first:last], begin)
     sums[...] = dot(pick, local[...].astype(BF16)).astype(BF16)
 
 
@@ -112,26 +112,34 @@
     one_t[...] = jnp.zeros(one_t.shape, BF16)
     one_t[:, :shared] = (first * has_before).astype(BF16)
     one_t[:, padded : padded + shared] = (second * has_after).astype(BF16)
-    on_first = jnp.sum(first, axis=1, keepdims=True) * has_before
-    on_second = jnp.sum(second, axis=1, keepdims=True)
-    keep[...] = jnp.broadcast_to(1.0 - on_first - on_second, keep.shape)
-
-
-def second_kernel(local, before, after, ham, start, one, one_t, keep, partial, block, sums):
-    count = local.shape[0]
-    padded = before.shape[0]
-    head = block.shape[0] - padded
+    keep[...] = jnp.broadcast_to(1.0 - jnp.sum(first, axis=1, keepdims=True) * has_before, keep.shape)
+
+
+def second_kernel(local, before, after, ham, start, one_t, keep, result, block):
     halo = jnp.concatenate([before[...], after[...]], axis=0)
     newer = 0.5 * (local[...] + dot(one_t[...], halo))
-    width = local.shape[1]
-    result = tall_dot(lambda first, last: ham[first:last], newer.astype(BF16))
-    rest = result - start[...].astype(F32)
-    partial[...] = rest
-    on_faces = dot(one[...], jnp.concatenate([result.astype(BF16), rest.astype(BF16)], axis=1)).astype(BF16)
-    sums[...] = on_faces[:, :width]
-    block[count:head, :] = jnp.zeros((head - count, width), BF16)
-    block[:count, :] = (rest * keep[...]).astype(BF16)
-    block[head:, :] = on_faces[padded:, width:]
+    sums = tall_dot(lambda first, last: ham[first:last], newer.astype(BF16))
+    result[...] = sums
+    block[...] = (sums - start[...].astype(F32) * keep[...]).astype(BF16)
+
+
+def face_kernel(result, start, one, sums):
+    sums[...] = dot(one[...], jnp.concatenate([result[...].astype(BF16), start[...]], axis=1)).astype(BF16)
+
+
+def third_kernel(result, start, keep, before, after, one_t, *rest):
+    blocks, (filtered, gram) = rest[:-2], rest[-2:]
+    width = result.shape[1]
+    here = jnp.concatenate([before[:, :width], after[:, :width]], axis=0)
+    there = jnp.concatenate([before[:, width:], jnp.zeros((after.shape[0], width), BF16)], axis=0)
+    halo = dot(one_t[...], jnp.concatenate([here, there], axis=1))
+    older = start[...].astype(F32)
+    whole = result[...] + halo[:, :width]
+    filtered[...] = whole - older
+    right = (whole - older * keep[...] - halo[:, width:]).astype(BF16)
+    product = dot_t(right, jnp.concatenate([block[...] for block in blocks], axis=1))
+    for at in range(len(blocks)):
+        gram[at] = jnp.transpose(product[:, at * width : (at + 1) * width]).astype(BF16)
 
 
 def vmem(count):
@@ -142,7 +150,6 @@
     node_count, width = wavefunctions.shape
     shared = face_nodes.shape[1]
     padded = -(-shared // 32) * 32
-    head = -(-node_count // 16) * 16
     lanes = -(-node_count // 128) * 128
     parts = lax.axis_size("cells")
     groups = lax.axis_size("bands")
@@ -175,7 +182,7 @@
     )(*(pltpu.with_memory_space_constraint(x, pltpu.HBM) for x in (wavefunctions, connectivity, face_nodes, hamiltonians)))
 
     both = ("cells", "bands")
-    stride, radix = digits(groups)[-1] if groups > 1 else (1, 1)
+    chip = digits(groups)[-1] if groups > 1 else (1, 1)
 
     def pair_swap(first):
         pairs = []
@@ -185,7 +192,7 @@
                 if part >= first and other < parts:
                     pairs.append((part * groups + band, other * groups + band))
                 else:
-                    pairs.append((part * groups + band, part * groups + turn(band, stride, radix, 1)))
+                    pairs.append((part * groups + band, part * groups + turn(band, *chip, 1)))
         return pairs
 
     odd = place % 2 == 1
@@ -205,55 +212,35 @@
         out_specs=tuple(vmem(2)),
         compiler_params=params,
     )(ends, columns, face_nodes)
-    partial, block, sums = pl.pallas_call(
+    result, block = pl.pallas_call(
         second_kernel,
-        out_shape=(shape(nodal, F32), shape((head + padded, width), BF16), shape((2 * padded, width), BF16)),
-        in_specs=vmem(8),
-        out_specs=tuple(vmem(3)),
-        compiler_params=params,
-    )(local, before, after, ham, start, one, one_t, keep)
-
-    core, chips = digits(groups)[:1], digits(groups)[1:]
-    low = sums[:padded]
-    has_after = place < parts - 1
+        out_shape=(shape(nodal, F32), shape(nodal, BF16)),
+        in_specs=vmem(7),
+        out_specs=tuple(vmem(2)),
+        compiler_params=params,
+    )(local, before, after, ham, start, one_t, keep)
+
     blocks = {0: block}
-    for stride, radix in chips:
+    for stride, radix in reversed(digits(groups)):
         for at in list(blocks):
             for by in range(1, radix):
                 blocks[at + by * stride] = lax.ppermute(blocks[at], "bands", turned(groups, stride, radix, radix - by))
-    raw = {}
-    for stride, radix in core:
-        for by in range(1, radix):
-            raw[by * stride] = lax.ppermute(block, "bands", turned(groups, stride, radix, radix - by))
+    sums = pl.pallas_call(
+        face_kernel,
+        out_shape=shape((2 * padded, 2 * width), BF16),
+        in_specs=vmem(3),
+        out_specs=vmem(1)[0],
+        compiler_params=params,
+    )(result, start, one)
     before, after = neighbours(sums)
-    tails = {0: jnp.where(has_after, after, jnp.zeros_like(after))}
-    blocks[0] = blocks[0].at[head:].add(tails[0])
-    for at in list(blocks)[1:]:
-        pairs = []
-        for part in range(parts):
-            for band in range(groups):
-                target = band
-                for stride, radix in chips:
-                    target = turn(target, stride, radix, radix - at // stride % radix)
-                pairs.append((part * groups + band, (part - 1) % parts * groups + target))
-        tail = lax.ppermute(low, both, pairs)
-        tails[at] = jnp.where(has_after, tail, jnp.zeros_like(tail))
-        blocks[at] = blocks[at].at[head:].add(tails[at])
-    after = tails[0]
-    relayed = jnp.concatenate([after] + [blocks[at] for at in list(blocks)[1:]])
-    for stride, radix in core:
-        for by in range(1, radix):
-            got = lax.ppermute(relayed, "bands", turned(groups, stride, radix, radix - by))
-            raw[by * stride] = raw[by * stride].at[head:].add(got[:padded])
-            for place_at, at in enumerate(list(blocks)[1:]):
-                first = padded + place_at * block.shape[0]
-                raw[at + by * stride] = got[first : first + block.shape[0]]
-    blocks.update(raw)
-    gram = jnp.stack([dot_t(blocks[at], blocks[0]) for at in range(groups)])
-
-    gram, partial, before, after = lax.optimization_barrier((gram, partial, before, after))
+    filtered, gram = pl.pallas_call(
+        third_kernel,
+        out_shape=(shape(nodal, F32), shape((groups, width, width), BF16)),
+        in_specs=vmem(6 + groups),
+        out_specs=tuple(vmem(2)),
+        compiler_params=params,
+    )(result, start, keep, before, after, one_t, *(blocks[at] for at in range(groups)))
     total = sum_over_cells(gram) * (1.0 / (parts * node_count))
-    before = jnp.where(place > 0, before, jnp.zeros_like(before))
     radices = digits(groups)
     total = total.reshape(tuple(radix for _, radix in reversed(radices)) + (width, width))
     for at, (stride, radix) in enumerate(radices):
@@ -264,16 +251,12 @@
         total = moved
     correlation = total.reshape(groups * width, width)
 
-    nodes = lax.broadcasted_iota(jnp.int32, (node_count, node_count), 0)
-    place_of = (nodes == connectivity).astype(BF16)
-    face_of = (face_nodes.reshape(-1)[None, :] == nodes[:, :1]).astype(BF16)
-    top = partial.astype(BF16)
-    rest = partial - top.astype(F32)
+    place_of = (lax.broadcasted_iota(jnp.int32, (node_count, node_count), 0) == connectivity).astype(BF16)
+    top = filtered.astype(BF16)
+    rest = filtered - top.astype(F32)
     middle = rest.astype(BF16)
     small = (rest - middle.astype(F32)).astype(BF16)
-    halo = jnp.concatenate([before[:shared], after[:shared]])
-    filtered = dot(place_of, small) + dot(place_of, middle) + dot(face_of, halo) + dot(place_of, top)
-    return filtered, correlation
+    return dot(place_of, small) + dot(place_of, middle) + dot(place_of, top), correlation
 
 
 def solution(mesh):

time: 41 us -> 37.8 us (0.922)
  waiting for transfers between devices: 17.5 us -> 13.2 us
  starting transfers between devices: 13 us -> 15.4 us
  matrix products: 3.61 us -> 2.28 us
    ppermute x3, starting transfers between devices: 2.67 us -> 7.59 us  [sum_over_cells(): value = value + lax.ppermute(word, ('cells', 'bands'), pairs).astype(F32)]
    ppermute x3, waiting for transfers between devices: 11.6 us -> 7.88 us  [sum_over_cells(): value = value + lax.ppermute(word, ('cells', 'bands'), pairs).astype(F32)]
    ppermute x3 -> x0, starting transfers between devices: 3.71 us -> none  [the longest x1 3.57 us: body(): tail = lax.ppermute(low, both, pairs)]
    ppermute x2, waiting for transfers between devices: 2.84 us -> 0.01 us  [neighbours(): even_odd = lax.ppermute(jnp.where(odd, low, high), both, pair_swap(0))]
    ppermute x1 -> x3, waiting for transfers between devices: 0.01 us -> 2.72 us  [body(): lax.ppermute(blocks[at], 'bands', turned(groups, stride, radix, radix - by))]
    ppermute x3 -> x0, waiting for transfers between devices: 1.72 us -> none  [the longest x1 0.95 us: body(): lax.ppermute(relayed, 'bands', turned(groups, stride, radix, radix - by))]
    ppermute x2, starting transfers between devices: 3.05 us -> 4.5 us  [neighbours(): even_odd = lax.ppermute(jnp.where(odd, low, high), both, pair_swap(0))]
    ppermute x2, waiting for transfers between devices: 1.34 us -> 2.57 us  [neighbours(): odd_even = lax.ppermute(jnp.where(odd, high, low), both, pair_swap(1))]
  transfers between devices with their start and end apart: 11 -> 10, of which waited for: 8 -> 7; matrix products, arithmetic and copies ran while one was open for 8% -> 6% of each run, Pallas kernels for 2% -> 3%
where the time goes in v4:
time: 37.8 us; the launch traced here: 37.7 us
  starting transfers between devices  15.4 us (41%)
  waiting for transfers between devices  13.2 us (35%)
  Pallas kernels  4.92 us (13%)
  matrix products  2.28 us (6%)
  other arithmetic  1.05 us (3%)
  between operations  0.83 us (2%)
    ppermute x3, waiting for transfers between devices, sum_over_cells(): value = value + lax.ppermute(word, ('cells', 'bands'), pairs).astype(F32)  7.88 us
    ppermute x3, starting transfers between devices, sum_over_cells(): value = value + lax.ppermute(word, ('cells', 'bands'), pairs).astype(F32)  7.59 us
    ppermute x2, starting transfers between devices, neighbours(): even_odd = lax.ppermute(jnp.where(odd, low, high), both, pair_swap(0))  4.5 us
    ppermute x3, waiting for transfers between devices, body(): lax.ppermute(blocks[at], 'bands', turned(groups, stride, radix, radix - by))  2.72 us
    ppermute x2, waiting for transfers between devices, neighbours(): odd_even = lax.ppermute(jnp.where(odd, high, low), both, pair_swap(1))  2.57 us
    pallas_call x1, Pallas kernels, body(): pl.pallas_call(first_kernel, out_shape=(shape(nodal, BF16), shape(nodal,...  2.3 us
    dot_general x3, matrix products, dot(): return jnp.dot(a, b, preferred_element_type=F32)  2.28 us
    ppermute x3, starting transfers between devices, body(): lax.ppermute(blocks[at], 'bands', turned(groups, stride, radix, radix - by))  1.67 us
  transfers between devices with their start and end apart: 10, of which 7 were waited for; matrix products, arithmetic and copies ran while one was open for 6% of the time, Pallas kernels for 3%

profile of v4, /device:TPU:0, one launch (start us, length us, event | category | flops | bytes accessed | tf_op | source)
XLA Modules:
  0.0 37.7 jit_solution(11858848651081258461)
XLA Ops:
  0.6 0.0 copy-start
  0.7 2.3 %shard_map.59 = (bf16[729,128]{1,0:T(8,128)(2,1)S(1)}, f32[729,128]{1,0:T(8,128)S(1)}, bf16[192,128]{1,0:T(8,128)(2,1)S(1)}, bf16[729,729]{1,0:T(8,128)(2,1)S(1)...) custom-call(bf16[729,128]{1,0:T(8,128)(2,1)} %waves_hbm.1, s32[1,729]{1,0:T(1,128)} %cell_hbm.1, s32[2,81]{1,0:T(2,128)} %faces.1, ...), custom_call_target="tpu_custom_call" | custom-call | tf_op jit(solution)/shard_map/pallas_call | solution.py:162
  3.0 3.0 %collective-permute-start = (bf16[96,128]{1,0:T(8,128)(2,1)S(1)}, bf16[96,128]{1,0:T(8,128)(2,1)S(1)}, u32[]{:S(2)}, u32[]{:S(2)}) collective-permute-start(bf16[96,128]{1,0:T(8,128)(2,1)S(1)} %get-tuple-element.39), channel_id=1, source_target_pairs={{0,4},{1,5},{2,6},{3,7},{4,0},{5,1},{6,2},{7,3},{8,12},{9,13},{10,... | collective-permute-start | bytes 73736 | tf_op jit(solution)/shard_map/ppermute | solution.py:202
  6.0 1.5 %collective-permute-start.1 = (bf16[96,128]{1,0:T(8,128)(2,1)S(1)}, bf16[96,128]{1,0:T(8,128)(2,1)S(1)}, u32[]{:S(2)}, u32[]{:S(2)}) collective-permute-start(bf16[96,128]{1,0:T(8,128)(2,1)S(1)} %get-tuple-element.38), channel_id=1, source_target_pairs={{0,2},{1,3},{2,0},{3,1},{4,8},{5,9},{6,10},{7,11},{8,4},{9,5},{10,... | collective-permute-start | bytes 73736 | tf_op jit(solution)/shard_map/ppermute | solution.py:203
  7.5 0.1 pad_add_fusion.ends
  7.6 0.0 copy-done
  7.6 0.9 %shard_map.60 = (bf16[729,192]{1,0:T(8,128)(2,1)S(1)}, f32[729,128]{1,0:T(8,128)S(1)}) custom-call(s32[2]{0:T(128)S(1)} %pad_add_fusion.ends, f32[768,8]{1,0:T(8,128)S(1)} %get-tuple-element.18.columns, s32[2,81]{1,0:T(2,128)S(1)} %copy-done), custom_call_target="tpu_custom_call" | custom-call | tf_op jit(solution)/shard_map/pallas_call | solution.py:208
  8.5 0.0 collective-permute-done
  8.5 1.3 %collective-permute-done.1 = bf16[96,128]{1,0:T(8,128)(2,1)S(1)} collective-permute-done((bf16[96,128]{1,0:T(8,128)(2,1)S(1)}, bf16[96,128]{1,0:T(8,128)(2,1)S(1)}, u32[]{:S(2)}, u32[]{:S(2)}) %collective-permute-start.1) | collective-permute-done | bytes 24608 | tf_op jit(solution)/shard_map/ppermute | solution.py:203
  9.8 0.7 %shard_map.61 = (f32[729,128]{1,0:T(8,128)S(1)}, bf16[729,128]{1,0:T(8,128)(2,1)S(1)}) custom-call(f32[729,128]{1,0:T(8,128)S(1)} %get-tuple-element.14.local, bf16[96,128]{1,0:T(8,128)(2,1)S(1)} %get-tuple-element.37.before, bf16[96,128]{1,0:T(8,128)(2,1)S(1)} %get-tuple-element.36.after, bf16[729,729]{1,0:T(8,128)(2,1)S(1)} %get-tuple-element.16.ham, ...), custom_call_target="tpu_custom_call" | custom-call | tf_op jit(solution)/shard_map/pallas_call | solution.py:215
  10.6 0.0 copy-start.1
  10.6 1.6 %collective-permute-start.5 = (bf16[729,128]{1,0:T(8,128)(2,1)S(1)}, bf16[729,128]{1,0:T(8,128)(2,1)S(1)}, u32[]{:S(2)}, u32[]{:S(2)}) collective-permute-start(bf16[729,128]{1,0:T(8,128)(2,1)S(1)} %get-tuple-element.23.rest_0_), channel_id=1, source_target_pairs={{0,2},{1,3},{2,0},{3,1},{4,6},{5,7},{6,4},{7,5},{8,10},{9,11},{10,... | collective-permute-start | bytes 559880 | tf_op jit(solution)/shard_map/ppermute | solution.py:227
  12.2 0.3 shard_map.62
  12.5 1.5 %collective-permute-start.2 = (bf16[96,256]{1,0:T(8,128)(2,1)S(1)}, bf16[96,256]{1,0:T(8,128)(2,1)S(1)}, u32[]{:S(2)}, u32[]{:S(2)}) collective-permute-start(bf16[96,256]{1,0:T(8,128)(2,1)S(1)} %get-tuple-element.35), channel_id=1, source_target_pairs={{0,4},{1,5},{2,6},{3,7},{4,0},{5,1},{6,2},{7,3},{8,12},{9,13},{10,... | collective-permute-start | bytes 147464 | tf_op jit(solution)/shard_map/ppermute | solution.py:202
  13.9 0.1 collective-permute-start.3
  14.0 0.0 copy-done.1
  14.1 0.1 collective-permute-start.4
  14.2 2.6 %collective-permute-done.5.rest_2_ = bf16[729,128]{1,0:T(8,128)(2,1)S(1)} collective-permute-done((bf16[729,128]{1,0:T(8,128)(2,1)S(1)}, bf16[729,128]{1,0:T(8,128)(2,1)S(1)}, u32[]{:S(2)}, u32[]{:S(2)}) %collective-permute-start.5) | collective-permute-done | bytes 186656 | tf_op jit(solution)/shard_map/ppermute | solution.py:227
  16.7 0.0 collective-permute-start.6
  16.8 0.0 collective-permute-done.2
  16.8 1.3 %collective-permute-done.3 = bf16[96,256]{1,0:T(8,128)(2,1)S(1)} collective-permute-done((bf16[96,256]{1,0:T(8,128)(2,1)S(1)}, bf16[96,256]{1,0:T(8,128)(2,1)S(1)}, u32[]{:S(2)}, u32[]{:S(2)}) %collective-permute-start.3) | collective-permute-done | bytes 49184 | tf_op jit(solution)/shard_map/ppermute | solution.py:203
  18.1 0.0 collective-permute-done.4.rest_1_
  18.1 0.1 collective-permute-done.6.rest_3_
  18.2 0.7 %shard_map.63 = (f32[729,128]{1,0:T(8,128)S(1)}, bf16[4,128,128]{2,1,0:T(8,128)(2,1)S(1)}) custom-call(f32[729,128]{1,0:T(8,128)S(1)} %get-tuple-element.21.result, bf16[729,128]{1,0:T(8,128)(2,1)S(1)} %get-tuple-element.17.start, f32[729,128]{1,0:T(8,128)S(1)} %get-tuple-element.20.keep, bf16[96,256]{1,0:T(8,128)(2,1)S(1)} %get-tuple-element.33.before, ...), custom_call_target="tpu_custom_call" | custom-call | tf_op jit(solution)/shard_map/pallas_call | solution.py:236
  18.9 1.5 %collective-permute-start.7 = (bf16[4,128,128]{2,1,0:T(8,128)(2,1)S(1)}, bf16[4,128,128]{2,1,0:T(8,128)(2,1)S(1)}, u32[]{:S(2)}, u32[]{:S(2)}) collective-permute-start(bf16[4,128,128]{2,1,0:T(8,128)(2,1)S(1)} %get-tuple-element.25), channel_id=1, source_target_pairs={{0,4},{1,25},{2,6},{3,27},{4,0},{5,29},{6,2},{7,31},{8,12},{9,17},... | collective-permute-start | bytes 393224 | tf_op jit(solution)/shard_map/ppermute | solution.py:47
  20.4 0.5 %fusion.2 = f32[729,128]{1,0:T(8,128)S(1)} fusion(s32[729]{0:T(1024)S(1)} %reduce, f32[729,128]{1,0:T(8,128)S(1)} %get-tuple-element.24), kind=kOutput, calls=%fused_computation.3 | convolution fusion | flops 137233520 | bytes 749412 | tf_op jit(solution)/shard_map/dot_general | solution.py:52
  20.9 3.1 %collective-permute-done.7 = bf16[4,128,128]{2,1,0:T(8,128)(2,1)S(1)} collective-permute-done((bf16[4,128,128]{2,1,0:T(8,128)(2,1)S(1)}, bf16[4,128,128]{2,1,0:T(8,128)(2,1)S(1)}, u32[]{:S(2)}, u32[]{:S(2)}) %collective-permute-start.7) | collective-permute-done | bytes 131104 | tf_op jit(solution)/shard_map/ppermute | solution.py:47
  24.0 2.4 %collective-permute-start.8 = (bf16[4,128,128]{2,1,0:T(8,128)(2,1)S(1)}, bf16[4,128,128]{2,1,0:T(8,128)(2,1)S(1)}, u32[]{:S(2)}, u32[]{:S(2)}) collective-permute-start(bf16[4,128,128]{2,1,0:T(8,128)(2,1)S(1)} %add_convert_fusion.1), channel_id=1, source_target_pairs={{0,8},{1,5},{2,10},{3,7},{4,12},{5,1},{6,14},{7,3},{8,0},{9,13},{1... | collective-permute-start | bytes 393224 | tf_op jit(solution)/shard_map/ppermute | solution.py:47
  26.4 0.5 %fusion = f32[729,128]{1,0:T(8,128)S(1)} fusion(s32[729]{0:T(1024)S(1)} %reduce, f32[729,128]{1,0:T(8,128)S(1)} %get-tuple-element.24), kind=kOutput, calls=%fused_computation.1 | convolution fusion | flops 136673648 | bytes 749412 | tf_op jit(solution)/shard_map/dot_general | solution.py:52
  26.9 2.4 %collective-permute-done.8 = bf16[4,128,128]{2,1,0:T(8,128)(2,1)S(1)} collective-permute-done((bf16[4,128,128]{2,1,0:T(8,128)(2,1)S(1)}, bf16[4,128,128]{2,1,0:T(8,128)(2,1)S(1)}, u32[]{:S(2)}, u32[]{:S(2)}) %collective-permute-start.8) | collective-permute-done | bytes 131104 | tf_op jit(solution)/shard_map/ppermute | solution.py:47
  29.4 3.7 %collective-permute-start.9 = (bf16[4,128,128]{2,1,0:T(8,128)(2,1)S(1)}, bf16[4,128,128]{2,1,0:T(8,128)(2,1)S(1)}, u32[]{:S(2)}, u32[]{:S(2)}) collective-permute-start(bf16[4,128,128]{2,1,0:T(8,128)(2,1)S(1)} %add_convert_fusion), channel_id=1, source_target_pairs={{0,24},{1,9},{2,26},{3,11},{4,28},{5,13},{6,30},{7,15},{8,16},{9,1... | collective-permute-start | bytes 393224 | tf_op jit(solution)/shard_map/ppermute | solution.py:47
  33.1 1.3 %fusion.4 = f32[729,128]{1,0:T(8,128)} fusion(f32[729,128]{1,0:T(8,128)S(1)} %fusion, f32[729,128]{1,0:T(8,128)S(1)} %fusion.2, s32[729]{0:T(1024)S(1)} %reduce, f32[729,128]{1,0:T(8,128)S(1)} %get-tuple-element.24), kind=kOutput, calls=%fused_computation.5 | convolution fusion | flops 137140208 | bytes 1495908 | tf_op jit(solution)/shard_map/dot_general | solution.py:52
  34.4 2.4 %collective-permute-done.9 = bf16[4,128,128]{2,1,0:T(8,128)(2,1)S(1)} collective-permute-done((bf16[4,128,128]{2,1,0:T(8,128)(2,1)S(1)}, bf16[4,128,128]{2,1,0:T(8,128)(2,1)S(1)}, u32[]{:S(2)}, u32[]{:S(2)}) %collective-permute-start.9) | collective-permute-done | bytes 131104 | tf_op jit(solution)/shard_map/ppermute | solution.py:47
  36.9 0.7 %fusion.8 = f32[512,128]{1,0:T(8,128)} fusion(f32[4,128,128]{2,1,0:T(8,128)S(1)} %add_multiply_fusion, f32[2,2,128,128]{3,2,1,0:T(8,128)S(1)} %get-tuple-element.29, f32[2,2,128,128]{3,2,1,0:T(8,128)S(1)} %pad_maximum_fusion.1, pred[]{:T(512)S(6)} %eq.28, pred[]{:T(512)S(6)} %eq.27), kind=kLoop, calls=%fused_computation.14 | loop fusion | flops 131072 | bytes 1048578 | tf_op jit(solution)/shard_map/jit(_where)/select_n | solution.py:250
  (12 shorter events, 0.3 us)
Async XLA Ops:
  0.6 7.0 %copy-start = (s32[2,81]{1,0:T(2,128)S(1)}, s32[2,81]{1,0:T(2,128)}, u32[]{:S(2)}) copy-start(s32[2,81]{1,0:T(2,128)} %faces.1) | copy-start | bytes 1948
  3.0 5.5 %collective-permute-start = (bf16[96,128]{1,0:T(8,128)(2,1)S(1)}, bf16[96,128]{1,0:T(8,128)(2,1)S(1)}, u32[]{:S(2)}, u32[]{:S(2)}) collective-permute-start(bf16[96,128]{1,0:T(8,128)(2,1)S(1)} %get-tuple-element.39), channel_id=1, source_target_pairs={{0,4},{1,5},{2,6},{3,7},{4,0},{5,1},{6,2},{7,3},{8,12},{9,13},{10,... | collective-permute-start | bytes 73736 | tf_op jit(solution)/shard_map/ppermute | solution.py:202
  6.0 3.8 %collective-permute-start.1 = (bf16[96,128]{1,0:T(8,128)(2,1)S(1)}, bf16[96,128]{1,0:T(8,128)(2,1)S(1)}, u32[]{:S(2)}, u32[]{:S(2)}) collective-permute-start(bf16[96,128]{1,0:T(8,128)(2,1)S(1)} %get-tuple-element.38), channel_id=1, source_target_pairs={{0,2},{1,3},{2,0},{3,1},{4,8},{5,9},{6,10},{7,11},{8,4},{9,5},{10,... | collective-permute-start | bytes 73736 | tf_op jit(solution)/shard_map/ppermute | solution.py:203
  10.6 3.5 %copy-start.1 = (s32[1,729]{1,0:T(1,128)S(1)}, s32[1,729]{1,0:T(1,128)}, u32[]{:S(2)}) copy-start(s32[1,729]{1,0:T(1,128)} %cell_hbm.1) | copy-start | bytes 8752
  10.6 6.2 %collective-permute-start.5 = (bf16[729,128]{1,0:T(8,128)(2,1)S(1)}, bf16[729,128]{1,0:T(8,128)(2,1)S(1)}, u32[]{:S(2)}, u32[]{:S(2)}) collective-permute-start(bf16[729,128]{1,0:T(8,128)(2,1)S(1)} %get-tuple-element.23.rest_0_), channel_id=1, source_target_pairs={{0,2},{1,3},{2,0},{3,1},{4,6},{5,7},{6,4},{7,5},{8,10},{9,11},{10,... | collective-permute-start | bytes 559880 | tf_op jit(solution)/shard_map/ppermute | solution.py:227
  12.5 4.3 %collective-permute-start.2 = (bf16[96,256]{1,0:T(8,128)(2,1)S(1)}, bf16[96,256]{1,0:T(8,128)(2,1)S(1)}, u32[]{:S(2)}, u32[]{:S(2)}) collective-permute-start(bf16[96,256]{1,0:T(8,128)(2,1)S(1)} %get-tuple-element.35), channel_id=1, source_target_pairs={{0,4},{1,5},{2,6},{3,7},{4,0},{5,1},{6,2},{7,3},{8,12},{9,13},{10,... | collective-permute-start | bytes 147464 | tf_op jit(solution)/shard_map/ppermute | solution.py:202
  13.9 4.1 %collective-permute-start.3 = (bf16[96,256]{1,0:T(8,128)(2,1)S(1)}, bf16[96,256]{1,0:T(8,128)(2,1)S(1)}, u32[]{:S(2)}, u32[]{:S(2)}) collective-permute-start(bf16[96,256]{1,0:T(8,128)(2,1)S(1)} %get-tuple-element.34), channel_id=1, source_target_pairs={{0,2},{1,3},{2,0},{3,1},{4,8},{5,9},{6,10},{7,11},{8,4},{9,5},{10,... | collective-permute-start | bytes 147464 | tf_op jit(solution)/shard_map/ppermute | solution.py:203
  14.1 4.0 %collective-permute-start.4 = (bf16[729,128]{1,0:T(8,128)(2,1)S(1)}, bf16[729,128]{1,0:T(8,128)(2,1)S(1)}, u32[]{:S(2)}, u32[]{:S(2)}) collective-permute-start(bf16[729,128]{1,0:T(8,128)(2,1)S(1)} %get-tuple-element.23.rest_0_), channel_id=1, source_target_pairs={{0,1},{1,0},{2,3},{3,2},{4,5},{5,4},{6,7},{7,6},{8,9},{9,8},{10,11... | collective-permute-start | bytes 559880 | tf_op jit(solution)/shard_map/ppermute | solution.py:227
  16.7 1.4 %collective-permute-start.6 = (bf16[729,128]{1,0:T(8,128)(2,1)S(1)}, bf16[729,128]{1,0:T(8,128)(2,1)S(1)}, u32[]{:S(2)}, u32[]{:S(2)}) collective-permute-start(bf16[729,128]{1,0:T(8,128)(2,1)S(1)} %collective-permute-done.5.rest_2_), channel_id=1, source_target_pairs={{0,1},{1,0},{2,3},{3,2},{4,5},{5,4},{6,7},{7,6},{8,9},{9,8},{10,11... | collective-permute-start | bytes 559880 | tf_op jit(solution)/shard_map/ppermute | solution.py:227
  18.9 5.0 %collective-permute-start.7 = (bf16[4,128,128]{2,1,0:T(8,128)(2,1)S(1)}, bf16[4,128,128]{2,1,0:T(8,128)(2,1)S(1)}, u32[]{:S(2)}, u32[]{:S(2)}) collective-permute-start(bf16[4,128,128]{2,1,0:T(8,128)(2,1)S(1)} %get-tuple-element.25), channel_id=1, source_target_pairs={{0,4},{1,25},{2,6},{3,27},{4,0},{5,29},{6,2},{7,31},{8,12},{9,17},... | collective-permute-start | bytes 393224 | tf_op jit(solution)/shard_map/ppermute | solution.py:47
  24.0 5.4 %collective-permute-start.8 = (bf16[4,128,128]{2,1,0:T(8,128)(2,1)S(1)}, bf16[4,128,128]{2,1,0:T(8,128)(2,1)S(1)}, u32[]{:S(2)}, u32[]{:S(2)}) collective-permute-start(bf16[4,128,128]{2,1,0:T(8,128)(2,1)S(1)} %add_convert_fusion.1), channel_id=1, source_target_pairs={{0,8},{1,5},{2,10},{3,7},{4,12},{5,1},{6,14},{7,3},{8,0},{9,13},{1... | collective-permute-start | bytes 393224 | tf_op jit(solution)/shard_map/ppermute | solution.py:47
  29.4 7.3 %collective-permute-start.9 = (bf16[4,128,128]{2,1,0:T(8,128)(2,1)S(1)}, bf16[4,128,128]{2,1,0:T(8,128)(2,1)S(1)}, u32[]{:S(2)}, u32[]{:S(2)}) collective-permute-start(bf16[4,128,128]{2,1,0:T(8,128)(2,1)S(1)} %add_convert_fusion), channel_id=1, source_target_pairs={{0,24},{1,9},{2,26},{3,11},{4,28},{5,13},{6,30},{7,15},{8,16},{9,1... | collective-permute-start | bytes 393224 | tf_op jit(solution)/shard_map/ppermute | solution.py:47

commit v5 on v4

--- a/solution.py
+++ b/solution.py
@@ -33,18 +33,28 @@
     binary = [stride for stride, radix in digits(parts) if radix == 2]
     other = [(stride, radix) for stride, radix in digits(parts) if radix != 2]
     masks = [stride + (stride // 2 if stride > 2 else 0) for stride in binary]
-    steps = [[(mask, masks[at - 1])] for at, mask in enumerate(masks)]
+    steps = []
+    if len(masks) >= 2:
+        first, second = masks[:2]
+        steps.append([(first, second), (second, first), (first ^ second, first ^ second)])
+        masks = masks[2:]
+    steps += [[(mask, mask)] for mask in masks]
     steps = [[lambda part, band, m=m: part ^ m[band % 2] for m in step] for step in steps]
     for stride, radix in other:
         steps.append([lambda part, band, d=(stride, radix, by): turn(part, *d) for by in range(1, radix)])
     for step in steps:
         word = value.astype(BF16)
-        value = word.astype(F32)
+        words = [word.astype(F32)]
         for move in step:
             pairs = [
                 (part * groups + band, move(part, band) * groups + band) for part in range(parts) for band in range(groups)
             ]
-            value = value + lax.ppermute(word, ("cells", "bands"), pairs).astype(F32)
+            words.append(lax.ppermute(word, ("cells", "bands"), pairs).astype(F32))
+        value = words[0] + words[1]
+        if len(words) == 4:
+            value = value + (words[2] + words[3])
+        elif len(words) == 3:
+            value = value + words[2]
     return value
 
 
@@ -196,12 +206,13 @@
         return pairs
 
     odd = place % 2 == 1
+    even = place % 2 == 0
 
     def neighbours(sums):
         low, high = sums[:padded], sums[padded:]
         even_odd = lax.ppermute(jnp.where(odd, low, high), both, pair_swap(0))
         odd_even = lax.ppermute(jnp.where(odd, high, low), both, pair_swap(1))
-        return jnp.where(odd, even_odd, odd_even), jnp.where(odd, odd_even, even_odd)
+        return jnp.where(even, odd_even, even_odd), jnp.where(even, even_odd, odd_even)
 
     before, after = neighbours(sums)
     ends = jnp.stack([place, parts - 1 - place]).astype(jnp.int32)

time: 37.8 us -> 35.9 us (0.950)
  waiting for transfers between devices: 13.2 us -> 10.1 us
  starting transfers between devices: 15.4 us -> 16.5 us
    ppermute x2, starting transfers between devices: 1.61 us -> 4.1 us  [neighbours(): odd_even = lax.ppermute(jnp.where(odd, high, low), both, pair_swap(1))]
    ppermute x2, waiting for transfers between devices: 2.57 us -> 0.53 us  [neighbours(): odd_even = lax.ppermute(jnp.where(odd, high, low), both, pair_swap(1))]
    ppermute x2, waiting for transfers between devices: 0.01 us -> 2.02 us  [neighbours(): even_odd = lax.ppermute(jnp.where(odd, low, high), both, pair_swap(0))]
    ppermute x3, waiting for transfers between devices: 2.72 us -> 0.84 us  [body(): lax.ppermute(blocks[at], 'bands', turned(groups, stride, radix, radix - by))]
    ppermute x3 -> x4, waiting for transfers between devices: 7.88 us -> 6.72 us  [sum_over_cells(): words.append(lax.ppermute(word, ('cells', 'bands'), pairs).astype(F32))]
    ppermute x2, starting transfers between devices: 4.5 us -> 3.92 us  [neighbours(): even_odd = lax.ppermute(jnp.where(odd, low, high), both, pair_swap(0))]
    ppermute x3, starting transfers between devices: 1.67 us -> 1.16 us  [body(): lax.ppermute(blocks[at], 'bands', turned(groups, stride, radix, radix - by))]
    ppermute x3 -> x4, starting transfers between devices: 7.59 us -> 7.32 us  [sum_over_cells(): words.append(lax.ppermute(word, ('cells', 'bands'), pairs).astype(F32))]
  transfers between devices with their start and end apart: 10 -> 11, of which waited for: 7 -> 9; matrix products, arithmetic and copies ran while one was open for 6% -> 7% of each run, Pallas kernels for 3% -> 3%
where the time goes in v5:
time: 35.9 us; the launch traced here: 35.7 us
  starting transfers between devices  16.5 us (46%)
  waiting for transfers between devices  10.1 us (28%)
  Pallas kernels  4.93 us (14%)
  matrix products  2.28 us (6%)
  other arithmetic  1.05 us (3%)
  between operations  0.82 us (2%)
    ppermute x4, starting transfers between devices, sum_over_cells(): words.append(lax.ppermute(word, ('cells', 'bands'), pairs).astype(F32))  7.32 us
    ppermute x4, waiting for transfers between devices, sum_over_cells(): words.append(lax.ppermute(word, ('cells', 'bands'), pairs).astype(F32))  6.72 us
    ppermute x2, starting transfers between devices, neighbours(): odd_even = lax.ppermute(jnp.where(odd, high, low), both, pair_swap(1))  4.1 us
    ppermute x2, starting transfers between devices, neighbours(): even_odd = lax.ppermute(jnp.where(odd, low, high), both, pair_swap(0))  3.92 us
    pallas_call x1, Pallas kernels, body(): pl.pallas_call(first_kernel, out_shape=(shape(nodal, BF16), shape(nodal,...  2.3 us
    dot_general x3, matrix products, dot(): return jnp.dot(a, b, preferred_element_type=F32)  2.28 us
    ppermute x2, waiting for transfers between devices, neighbours(): even_odd = lax.ppermute(jnp.where(odd, low, high), both, pair_swap(0))  2.02 us
    ppermute x3, starting transfers between devices, body(): lax.ppermute(blocks[at], 'bands', turned(groups, stride, radix, radix - by))  1.16 us
  transfers between devices with their start and end apart: 11, of which 9 were waited for; matrix products, arithmetic and copies ran while one was open for 7% of the time, Pallas kernels for 3%

profile of v5, /device:TPU:0, one launch (start us, length us, event | category | flops | bytes accessed | tf_op | source)
XLA Modules:
  0.0 35.7 jit_solution(13235341534573011269)
XLA Ops:
  0.6 0.0 copy-start
  0.7 2.3 %shard_map.59 = (bf16[729,128]{1,0:T(8,128)(2,1)S(1)}, f32[729,128]{1,0:T(8,128)S(1)}, bf16[192,128]{1,0:T(8,128)(2,1)S(1)}, bf16[729,729]{1,0:T(8,128)(2,1)S(1)...) custom-call(bf16[729,128]{1,0:T(8,128)(2,1)} %waves_hbm.1, s32[1,729]{1,0:T(1,128)} %cell_hbm.1, s32[2,81]{1,0:T(2,128)} %faces.1, ...), custom_call_target="tpu_custom_call" | custom-call | tf_op jit(solution)/shard_map/pallas_call | solution.py:172
  3.0 3.0 %collective-permute-start = (bf16[96,128]{1,0:T(8,128)(2,1)S(1)}, bf16[96,128]{1,0:T(8,128)(2,1)S(1)}, u32[]{:S(2)}, u32[]{:S(2)}) collective-permute-start(bf16[96,128]{1,0:T(8,128)(2,1)S(1)} %get-tuple-element.39), channel_id=1, source_target_pairs={{0,2},{1,3},{2,0},{3,1},{4,8},{5,9},{6,10},{7,11},{8,4},{9,5},{10,... | collective-permute-start | bytes 73736 | tf_op jit(solution)/shard_map/ppermute | solution.py:214
  6.0 1.5 %collective-permute-start.1 = (bf16[96,128]{1,0:T(8,128)(2,1)S(1)}, bf16[96,128]{1,0:T(8,128)(2,1)S(1)}, u32[]{:S(2)}, u32[]{:S(2)}) collective-permute-start(bf16[96,128]{1,0:T(8,128)(2,1)S(1)} %get-tuple-element.38), channel_id=1, source_target_pairs={{0,4},{1,5},{2,6},{3,7},{4,0},{5,1},{6,2},{7,3},{8,12},{9,13},{10,... | collective-permute-start | bytes 73736 | tf_op jit(solution)/shard_map/ppermute | solution.py:213
  7.5 0.1 pad_add_fusion.ends
  7.6 0.0 copy-done
  7.6 0.9 %shard_map.60 = (bf16[729,192]{1,0:T(8,128)(2,1)S(1)}, f32[729,128]{1,0:T(8,128)S(1)}) custom-call(s32[2]{0:T(128)S(1)} %pad_add_fusion.ends, f32[768,8]{1,0:T(8,128)S(1)} %get-tuple-element.18.columns, s32[2,81]{1,0:T(2,128)S(1)} %copy-done), custom_call_target="tpu_custom_call" | custom-call | tf_op jit(solution)/shard_map/pallas_call | solution.py:219
  8.5 0.0 collective-permute-done
  8.5 1.3 %collective-permute-done.1 = bf16[96,128]{1,0:T(8,128)(2,1)S(1)} collective-permute-done((bf16[96,128]{1,0:T(8,128)(2,1)S(1)}, bf16[96,128]{1,0:T(8,128)(2,1)S(1)}, u32[]{:S(2)}, u32[]{:S(2)}) %collective-permute-start.1) | collective-permute-done | bytes 24608 | tf_op jit(solution)/shard_map/ppermute | solution.py:213
  9.8 0.7 %shard_map.61 = (f32[729,128]{1,0:T(8,128)S(1)}, bf16[729,128]{1,0:T(8,128)(2,1)S(1)}) custom-call(f32[729,128]{1,0:T(8,128)S(1)} %get-tuple-element.14.local, bf16[96,128]{1,0:T(8,128)(2,1)S(1)} %get-tuple-element.37.before, bf16[96,128]{1,0:T(8,128)(2,1)S(1)} %get-tuple-element.36.after, bf16[729,729]{1,0:T(8,128)(2,1)S(1)} %get-tuple-element.16.ham, ...), custom_call_target="tpu_custom_call" | custom-call | tf_op jit(solution)/shard_map/pallas_call | solution.py:226
  10.6 0.0 copy-start.1
  10.6 1.1 %collective-permute-start.5 = (bf16[729,128]{1,0:T(8,128)(2,1)S(1)}, bf16[729,128]{1,0:T(8,128)(2,1)S(1)}, u32[]{:S(2)}, u32[]{:S(2)}) collective-permute-start(bf16[729,128]{1,0:T(8,128)(2,1)S(1)} %get-tuple-element.23.rest_0_), channel_id=1, source_target_pairs={{0,2},{1,3},{2,0},{3,1},{4,6},{5,7},{6,4},{7,5},{8,10},{9,11},{10,... | collective-permute-start | bytes 559880 | tf_op jit(solution)/shard_map/ppermute | solution.py:238
  11.7 0.3 shard_map.62
  12.0 1.1 %collective-permute-start.2 = (bf16[96,256]{1,0:T(8,128)(2,1)S(1)}, bf16[96,256]{1,0:T(8,128)(2,1)S(1)}, u32[]{:S(2)}, u32[]{:S(2)}) collective-permute-start(bf16[96,256]{1,0:T(8,128)(2,1)S(1)} %get-tuple-element.35), channel_id=1, source_target_pairs={{0,2},{1,3},{2,0},{3,1},{4,8},{5,9},{6,10},{7,11},{8,4},{9,5},{10,... | collective-permute-start | bytes 147464 | tf_op jit(solution)/shard_map/ppermute | solution.py:214
  13.0 2.4 %collective-permute-start.3 = (bf16[96,256]{1,0:T(8,128)(2,1)S(1)}, bf16[96,256]{1,0:T(8,128)(2,1)S(1)}, u32[]{:S(2)}, u32[]{:S(2)}) collective-permute-start(bf16[96,256]{1,0:T(8,128)(2,1)S(1)} %get-tuple-element.34), channel_id=1, source_target_pairs={{0,4},{1,5},{2,6},{3,7},{4,0},{5,1},{6,2},{7,3},{8,12},{9,13},{10,... | collective-permute-start | bytes 147464 | tf_op jit(solution)/shard_map/ppermute | solution.py:213
  15.4 0.0 copy-done.1
  15.5 0.1 collective-permute-start.4
  15.6 0.7 %collective-permute-done.5.rest_2_ = bf16[729,128]{1,0:T(8,128)(2,1)S(1)} collective-permute-done((bf16[729,128]{1,0:T(8,128)(2,1)S(1)}, bf16[729,128]{1,0:T(8,128)(2,1)S(1)}, u32[]{:S(2)}, u32[]{:S(2)}) %collective-permute-start.5) | collective-permute-done | bytes 186656 | tf_op jit(solution)/shard_map/ppermute | solution.py:238
  16.3 0.0 collective-permute-start.6
  16.3 0.5 %collective-permute-done.2 = bf16[96,256]{1,0:T(8,128)(2,1)S(1)} collective-permute-done((bf16[96,256]{1,0:T(8,128)(2,1)S(1)}, bf16[96,256]{1,0:T(8,128)(2,1)S(1)}, u32[]{:S(2)}, u32[]{:S(2)}) %collective-permute-start.2) | collective-permute-done | bytes 49184 | tf_op jit(solution)/shard_map/ppermute | solution.py:214
  16.8 0.7 %collective-permute-done.3 = bf16[96,256]{1,0:T(8,128)(2,1)S(1)} collective-permute-done((bf16[96,256]{1,0:T(8,128)(2,1)S(1)}, bf16[96,256]{1,0:T(8,128)(2,1)S(1)}, u32[]{:S(2)}, u32[]{:S(2)}) %collective-permute-start.3) | collective-permute-done | bytes 49184 | tf_op jit(solution)/shard_map/ppermute | solution.py:213
  17.5 0.0 collective-permute-done.4.rest_1_
  17.5 0.1 collective-permute-done.6.rest_3_
  17.7 0.7 %shard_map.63 = (f32[729,128]{1,0:T(8,128)S(1)}, bf16[4,128,128]{2,1,0:T(8,128)(2,1)S(1)}) custom-call(f32[729,128]{1,0:T(8,128)S(1)} %get-tuple-element.21.result, bf16[729,128]{1,0:T(8,128)(2,1)S(1)} %get-tuple-element.17.start, f32[729,128]{1,0:T(8,128)S(1)} %get-tuple-element.20.keep, bf16[96,256]{1,0:T(8,128)(2,1)S(1)} %get-tuple-element.33.before, ...), custom_call_target="tpu_custom_call" | custom-call | tf_op jit(solution)/shard_map/pallas_call | solution.py:247
  18.4 2.0 %collective-permute-start.7 = (bf16[4,128,128]{2,1,0:T(8,128)(2,1)S(1)}, bf16[4,128,128]{2,1,0:T(8,128)(2,1)S(1)}, u32[]{:S(2)}, u32[]{:S(2)}) collective-permute-start(bf16[4,128,128]{2,1,0:T(8,128)(2,1)S(1)} %get-tuple-element.25), channel_id=1, source_target_pairs={{0,4},{1,9},{2,6},{3,11},{4,0},{5,13},{6,2},{7,15},{8,12},{9,1},{1... | collective-permute-start | bytes 393224 | tf_op jit(solution)/shard_map/ppermute | solution.py:52
  20.4 1.6 %collective-permute-start.8 = (bf16[4,128,128]{2,1,0:T(8,128)(2,1)S(1)}, bf16[4,128,128]{2,1,0:T(8,128)(2,1)S(1)}, u32[]{:S(2)}, u32[]{:S(2)}) collective-permute-start(bf16[4,128,128]{2,1,0:T(8,128)(2,1)S(1)} %get-tuple-element.25), channel_id=1, source_target_pairs={{0,8},{1,5},{2,10},{3,7},{4,12},{5,1},{6,14},{7,3},{8,0},{9,13},{1... | collective-permute-start | bytes 393224 | tf_op jit(solution)/shard_map/ppermute | solution.py:52
  22.0 0.0 collective-permute-start.9
  22.0 0.5 %fusion.2 = f32[729,128]{1,0:T(8,128)S(1)} fusion(s32[729]{0:T(1024)S(1)} %reduce, f32[729,128]{1,0:T(8,128)S(1)} %get-tuple-element.24), kind=kOutput, calls=%fused_computation.3 | convolution fusion | flops 137233520 | bytes 749412 | tf_op jit(solution)/shard_map/dot_general | solution.py:62
  22.5 0.5 %fusion = f32[729,128]{1,0:T(8,128)S(1)} fusion(s32[729]{0:T(1024)S(1)} %reduce, f32[729,128]{1,0:T(8,128)S(1)} %get-tuple-element.24), kind=kOutput, calls=%fused_computation.1 | convolution fusion | flops 136673648 | bytes 749412 | tf_op jit(solution)/shard_map/dot_general | solution.py:62
  23.0 2.5 %collective-permute-done.7 = bf16[4,128,128]{2,1,0:T(8,128)(2,1)S(1)} collective-permute-done((bf16[4,128,128]{2,1,0:T(8,128)(2,1)S(1)}, bf16[4,128,128]{2,1,0:T(8,128)(2,1)S(1)}, u32[]{:S(2)}, u32[]{:S(2)}) %collective-permute-start.7) | collective-permute-done | bytes 131104 | tf_op jit(solution)/shard_map/ppermute | solution.py:52
  25.5 0.9 %collective-permute-done.8 = bf16[4,128,128]{2,1,0:T(8,128)(2,1)S(1)} collective-permute-done((bf16[4,128,128]{2,1,0:T(8,128)(2,1)S(1)}, bf16[4,128,128]{2,1,0:T(8,128)(2,1)S(1)}, u32[]{:S(2)}, u32[]{:S(2)}) %collective-permute-start.8) | collective-permute-done | bytes 131104 | tf_op jit(solution)/shard_map/ppermute | solution.py:52
  26.3 1.5 %collective-permute-done.9 = bf16[4,128,128]{2,1,0:T(8,128)(2,1)S(1)} collective-permute-done((bf16[4,128,128]{2,1,0:T(8,128)(2,1)S(1)}, bf16[4,128,128]{2,1,0:T(8,128)(2,1)S(1)}, u32[]{:S(2)}, u32[]{:S(2)}) %collective-permute-start.9) | collective-permute-done | bytes 131104 | tf_op jit(solution)/shard_map/ppermute | solution.py:52
  27.8 0.1 add_convert_fusion
  27.9 3.7 %collective-permute-start.10 = (bf16[4,128,128]{2,1,0:T(8,128)(2,1)S(1)}, bf16[4,128,128]{2,1,0:T(8,128)(2,1)S(1)}, u32[]{:S(2)}, u32[]{:S(2)}) collective-permute-start(bf16[4,128,128]{2,1,0:T(8,128)(2,1)S(1)} %add_convert_fusion), channel_id=1, source_target_pairs={{0,24},{1,25},{2,26},{3,27},{4,28},{5,29},{6,30},{7,31},{8,16},{9,... | collective-permute-start | bytes 393224 | tf_op jit(solution)/shard_map/ppermute | solution.py:52
  31.7 1.3 %fusion.4 = f32[729,128]{1,0:T(8,128)} fusion(f32[729,128]{1,0:T(8,128)S(1)} %fusion, f32[729,128]{1,0:T(8,128)S(1)} %fusion.2, s32[729]{0:T(1024)S(1)} %reduce, f32[729,128]{1,0:T(8,128)S(1)} %get-tuple-element.24), kind=kOutput, calls=%fused_computation.5 | convolution fusion | flops 137140208 | bytes 1495908 | tf_op jit(solution)/shard_map/dot_general | solution.py:62
  32.9 1.9 %collective-permute-done.10 = bf16[4,128,128]{2,1,0:T(8,128)(2,1)S(1)} collective-permute-done((bf16[4,128,128]{2,1,0:T(8,128)(2,1)S(1)}, bf16[4,128,128]{2,1,0:T(8,128)(2,1)S(1)}, u32[]{:S(2)}, u32[]{:S(2)}) %collective-permute-start.10) | collective-permute-done | bytes 131104 | tf_op jit(solution)/shard_map/ppermute | solution.py:52
  35.0 0.7 %fusion.8 = f32[512,128]{1,0:T(8,128)} fusion(f32[4,128,128]{2,1,0:T(8,128)S(1)} %add_multiply_fusion, f32[2,2,128,128]{3,2,1,0:T(8,128)S(1)} %get-tuple-element.29, f32[2,2,128,128]{3,2,1,0:T(8,128)S(1)} %pad_maximum_fusion.1, pred[]{:T(512)S(6)} %eq.33, pred[]{:T(512)S(6)} %eq.32), kind=kLoop, calls=%fused_computation.14 | loop fusion | flops 131072 | bytes 1048578 | tf_op jit(solution)/shard_map/jit(_where)/select_n | solution.py:261
  (10 shorter events, 0.2 us)
Async XLA Ops:
  0.6 7.0 %copy-start = (s32[2,81]{1,0:T(2,128)S(1)}, s32[2,81]{1,0:T(2,128)}, u32[]{:S(2)}) copy-start(s32[2,81]{1,0:T(2,128)} %faces.1) | copy-start | bytes 1948
  3.0 5.6 %collective-permute-start = (bf16[96,128]{1,0:T(8,128)(2,1)S(1)}, bf16[96,128]{1,0:T(8,128)(2,1)S(1)}, u32[]{:S(2)}, u32[]{:S(2)}) collective-permute-start(bf16[96,128]{1,0:T(8,128)(2,1)S(1)} %get-tuple-element.39), channel_id=1, source_target_pairs={{0,2},{1,3},{2,0},{3,1},{4,8},{5,9},{6,10},{7,11},{8,4},{9,5},{10,... | collective-permute-start | bytes 73736 | tf_op jit(solution)/shard_map/ppermute | solution.py:214
  6.0 3.8 %collective-permute-start.1 = (bf16[96,128]{1,0:T(8,128)(2,1)S(1)}, bf16[96,128]{1,0:T(8,128)(2,1)S(1)}, u32[]{:S(2)}, u32[]{:S(2)}) collective-permute-start(bf16[96,128]{1,0:T(8,128)(2,1)S(1)} %get-tuple-element.38), channel_id=1, source_target_pairs={{0,4},{1,5},{2,6},{3,7},{4,0},{5,1},{6,2},{7,3},{8,12},{9,13},{10,... | collective-permute-start | bytes 73736 | tf_op jit(solution)/shard_map/ppermute | solution.py:213
  10.6 4.9 %copy-start.1 = (s32[1,729]{1,0:T(1,128)S(1)}, s32[1,729]{1,0:T(1,128)}, u32[]{:S(2)}) copy-start(s32[1,729]{1,0:T(1,128)} %cell_hbm.1) | copy-start | bytes 8752
  10.6 5.6 %collective-permute-start.5 = (bf16[729,128]{1,0:T(8,128)(2,1)S(1)}, bf16[729,128]{1,0:T(8,128)(2,1)S(1)}, u32[]{:S(2)}, u32[]{:S(2)}) collective-permute-start(bf16[729,128]{1,0:T(8,128)(2,1)S(1)} %get-tuple-element.23.rest_0_), channel_id=1, source_target_pairs={{0,2},{1,3},{2,0},{3,1},{4,6},{5,7},{6,4},{7,5},{8,10},{9,11},{10,... | collective-permute-start | bytes 559880 | tf_op jit(solution)/shard_map/ppermute | solution.py:238
  12.0 4.8 %collective-permute-start.2 = (bf16[96,256]{1,0:T(8,128)(2,1)S(1)}, bf16[96,256]{1,0:T(8,128)(2,1)S(1)}, u32[]{:S(2)}, u32[]{:S(2)}) collective-permute-start(bf16[96,256]{1,0:T(8,128)(2,1)S(1)} %get-tuple-element.35), channel_id=1, source_target_pairs={{0,2},{1,3},{2,0},{3,1},{4,8},{5,9},{6,10},{7,11},{8,4},{9,5},{10,... | collective-permute-start | bytes 147464 | tf_op jit(solution)/shard_map/ppermute | solution.py:214
  13.0 4.5 %collective-permute-start.3 = (bf16[96,256]{1,0:T(8,128)(2,1)S(1)}, bf16[96,256]{1,0:T(8,128)(2,1)S(1)}, u32[]{:S(2)}, u32[]{:S(2)}) collective-permute-start(bf16[96,256]{1,0:T(8,128)(2,1)S(1)} %get-tuple-element.34), channel_id=1, source_target_pairs={{0,4},{1,5},{2,6},{3,7},{4,0},{5,1},{6,2},{7,3},{8,12},{9,13},{10,... | collective-permute-start | bytes 147464 | tf_op jit(solution)/shard_map/ppermute | solution.py:213
  15.5 2.0 %collective-permute-start.4 = (bf16[729,128]{1,0:T(8,128)(2,1)S(1)}, bf16[729,128]{1,0:T(8,128)(2,1)S(1)}, u32[]{:S(2)}, u32[]{:S(2)}) collective-permute-start(bf16[729,128]{1,0:T(8,128)(2,1)S(1)} %get-tuple-element.23.rest_0_), channel_id=1, source_target_pairs={{0,1},{1,0},{2,3},{3,2},{4,5},{5,4},{6,7},{7,6},{8,9},{9,8},{10,11... | collective-permute-start | bytes 559880 | tf_op jit(solution)/shard_map/ppermute | solution.py:238
  16.3 1.4 %collective-permute-start.6 = (bf16[729,128]{1,0:T(8,128)(2,1)S(1)}, bf16[729,128]{1,0:T(8,128)(2,1)S(1)}, u32[]{:S(2)}, u32[]{:S(2)}) collective-permute-start(bf16[729,128]{1,0:T(8,128)(2,1)S(1)} %collective-permute-done.5.rest_2_), channel_id=1, source_target_pairs={{0,1},{1,0},{2,3},{3,2},{4,5},{5,4},{6,7},{7,6},{8,9},{9,8},{10,11... | collective-permute-start | bytes 559880 | tf_op jit(solution)/shard_map/ppermute | solution.py:238
  18.4 7.1 %collective-permute-start.7 = (bf16[4,128,128]{2,1,0:T(8,128)(2,1)S(1)}, bf16[4,128,128]{2,1,0:T(8,128)(2,1)S(1)}, u32[]{:S(2)}, u32[]{:S(2)}) collective-permute-start(bf16[4,128,128]{2,1,0:T(8,128)(2,1)S(1)} %get-tuple-element.25), channel_id=1, source_target_pairs={{0,4},{1,9},{2,6},{3,11},{4,0},{5,13},{6,2},{7,15},{8,12},{9,1},{1... | collective-permute-start | bytes 393224 | tf_op jit(solution)/shard_map/ppermute | solution.py:52
  20.4 6.0 %collective-permute-start.8 = (bf16[4,128,128]{2,1,0:T(8,128)(2,1)S(1)}, bf16[4,128,128]{2,1,0:T(8,128)(2,1)S(1)}, u32[]{:S(2)}, u32[]{:S(2)}) collective-permute-start(bf16[4,128,128]{2,1,0:T(8,128)(2,1)S(1)} %get-tuple-element.25), channel_id=1, source_target_pairs={{0,8},{1,5},{2,10},{3,7},{4,12},{5,1},{6,14},{7,3},{8,0},{9,13},{1... | collective-permute-start | bytes 393224 | tf_op jit(solution)/shard_map/ppermute | solution.py:52
  22.0 5.9 %collective-permute-start.9 = (bf16[4,128,128]{2,1,0:T(8,128)(2,1)S(1)}, bf16[4,128,128]{2,1,0:T(8,128)(2,1)S(1)}, u32[]{:S(2)}, u32[]{:S(2)}) collective-permute-start(bf16[4,128,128]{2,1,0:T(8,128)(2,1)S(1)} %get-tuple-element.25), channel_id=1, source_target_pairs={{0,12},{1,13},{2,14},{3,15},{4,8},{5,9},{6,10},{7,11},{8,4},{9,5},... | collective-permute-start | bytes 393224 | tf_op jit(solution)/shard_map/ppermute | solution.py:52
  27.9 6.9 %collective-permute-start.10 = (bf16[4,128,128]{2,1,0:T(8,128)(2,1)S(1)}, bf16[4,128,128]{2,1,0:T(8,128)(2,1)S(1)}, u32[]{:S(2)}, u32[]{:S(2)}) collective-permute-start(bf16[4,128,128]{2,1,0:T(8,128)(2,1)S(1)} %add_convert_fusion), channel_id=1, source_target_pairs={{0,24},{1,25},{2,26},{3,27},{4,28},{5,29},{6,30},{7,31},{8,16},{9,... | collective-permute-start | bytes 393224 | tf_op jit(solution)/shard_map/ppermute | solution.py:52

commit v6 on v5

--- a/solution.py
+++ b/solution.py
@@ -109,7 +109,7 @@
     sums[...] = dot(pick, local[...].astype(BF16)).astype(BF16)
 
 
-def middle_kernel(ends, columns, faces, one_t, keep):
+def middle_kernel(ends, columns, faces, local, ham, one_t, keep, mine, border):
     count = one_t.shape[0]
     shared = faces.shape[1]
     padded = one_t.shape[1] // 2
@@ -123,12 +123,16 @@
     one_t[:, :shared] = (first * has_before).astype(BF16)
     one_t[:, padded : padded + shared] = (second * has_after).astype(BF16)
     keep[...] = jnp.broadcast_to(1.0 - jnp.sum(first, axis=1, keepdims=True) * has_before, keep.shape)
-
-
-def second_kernel(local, before, after, ham, start, one_t, keep, result, block):
-    halo = jnp.concatenate([before[...], after[...]], axis=0)
-    newer = 0.5 * (local[...] + dot(one_t[...], halo))
-    sums = tall_dot(lambda first, last: ham[first:last], newer.astype(BF16))
+    half = (0.5 * local[...]).astype(BF16)
+    both = tall_dot(lambda first, last: ham[first:last], jnp.concatenate([half, one_t[...]], axis=1))
+    width = local.shape[1]
+    mine[...] = both[:, :width]
+    border[...] = both[:, width:].astype(BF16)
+
+
+def second_kernel(before, after, mine, border, start, keep, result, block):
+    halo = 0.5 * jnp.concatenate([before[...], after[...]], axis=0).astype(F32)
+    sums = mine[...] + dot(border[...], halo.astype(BF16))
     result[...] = sums
     block[...] = (sums - start[...].astype(F32) * keep[...]).astype(BF16)
 
@@ -216,20 +220,25 @@
 
     before, after = neighbours(sums)
     ends = jnp.stack([place, parts - 1 - place]).astype(jnp.int32)
-    one_t, keep = pl.pallas_call(
+    one_t, keep, mine, border = pl.pallas_call(
         middle_kernel,
-        out_shape=(shape((node_count, 2 * padded), BF16), shape(nodal, F32)),
-        in_specs=[pl.BlockSpec(memory_space=pltpu.SMEM)] + vmem(2),
-        out_specs=tuple(vmem(2)),
-        compiler_params=params,
-    )(ends, columns, face_nodes)
+        out_shape=(
+            shape((node_count, 2 * padded), BF16),
+            shape(nodal, F32),
+            shape(nodal, F32),
+            shape((node_count, 2 * padded), BF16),
+        ),
+        in_specs=[pl.BlockSpec(memory_space=pltpu.SMEM)] + vmem(4),
+        out_specs=tuple(vmem(4)),
+        compiler_params=params,
+    )(ends, columns, face_nodes, local, ham)
     result, block = pl.pallas_call(
         second_kernel,
         out_shape=(shape(nodal, F32), shape(nodal, BF16)),
-        in_specs=vmem(7),
+        in_specs=vmem(6),
         out_specs=tuple(vmem(2)),
         compiler_params=params,
-    )(local, before, after, ham, start, one_t, keep)
+    )(before, after, mine, border, start, keep)
 
     blocks = {0: block}
     for stride, radix in reversed(digits(groups)):

time: 35.9 us -> 35.5 us (0.989)
  waiting for transfers between devices: 10.1 us -> 9.68 us
    ppermute x2, waiting for transfers between devices: 2.02 us -> 1.11 us  [neighbours(): even_odd = lax.ppermute(jnp.where(odd, low, high), both, pair_swap(0))]
    pallas_call x1, Pallas kernels: 0.92 us -> 1.59 us  [body(): pl.pallas_call(middle_kernel, out_shape=(shape((node_count, 2 * padded),...]
    ppermute x3, waiting for transfers between devices: 0.84 us -> 1.32 us  [body(): lax.ppermute(blocks[at], 'bands', turned(groups, stride, radix, radix - by))]
    pallas_call x1, Pallas kernels: 0.74 us -> 0.26 us  [body(): pl.pallas_call(second_kernel, out_shape=(shape(nodal, F32), shape(nodal,...]
  transfers between devices with their start and end apart: 11 -> 11, of which waited for: 9 -> 9; matrix products, arithmetic and copies ran while one was open for 7% -> 7% of each run, Pallas kernels for 3% -> 5%
where the time goes in v6:
time: 35.5 us; the launch traced here: 35.4 us
  starting transfers between devices  16.4 us (46%)
  waiting for transfers between devices  9.68 us (27%)
  Pallas kernels  5.11 us (14%)
  matrix products  2.28 us (6%)
  other arithmetic  1.05 us (3%)
  between operations  0.82 us (2%)
    ppermute x4, starting transfers between devices, sum_over_cells(): words.append(lax.ppermute(word, ('cells', 'bands'), pairs).astype(F32))  7.18 us
    ppermute x4, waiting for transfers between devices, sum_over_cells(): words.append(lax.ppermute(word, ('cells', 'bands'), pairs).astype(F32))  6.72 us
    ppermute x2, starting transfers between devices, neighbours(): odd_even = lax.ppermute(jnp.where(odd, high, low), both, pair_swap(1))  4.12 us
    ppermute x2, starting transfers between devices, neighbours(): even_odd = lax.ppermute(jnp.where(odd, low, high), both, pair_swap(0))  3.92 us
    pallas_call x1, Pallas kernels, body(): pl.pallas_call(first_kernel, out_shape=(shape(nodal, BF16), shape(nodal,...  2.3 us
    dot_general x3, matrix products, dot(): return jnp.dot(a, b, preferred_element_type=F32)  2.28 us
    pallas_call x1, Pallas kernels, body(): pl.pallas_call(middle_kernel, out_shape=(shape((node_count, 2 * padded),...  1.59 us
    ppermute x3, waiting for transfers between devices, body(): lax.ppermute(blocks[at], 'bands', turned(groups, stride, radix, radix - by))  1.32 us
  transfers between devices with their start and end apart: 11, of which 9 were waited for; matrix products, arithmetic and copies ran while one was open for 7% of the time, Pallas kernels for 5%

profile of v6, /device:TPU:0, one launch (start us, length us, event | category | flops | bytes accessed | tf_op | source)
XLA Modules:
  0.0 35.4 jit_solution(10410731570133218953)
XLA Ops:
  0.6 0.0 copy-start
  0.7 2.3 %shard_map.59 = (bf16[729,128]{1,0:T(8,128)(2,1)S(1)}, f32[729,128]{1,0:T(8,128)S(1)}, bf16[192,128]{1,0:T(8,128)(2,1)S(1)}, bf16[729,729]{1,0:T(8,128)(2,1)S(1)...) custom-call(bf16[729,128]{1,0:T(8,128)(2,1)} %waves_hbm.1, s32[1,729]{1,0:T(1,128)} %cell_hbm.1, s32[2,81]{1,0:T(2,128)} %faces.1, ...), custom_call_target="tpu_custom_call" | custom-call | tf_op jit(solution)/shard_map/pallas_call | solution.py:176
  3.0 3.0 %collective-permute-start = (bf16[96,128]{1,0:T(8,128)(2,1)S(1)}, bf16[96,128]{1,0:T(8,128)(2,1)S(1)}, u32[]{:S(2)}, u32[]{:S(2)}) collective-permute-start(bf16[96,128]{1,0:T(8,128)(2,1)S(1)} %get-tuple-element.43), channel_id=1, source_target_pairs={{0,2},{1,3},{2,0},{3,1},{4,8},{5,9},{6,10},{7,11},{8,4},{9,5},{10,... | collective-permute-start | bytes 73736 | tf_op jit(solution)/shard_map/ppermute | solution.py:218
  6.0 1.5 %collective-permute-start.1 = (bf16[96,128]{1,0:T(8,128)(2,1)S(1)}, bf16[96,128]{1,0:T(8,128)(2,1)S(1)}, u32[]{:S(2)}, u32[]{:S(2)}) collective-permute-start(bf16[96,128]{1,0:T(8,128)(2,1)S(1)} %get-tuple-element.42), channel_id=1, source_target_pairs={{0,4},{1,5},{2,6},{3,7},{4,0},{5,1},{6,2},{7,3},{8,12},{9,13},{10,... | collective-permute-start | bytes 73736 | tf_op jit(solution)/shard_map/ppermute | solution.py:217
  7.5 0.1 pad_add_fusion.ends
  7.6 0.0 copy-done
  7.6 1.6 %shard_map.60 = (bf16[729,192]{1,0:T(8,128)(2,1)S(1)}, f32[729,128]{1,0:T(8,128)S(1)}, f32[729,128]{1,0:T(8,128)S(1)}, bf16[729,192]{1,0:T(8,128)(2,1)S(1)}) custom-call(s32[2]{0:T(128)S(1)} %pad_add_fusion.ends, f32[768,8]{1,0:T(8,128)S(1)} %get-tuple-element.17.columns, s32[2,81]{1,0:T(2,128)S(1)} %copy-done, f32[729,128]{1,0:T(8,128)S(1)} %get-tuple-element.18.local, ...), custom_call_target="tpu_custom_call" | custom-call | tf_op jit(solution)/shard_map/pallas_call | solution.py:223
  9.2 0.0 collective-permute-done
  9.2 0.6 %collective-permute-done.1 = bf16[96,128]{1,0:T(8,128)(2,1)S(1)} collective-permute-done((bf16[96,128]{1,0:T(8,128)(2,1)S(1)}, bf16[96,128]{1,0:T(8,128)(2,1)S(1)}, u32[]{:S(2)}, u32[]{:S(2)}) %collective-permute-start.1) | collective-permute-done | bytes 24608 | tf_op jit(solution)/shard_map/ppermute | solution.py:217
  9.8 0.0 copy-start.1
  9.9 0.3 shard_map.61
  10.1 1.1 %collective-permute-start.5 = (bf16[729,128]{1,0:T(8,128)(2,1)S(1)}, bf16[729,128]{1,0:T(8,128)(2,1)S(1)}, u32[]{:S(2)}, u32[]{:S(2)}) collective-permute-start(bf16[729,128]{1,0:T(8,128)(2,1)S(1)} %get-tuple-element.27.rest_0_), channel_id=1, source_target_pairs={{0,2},{1,3},{2,0},{3,1},{4,6},{5,7},{6,4},{7,5},{8,10},{9,11},{10,... | collective-permute-start | bytes 559880 | tf_op jit(solution)/shard_map/ppermute | solution.py:247
  11.2 0.3 shard_map.62
  11.5 1.1 %collective-permute-start.2 = (bf16[96,256]{1,0:T(8,128)(2,1)S(1)}, bf16[96,256]{1,0:T(8,128)(2,1)S(1)}, u32[]{:S(2)}, u32[]{:S(2)}) collective-permute-start(bf16[96,256]{1,0:T(8,128)(2,1)S(1)} %get-tuple-element.39), channel_id=1, source_target_pairs={{0,2},{1,3},{2,0},{3,1},{4,8},{5,9},{6,10},{7,11},{8,4},{9,5},{10,... | collective-permute-start | bytes 147464 | tf_op jit(solution)/shard_map/ppermute | solution.py:218
  12.6 2.4 %collective-permute-start.3 = (bf16[96,256]{1,0:T(8,128)(2,1)S(1)}, bf16[96,256]{1,0:T(8,128)(2,1)S(1)}, u32[]{:S(2)}, u32[]{:S(2)}) collective-permute-start(bf16[96,256]{1,0:T(8,128)(2,1)S(1)} %get-tuple-element.38), channel_id=1, source_target_pairs={{0,4},{1,5},{2,6},{3,7},{4,0},{5,1},{6,2},{7,3},{8,12},{9,13},{10,... | collective-permute-start | bytes 147464 | tf_op jit(solution)/shard_map/ppermute | solution.py:217
  15.0 0.0 copy-done.1
  15.0 0.1 collective-permute-start.4
  15.1 0.9 %collective-permute-done.5.rest_2_ = bf16[729,128]{1,0:T(8,128)(2,1)S(1)} collective-permute-done((bf16[729,128]{1,0:T(8,128)(2,1)S(1)}, bf16[729,128]{1,0:T(8,128)(2,1)S(1)}, u32[]{:S(2)}, u32[]{:S(2)}) %collective-permute-start.5) | collective-permute-done | bytes 186656 | tf_op jit(solution)/shard_map/ppermute | solution.py:247
  16.0 0.0 collective-permute-start.6
  16.0 0.5 %collective-permute-done.2 = bf16[96,256]{1,0:T(8,128)(2,1)S(1)} collective-permute-done((bf16[96,256]{1,0:T(8,128)(2,1)S(1)}, bf16[96,256]{1,0:T(8,128)(2,1)S(1)}, u32[]{:S(2)}, u32[]{:S(2)}) %collective-permute-start.2) | collective-permute-done | bytes 49184 | tf_op jit(solution)/shard_map/ppermute | solution.py:218
  16.5 0.5 %collective-permute-done.3 = bf16[96,256]{1,0:T(8,128)(2,1)S(1)} collective-permute-done((bf16[96,256]{1,0:T(8,128)(2,1)S(1)}, bf16[96,256]{1,0:T(8,128)(2,1)S(1)}, u32[]{:S(2)}, u32[]{:S(2)}) %collective-permute-start.3) | collective-permute-done | bytes 49184 | tf_op jit(solution)/shard_map/ppermute | solution.py:217
  17.1 0.0 collective-permute-done.4.rest_1_
  17.1 0.4 %collective-permute-done.6.rest_3_ = bf16[729,128]{1,0:T(8,128)(2,1)S(1)} collective-permute-done((bf16[729,128]{1,0:T(8,128)(2,1)S(1)}, bf16[729,128]{1,0:T(8,128)(2,1)S(1)}, u32[]{:S(2)}, u32[]{:S(2)}) %collective-permute-start.6) | collective-permute-done | bytes 186656 | tf_op jit(solution)/shard_map/ppermute | solution.py:247
  17.5 0.7 %shard_map.63 = (f32[729,128]{1,0:T(8,128)S(1)}, bf16[4,128,128]{2,1,0:T(8,128)(2,1)S(1)}) custom-call(f32[729,128]{1,0:T(8,128)S(1)} %get-tuple-element.24.result, bf16[729,128]{1,0:T(8,128)(2,1)S(1)} %get-tuple-element.22.start, f32[729,128]{1,0:T(8,128)S(1)} %get-tuple-element.23.keep, bf16[96,256]{1,0:T(8,128)(2,1)S(1)} %get-tuple-element.37.before, ...), custom_call_target="tpu_custom_call" | custom-call | tf_op jit(solution)/shard_map/pallas_call | solution.py:256
  18.2 1.7 %collective-permute-start.7 = (bf16[4,128,128]{2,1,0:T(8,128)(2,1)S(1)}, bf16[4,128,128]{2,1,0:T(8,128)(2,1)S(1)}, u32[]{:S(2)}, u32[]{:S(2)}) collective-permute-start(bf16[4,128,128]{2,1,0:T(8,128)(2,1)S(1)} %get-tuple-element.29), channel_id=1, source_target_pairs={{0,4},{1,9},{2,6},{3,11},{4,0},{5,13},{6,2},{7,15},{8,12},{9,1},{1... | collective-permute-start | bytes 393224 | tf_op jit(solution)/shard_map/ppermute | solution.py:52
  19.9 1.6 %collective-permute-start.8 = (bf16[4,128,128]{2,1,0:T(8,128)(2,1)S(1)}, bf16[4,128,128]{2,1,0:T(8,128)(2,1)S(1)}, u32[]{:S(2)}, u32[]{:S(2)}) collective-permute-start(bf16[4,128,128]{2,1,0:T(8,128)(2,1)S(1)} %get-tuple-element.29), channel_id=1, source_target_pairs={{0,8},{1,5},{2,10},{3,7},{4,12},{5,1},{6,14},{7,3},{8,0},{9,13},{1... | collective-permute-start | bytes 393224 | tf_op jit(solution)/shard_map/ppermute | solution.py:52
  21.5 0.2 collective-permute-start.9
  21.7 0.5 %fusion.2 = f32[729,128]{1,0:T(8,128)S(1)} fusion(s32[729]{0:T(1024)S(1)} %reduce, f32[729,128]{1,0:T(8,128)S(1)} %get-tuple-element.28), kind=kOutput, calls=%fused_computation.3 | convolution fusion | flops 137233520 | bytes 749412 | tf_op jit(solution)/shard_map/dot_general | solution.py:62
  22.2 0.5 %fusion = f32[729,128]{1,0:T(8,128)S(1)} fusion(s32[729]{0:T(1024)S(1)} %reduce, f32[729,128]{1,0:T(8,128)S(1)} %get-tuple-element.28), kind=kOutput, calls=%fused_computation.1 | convolution fusion | flops 136673648 | bytes 749412 | tf_op jit(solution)/shard_map/dot_general | solution.py:62
  22.7 2.3 %collective-permute-done.7 = bf16[4,128,128]{2,1,0:T(8,128)(2,1)S(1)} collective-permute-done((bf16[4,128,128]{2,1,0:T(8,128)(2,1)S(1)}, bf16[4,128,128]{2,1,0:T(8,128)(2,1)S(1)}, u32[]{:S(2)}, u32[]{:S(2)}) %collective-permute-start.7) | collective-permute-done | bytes 131104 | tf_op jit(solution)/shard_map/ppermute | solution.py:52
  25.0 0.9 %collective-permute-done.8 = bf16[4,128,128]{2,1,0:T(8,128)(2,1)S(1)} collective-permute-done((bf16[4,128,128]{2,1,0:T(8,128)(2,1)S(1)}, bf16[4,128,128]{2,1,0:T(8,128)(2,1)S(1)}, u32[]{:S(2)}, u32[]{:S(2)}) %collective-permute-start.8) | collective-permute-done | bytes 131104 | tf_op jit(solution)/shard_map/ppermute | solution.py:52
  25.9 1.6 %collective-permute-done.9 = bf16[4,128,128]{2,1,0:T(8,128)(2,1)S(1)} collective-permute-done((bf16[4,128,128]{2,1,0:T(8,128)(2,1)S(1)}, bf16[4,128,128]{2,1,0:T(8,128)(2,1)S(1)}, u32[]{:S(2)}, u32[]{:S(2)}) %collective-permute-start.9) | collective-permute-done | bytes 131104 | tf_op jit(solution)/shard_map/ppermute | solution.py:52
  27.5 0.1 add_convert_fusion
  27.5 3.6 %collective-permute-start.10 = (bf16[4,128,128]{2,1,0:T(8,128)(2,1)S(1)}, bf16[4,128,128]{2,1,0:T(8,128)(2,1)S(1)}, u32[]{:S(2)}, u32[]{:S(2)}) collective-permute-start(bf16[4,128,128]{2,1,0:T(8,128)(2,1)S(1)} %add_convert_fusion), channel_id=1, source_target_pairs={{0,24},{1,25},{2,26},{3,27},{4,28},{5,29},{6,30},{7,31},{8,16},{9,... | collective-permute-start | bytes 393224 | tf_op jit(solution)/shard_map/ppermute | solution.py:52
  31.2 1.3 %fusion.4 = f32[729,128]{1,0:T(8,128)} fusion(f32[729,128]{1,0:T(8,128)S(1)} %fusion, f32[729,128]{1,0:T(8,128)S(1)} %fusion.2, s32[729]{0:T(1024)S(1)} %reduce, f32[729,128]{1,0:T(8,128)S(1)} %get-tuple-element.28), kind=kOutput, calls=%fused_computation.5 | convolution fusion | flops 137140208 | bytes 1495908 | tf_op jit(solution)/shard_map/dot_general | solution.py:62
  32.5 2.0 %collective-permute-done.10 = bf16[4,128,128]{2,1,0:T(8,128)(2,1)S(1)} collective-permute-done((bf16[4,128,128]{2,1,0:T(8,128)(2,1)S(1)}, bf16[4,128,128]{2,1,0:T(8,128)(2,1)S(1)}, u32[]{:S(2)}, u32[]{:S(2)}) %collective-permute-start.10) | collective-permute-done | bytes 131104 | tf_op jit(solution)/shard_map/ppermute | solution.py:52
  34.6 0.7 %fusion.8 = f32[512,128]{1,0:T(8,128)} fusion(f32[4,128,128]{2,1,0:T(8,128)S(1)} %add_multiply_fusion, f32[2,2,128,128]{3,2,1,0:T(8,128)S(1)} %get-tuple-element.33, f32[2,2,128,128]{3,2,1,0:T(8,128)S(1)} %pad_maximum_fusion.1, pred[]{:T(512)S(6)} %eq.33, pred[]{:T(512)S(6)} %eq.32), kind=kLoop, calls=%fused_computation.14 | loop fusion | flops 131072 | bytes 1048578 | tf_op jit(solution)/shard_map/jit(_where)/select_n | solution.py:270
  (10 shorter events, 0.2 us)
Async XLA Ops:
  0.6 7.0 %copy-start = (s32[2,81]{1,0:T(2,128)S(1)}, s32[2,81]{1,0:T(2,128)}, u32[]{:S(2)}) copy-start(s32[2,81]{1,0:T(2,128)} %faces.1) | copy-start | bytes 1948
  3.0 6.2 %collective-permute-start = (bf16[96,128]{1,0:T(8,128)(2,1)S(1)}, bf16[96,128]{1,0:T(8,128)(2,1)S(1)}, u32[]{:S(2)}, u32[]{:S(2)}) collective-permute-start(bf16[96,128]{1,0:T(8,128)(2,1)S(1)} %get-tuple-element.43), channel_id=1, source_target_pairs={{0,2},{1,3},{2,0},{3,1},{4,8},{5,9},{6,10},{7,11},{8,4},{9,5},{10,... | collective-permute-start | bytes 73736 | tf_op jit(solution)/shard_map/ppermute | solution.py:218
  6.0 3.8 %collective-permute-start.1 = (bf16[96,128]{1,0:T(8,128)(2,1)S(1)}, bf16[96,128]{1,0:T(8,128)(2,1)S(1)}, u32[]{:S(2)}, u32[]{:S(2)}) collective-permute-start(bf16[96,128]{1,0:T(8,128)(2,1)S(1)} %get-tuple-element.42), channel_id=1, source_target_pairs={{0,4},{1,5},{2,6},{3,7},{4,0},{5,1},{6,2},{7,3},{8,12},{9,13},{10,... | collective-permute-start | bytes 73736 | tf_op jit(solution)/shard_map/ppermute | solution.py:217
  9.8 5.1 %copy-start.1 = (s32[1,729]{1,0:T(1,128)S(1)}, s32[1,729]{1,0:T(1,128)}, u32[]{:S(2)}) copy-start(s32[1,729]{1,0:T(1,128)} %cell_hbm.1) | copy-start | bytes 8752
  10.1 5.9 %collective-permute-start.5 = (bf16[729,128]{1,0:T(8,128)(2,1)S(1)}, bf16[729,128]{1,0:T(8,128)(2,1)S(1)}, u32[]{:S(2)}, u32[]{:S(2)}) collective-permute-start(bf16[729,128]{1,0:T(8,128)(2,1)S(1)} %get-tuple-element.27.rest_0_), channel_id=1, source_target_pairs={{0,2},{1,3},{2,0},{3,1},{4,6},{5,7},{6,4},{7,5},{8,10},{9,11},{10,... | collective-permute-start | bytes 559880 | tf_op jit(solution)/shard_map/ppermute | solution.py:247
  11.5 5.1 %collective-permute-start.2 = (bf16[96,256]{1,0:T(8,128)(2,1)S(1)}, bf16[96,256]{1,0:T(8,128)(2,1)S(1)}, u32[]{:S(2)}, u32[]{:S(2)}) collective-permute-start(bf16[96,256]{1,0:T(8,128)(2,1)S(1)} %get-tuple-element.39), channel_id=1, source_target_pairs={{0,2},{1,3},{2,0},{3,1},{4,8},{5,9},{6,10},{7,11},{8,4},{9,5},{10,... | collective-permute-start | bytes 147464 | tf_op jit(solution)/shard_map/ppermute | solution.py:218
  12.6 4.5 %collective-permute-start.3 = (bf16[96,256]{1,0:T(8,128)(2,1)S(1)}, bf16[96,256]{1,0:T(8,128)(2,1)S(1)}, u32[]{:S(2)}, u32[]{:S(2)}) collective-permute-start(bf16[96,256]{1,0:T(8,128)(2,1)S(1)} %get-tuple-element.38), channel_id=1, source_target_pairs={{0,4},{1,5},{2,6},{3,7},{4,0},{5,1},{6,2},{7,3},{8,12},{9,13},{10,... | collective-permute-start | bytes 147464 | tf_op jit(solution)/shard_map/ppermute | solution.py:217
  15.0 2.0 %collective-permute-start.4 = (bf16[729,128]{1,0:T(8,128)(2,1)S(1)}, bf16[729,128]{1,0:T(8,128)(2,1)S(1)}, u32[]{:S(2)}, u32[]{:S(2)}) collective-permute-start(bf16[729,128]{1,0:T(8,128)(2,1)S(1)} %get-tuple-element.27.rest_0_), channel_id=1, source_target_pairs={{0,1},{1,0},{2,3},{3,2},{4,5},{5,4},{6,7},{7,6},{8,9},{9,8},{10,11... | collective-permute-start | bytes 559880 | tf_op jit(solution)/shard_map/ppermute | solution.py:247
  16.0 1.4 %collective-permute-start.6 = (bf16[729,128]{1,0:T(8,128)(2,1)S(1)}, bf16[729,128]{1,0:T(8,128)(2,1)S(1)}, u32[]{:S(2)}, u32[]{:S(2)}) collective-permute-start(bf16[729,128]{1,0:T(8,128)(2,1)S(1)} %collective-permute-done.5.rest_2_), channel_id=1, source_target_pairs={{0,1},{1,0},{2,3},{3,2},{4,5},{5,4},{6,7},{7,6},{8,9},{9,8},{10,11... | collective-permute-start | bytes 559880 | tf_op jit(solution)/shard_map/ppermute | solution.py:247
  18.2 6.8 %collective-permute-start.7 = (bf16[4,128,128]{2,1,0:T(8,128)(2,1)S(1)}, bf16[4,128,128]{2,1,0:T(8,128)(2,1)S(1)}, u32[]{:S(2)}, u32[]{:S(2)}) collective-permute-start(bf16[4,128,128]{2,1,0:T(8,128)(2,1)S(1)} %get-tuple-element.29), channel_id=1, source_target_pairs={{0,4},{1,9},{2,6},{3,11},{4,0},{5,13},{6,2},{7,15},{8,12},{9,1},{1... | collective-permute-start | bytes 393224 | tf_op jit(solution)/shard_map/ppermute | solution.py:52
  19.9 6.0 %collective-permute-start.8 = (bf16[4,128,128]{2,1,0:T(8,128)(2,1)S(1)}, bf16[4,128,128]{2,1,0:T(8,128)(2,1)S(1)}, u32[]{:S(2)}, u32[]{:S(2)}) collective-permute-start(bf16[4,128,128]{2,1,0:T(8,128)(2,1)S(1)} %get-tuple-element.29), channel_id=1, source_target_pairs={{0,8},{1,5},{2,10},{3,7},{4,12},{5,1},{6,14},{7,3},{8,0},{9,13},{1... | collective-permute-start | bytes 393224 | tf_op jit(solution)/shard_map/ppermute | solution.py:52
  21.5 6.0 %collective-permute-start.9 = (bf16[4,128,128]{2,1,0:T(8,128)(2,1)S(1)}, bf16[4,128,128]{2,1,0:T(8,128)(2,1)S(1)}, u32[]{:S(2)}, u32[]{:S(2)}) collective-permute-start(bf16[4,128,128]{2,1,0:T(8,128)(2,1)S(1)} %get-tuple-element.29), channel_id=1, source_target_pairs={{0,12},{1,13},{2,14},{3,15},{4,8},{5,9},{6,10},{7,11},{8,4},{9,5},... | collective-permute-start | bytes 393224 | tf_op jit(solution)/shard_map/ppermute | solution.py:52
  27.5 6.9 %collective-permute-start.10 = (bf16[4,128,128]{2,1,0:T(8,128)(2,1)S(1)}, bf16[4,128,128]{2,1,0:T(8,128)(2,1)S(1)}, u32[]{:S(2)}, u32[]{:S(2)}) collective-permute-start(bf16[4,128,128]{2,1,0:T(8,128)(2,1)S(1)} %add_convert_fusion), channel_id=1, source_target_pairs={{0,24},{1,25},{2,26},{3,27},{4,28},{5,29},{6,30},{7,31},{8,16},{9,... | collective-permute-start | bytes 393224 | tf_op jit(solution)/shard_map/ppermute | solution.py:52

commit v7 on v6

--- a/solution.py
+++ b/solution.py
@@ -109,14 +109,15 @@
     sums[...] = dot(pick, local[...].astype(BF16)).astype(BF16)
 
 
-def middle_kernel(ends, columns, faces, local, ham, one_t, keep, mine, border):
+def middle_kernel(columns, faces, local, ham, one_t, keep, mine, border):
     count = one_t.shape[0]
     shared = faces.shape[1]
     padded = one_t.shape[1] // 2
     col = columns[:count, 0:1]
     row = faces[...].astype(F32)
-    has_before = jnp.where(ends[0] > 0, jnp.float32(1), jnp.float32(0))
-    has_after = jnp.where(ends[1] > 0, jnp.float32(1), jnp.float32(0))
+    part, parts = lax.axis_index("cells"), lax.axis_size("cells")
+    has_before = jnp.where(part > 0, jnp.float32(1), jnp.float32(0))
+    has_after = jnp.where(part < parts - 1, jnp.float32(1), jnp.float32(0))
     first = jnp.where(col == row[0:1], jnp.float32(1), jnp.float32(0))
     second = jnp.where(col == row[1:2], jnp.float32(1), jnp.float32(0))
     one_t[...] = jnp.zeros(one_t.shape, BF16)
@@ -152,8 +153,12 @@
     filtered[...] = whole - older
     right = (whole - older * keep[...] - halo[:, width:]).astype(BF16)
     product = dot_t(right, jnp.concatenate([block[...] for block in blocks], axis=1))
+    group = lax.axis_index("bands")
     for at in range(len(blocks)):
-        gram[at] = jnp.transpose(product[:, at * width : (at + 1) * width]).astype(BF16)
+        target = 0
+        for stride, radix in digits(len(blocks)):
+            target = target + (group // stride + at // stride) % radix * stride
+        gram[target] = jnp.transpose(product[:, at * width : (at + 1) * width]).astype(BF16)
 
 
 def vmem(count):
@@ -168,7 +173,6 @@
     parts = lax.axis_size("cells")
     groups = lax.axis_size("bands")
     place = lax.axis_index("cells")
-    group = lax.axis_index("bands")
     nodal = (node_count, width)
     shape = jax.ShapeDtypeStruct
     params = pltpu.CompilerParams(vmem_limit_bytes=24 * 2**20)
@@ -219,7 +223,6 @@
         return jnp.where(even, odd_even, even_odd), jnp.where(even, even_odd, odd_even)
 
     before, after = neighbours(sums)
-    ends = jnp.stack([place, parts - 1 - place]).astype(jnp.int32)
     one_t, keep, mine, border = pl.pallas_call(
         middle_kernel,
         out_shape=(
@@ -228,10 +231,10 @@
             shape(nodal, F32),
             shape((node_count, 2 * padded), BF16),
         ),
-        in_specs=[pl.BlockSpec(memory_space=pltpu.SMEM)] + vmem(4),
+        in_specs=vmem(4),
         out_specs=tuple(vmem(4)),
         compiler_params=params,
-    )(ends, columns, face_nodes, local, ham)
+    )(columns, face_nodes, local, ham)
     result, block = pl.pallas_call(
         second_kernel,
         out_shape=(shape(nodal, F32), shape(nodal, BF16)),
@@ -261,14 +264,6 @@
         compiler_params=params,
     )(result, start, keep, before, after, one_t, *(blocks[at] for at in range(groups)))
     total = sum_over_cells(gram) * (1.0 / (parts * node_count))
-    radices = digits(groups)
-    total = total.reshape(tuple(radix for _, radix in reversed(radices)) + (width, width))
-    for at, (stride, radix) in enumerate(radices):
-        digit = group // stride % radix
-        moved = total
-        for by in range(1, radix):
-            moved = jnp.where(digit == by, jnp.roll(total, by, axis=len(radices) - 1 - at), moved)
-        total = moved
     correlation = total.reshape(groups * width, width)
 
     place_of = (lax.broadcasted_iota(jnp.int32, (node_count, node_count), 0) == connectivity).astype(BF16)

time: 35.5 us -> 35.2 us (level)
  Pallas kernels: 5.11 us -> 4.59 us
  waiting for transfers between devices: 9.68 us -> 10.1 us
    ppermute x2, waiting for transfers between devices: 1.11 us -> 1.96 us  [neighbours(): even_odd = lax.ppermute(jnp.where(odd, low, high), both, pair_swap(0))]
    select_n x2 -> x0, other arithmetic: 0.78 us -> none  [body(): jnp.where(digit == by, jnp.roll(total, by, axis=len(radices) - 1 - at), m...]
    mul x1, other arithmetic: 0.04 us -> 0.74 us  [body(): total = sum_over_cells(gram) * (1.0 / (parts * node_count))]
    pallas_call x1, Pallas kernels: 1.59 us -> 1.07 us  [body(): pl.pallas_call(middle_kernel, out_shape=(shape((node_count, 2 * padded),...]
    ppermute x3, waiting for transfers between devices: 1.32 us -> 0.85 us  [body(): lax.ppermute(blocks[at], 'bands', turned(groups, stride, radix, radix - by))]
  transfers between devices with their start and end apart: 11 -> 11, of which waited for: 9 -> 9; matrix products, arithmetic and copies ran while one was open for 7% -> 7% of each run, Pallas kernels for 5% -> 4%
where the time goes in v7:
time: 35.2 us; the launch traced here: 35.1 us
  starting transfers between devices  16.5 us (47%)
  waiting for transfers between devices  10.1 us (29%)
  Pallas kernels  4.59 us (13%)
  matrix products  2.28 us (6%)
  other arithmetic  0.87 us (2%)
  between operations  0.77 us (2%)
    ppermute x4, starting transfers between devices, sum_over_cells(): words.append(lax.ppermute(word, ('cells', 'bands'), pairs).astype(F32))  7.31 us
    ppermute x4, waiting for transfers between devices, sum_over_cells(): words.append(lax.ppermute(word, ('cells', 'bands'), pairs).astype(F32))  6.72 us
    ppermute x2, starting transfers between devices, neighbours(): odd_even = lax.ppermute(jnp.where(odd, high, low), both, pair_swap(1))  4.12 us
    ppermute x2, starting transfers between devices, neighbours(): even_odd = lax.ppermute(jnp.where(odd, low, high), both, pair_swap(0))  3.92 us
    pallas_call x1, Pallas kernels, body(): pl.pallas_call(first_kernel, out_shape=(shape(nodal, BF16), shape(nodal,...  2.3 us
    dot_general x3, matrix products, dot(): return jnp.dot(a, b, preferred_element_type=F32)  2.28 us
    ppermute x2, waiting for transfers between devices, neighbours(): even_odd = lax.ppermute(jnp.where(odd, low, high), both, pair_swap(0))  1.96 us
    ppermute x3, starting transfers between devices, body(): lax.ppermute(blocks[at], 'bands', turned(groups, stride, radix, radix - by))  1.15 us
  transfers between devices with their start and end apart: 11, of which 9 were waited for; matrix products, arithmetic and copies ran while one was open for 7% of the time, Pallas kernels for 4%

profile of v7, /device:TPU:0, one launch (start us, length us, event | category | flops | bytes accessed | tf_op | source)
XLA Modules:
  0.0 35.1 jit_solution(6663718788320795874)
XLA Ops:
  0.6 0.0 copy-start
  0.7 2.3 %shard_map.59 = (bf16[729,128]{1,0:T(8,128)(2,1)S(1)}, f32[729,128]{1,0:T(8,128)S(1)}, bf16[192,128]{1,0:T(8,128)(2,1)S(1)}, bf16[729,729]{1,0:T(8,128)(2,1)S(1)...) custom-call(bf16[729,128]{1,0:T(8,128)(2,1)} %waves_hbm.1, s32[1,729]{1,0:T(1,128)} %cell_hbm.1, s32[2,81]{1,0:T(2,128)} %faces.1, ...), custom_call_target="tpu_custom_call" | custom-call | tf_op jit(solution)/shard_map/pallas_call | solution.py:180
  3.0 3.0 %collective-permute-start = (bf16[96,128]{1,0:T(8,128)(2,1)S(1)}, bf16[96,128]{1,0:T(8,128)(2,1)S(1)}, u32[]{:S(2)}, u32[]{:S(2)}) collective-permute-start(bf16[96,128]{1,0:T(8,128)(2,1)S(1)} %get-tuple-element.37), channel_id=1, source_target_pairs={{0,2},{1,3},{2,0},{3,1},{4,8},{5,9},{6,10},{7,11},{8,4},{9,5},{10,... | collective-permute-start | bytes 73736 | tf_op jit(solution)/shard_map/ppermute | solution.py:222
  6.0 1.5 %collective-permute-start.1 = (bf16[96,128]{1,0:T(8,128)(2,1)S(1)}, bf16[96,128]{1,0:T(8,128)(2,1)S(1)}, u32[]{:S(2)}, u32[]{:S(2)}) collective-permute-start(bf16[96,128]{1,0:T(8,128)(2,1)S(1)} %get-tuple-element.36), channel_id=1, source_target_pairs={{0,4},{1,5},{2,6},{3,7},{4,0},{5,1},{6,2},{7,3},{8,12},{9,13},{10,... | collective-permute-start | bytes 73736 | tf_op jit(solution)/shard_map/ppermute | solution.py:221
  7.5 0.0 copy-done
  7.5 1.1 %shard_map.60 = (bf16[729,192]{1,0:T(8,128)(2,1)S(1)}, f32[729,128]{1,0:T(8,128)S(1)}, f32[729,128]{1,0:T(8,128)S(1)}, bf16[729,192]{1,0:T(8,128)(2,1)S(1)}) custom-call(f32[768,8]{1,0:T(8,128)S(1)} %get-tuple-element.17.columns, s32[2,81]{1,0:T(2,128)S(1)} %copy-done, f32[729,128]{1,0:T(8,128)S(1)} %get-tuple-element.18.local, ...), custom_call_target="tpu_custom_call" | custom-call | tf_op jit(solution)/shard_map/pallas_call | solution.py:226
  8.6 0.0 collective-permute-done
  8.6 1.2 %collective-permute-done.1 = bf16[96,128]{1,0:T(8,128)(2,1)S(1)} collective-permute-done((bf16[96,128]{1,0:T(8,128)(2,1)S(1)}, bf16[96,128]{1,0:T(8,128)(2,1)S(1)}, u32[]{:S(2)}, u32[]{:S(2)}) %collective-permute-start.1) | collective-permute-done | bytes 24608 | tf_op jit(solution)/shard_map/ppermute | solution.py:221
  9.8 0.0 copy-start.1
  9.9 0.3 shard_map.61
  10.1 1.1 %collective-permute-start.5 = (bf16[729,128]{1,0:T(8,128)(2,1)S(1)}, bf16[729,128]{1,0:T(8,128)(2,1)S(1)}, u32[]{:S(2)}, u32[]{:S(2)}) collective-permute-start(bf16[729,128]{1,0:T(8,128)(2,1)S(1)} %get-tuple-element.27.rest_0_), channel_id=1, source_target_pairs={{0,2},{1,3},{2,0},{3,1},{4,6},{5,7},{6,4},{7,5},{8,10},{9,11},{10,... | collective-permute-start | bytes 559880 | tf_op jit(solution)/shard_map/ppermute | solution.py:250
  11.2 0.3 shard_map.62
  11.5 1.1 %collective-permute-start.2 = (bf16[96,256]{1,0:T(8,128)(2,1)S(1)}, bf16[96,256]{1,0:T(8,128)(2,1)S(1)}, u32[]{:S(2)}, u32[]{:S(2)}) collective-permute-start(bf16[96,256]{1,0:T(8,128)(2,1)S(1)} %get-tuple-element.33), channel_id=1, source_target_pairs={{0,2},{1,3},{2,0},{3,1},{4,8},{5,9},{6,10},{7,11},{8,4},{9,5},{10,... | collective-permute-start | bytes 147464 | tf_op jit(solution)/shard_map/ppermute | solution.py:222
  12.6 2.4 %collective-permute-start.3 = (bf16[96,256]{1,0:T(8,128)(2,1)S(1)}, bf16[96,256]{1,0:T(8,128)(2,1)S(1)}, u32[]{:S(2)}, u32[]{:S(2)}) collective-permute-start(bf16[96,256]{1,0:T(8,128)(2,1)S(1)} %get-tuple-element.32), channel_id=1, source_target_pairs={{0,4},{1,5},{2,6},{3,7},{4,0},{5,1},{6,2},{7,3},{8,12},{9,13},{10,... | collective-permute-start | bytes 147464 | tf_op jit(solution)/shard_map/ppermute | solution.py:221
  15.0 0.0 copy-done.1
  15.0 0.1 collective-permute-start.4
  15.1 0.7 %collective-permute-done.5.rest_2_ = bf16[729,128]{1,0:T(8,128)(2,1)S(1)} collective-permute-done((bf16[729,128]{1,0:T(8,128)(2,1)S(1)}, bf16[729,128]{1,0:T(8,128)(2,1)S(1)}, u32[]{:S(2)}, u32[]{:S(2)}) %collective-permute-start.5) | collective-permute-done | bytes 186656 | tf_op jit(solution)/shard_map/ppermute | solution.py:250
  15.8 0.0 collective-permute-start.6
  15.8 0.5 %collective-permute-done.2 = bf16[96,256]{1,0:T(8,128)(2,1)S(1)} collective-permute-done((bf16[96,256]{1,0:T(8,128)(2,1)S(1)}, bf16[96,256]{1,0:T(8,128)(2,1)S(1)}, u32[]{:S(2)}, u32[]{:S(2)}) %collective-permute-start.2) | collective-permute-done | bytes 49184 | tf_op jit(solution)/shard_map/ppermute | solution.py:222
  16.3 0.7 %collective-permute-done.3 = bf16[96,256]{1,0:T(8,128)(2,1)S(1)} collective-permute-done((bf16[96,256]{1,0:T(8,128)(2,1)S(1)}, bf16[96,256]{1,0:T(8,128)(2,1)S(1)}, u32[]{:S(2)}, u32[]{:S(2)}) %collective-permute-start.3) | collective-permute-done | bytes 49184 | tf_op jit(solution)/shard_map/ppermute | solution.py:221
  17.1 0.0 collective-permute-done.4.rest_1_
  17.1 0.1 collective-permute-done.6.rest_3_
  17.2 0.7 %shard_map.63 = (f32[729,128]{1,0:T(8,128)S(1)}, bf16[4,128,128]{2,1,0:T(8,128)(2,1)S(1)}) custom-call(f32[729,128]{1,0:T(8,128)S(1)} %get-tuple-element.24.result, bf16[729,128]{1,0:T(8,128)(2,1)S(1)} %get-tuple-element.22.start, f32[729,128]{1,0:T(8,128)S(1)} %get-tuple-element.23.keep, bf16[96,256]{1,0:T(8,128)(2,1)S(1)} %get-tuple-element.31.before, ...), custom_call_target="tpu_custom_call" | custom-call | tf_op jit(solution)/shard_map/pallas_call | solution.py:259
  17.9 2.0 %collective-permute-start.7 = (bf16[4,128,128]{2,1,0:T(8,128)(2,1)S(1)}, bf16[4,128,128]{2,1,0:T(8,128)(2,1)S(1)}, u32[]{:S(2)}, u32[]{:S(2)}) collective-permute-start(bf16[4,128,128]{2,1,0:T(8,128)(2,1)S(1)} %get-tuple-element.29), channel_id=1, source_target_pairs={{0,4},{1,9},{2,6},{3,11},{4,0},{5,13},{6,2},{7,15},{8,12},{9,1},{1... | collective-permute-start | bytes 393224 | tf_op jit(solution)/shard_map/ppermute | solution.py:52
  19.9 1.6 %collective-permute-start.8 = (bf16[4,128,128]{2,1,0:T(8,128)(2,1)S(1)}, bf16[4,128,128]{2,1,0:T(8,128)(2,1)S(1)}, u32[]{:S(2)}, u32[]{:S(2)}) collective-permute-start(bf16[4,128,128]{2,1,0:T(8,128)(2,1)S(1)} %get-tuple-element.29), channel_id=1, source_target_pairs={{0,8},{1,5},{2,10},{3,7},{4,12},{5,1},{6,14},{7,3},{8,0},{9,13},{1... | collective-permute-start | bytes 393224 | tf_op jit(solution)/shard_map/ppermute | solution.py:52
  21.5 0.0 collective-permute-start.9
  21.5 0.5 %fusion.2 = f32[729,128]{1,0:T(8,128)S(1)} fusion(s32[729]{0:T(1024)S(1)} %reduce, f32[729,128]{1,0:T(8,128)S(1)} %get-tuple-element.28), kind=kOutput, calls=%fused_computation.3 | convolution fusion | flops 137233520 | bytes 749412 | tf_op jit(solution)/shard_map/dot_general | solution.py:62
  22.0 0.5 %fusion = f32[729,128]{1,0:T(8,128)S(1)} fusion(s32[729]{0:T(1024)S(1)} %reduce, f32[729,128]{1,0:T(8,128)S(1)} %get-tuple-element.28), kind=kOutput, calls=%fused_computation.1 | convolution fusion | flops 136673648 | bytes 749412 | tf_op jit(solution)/shard_map/dot_general | solution.py:62
  22.5 2.5 %collective-permute-done.7 = bf16[4,128,128]{2,1,0:T(8,128)(2,1)S(1)} collective-permute-done((bf16[4,128,128]{2,1,0:T(8,128)(2,1)S(1)}, bf16[4,128,128]{2,1,0:T(8,128)(2,1)S(1)}, u32[]{:S(2)}, u32[]{:S(2)}) %collective-permute-start.7) | collective-permute-done | bytes 131104 | tf_op jit(solution)/shard_map/ppermute | solution.py:52
  25.0 0.9 %collective-permute-done.8 = bf16[4,128,128]{2,1,0:T(8,128)(2,1)S(1)} collective-permute-done((bf16[4,128,128]{2,1,0:T(8,128)(2,1)S(1)}, bf16[4,128,128]{2,1,0:T(8,128)(2,1)S(1)}, u32[]{:S(2)}, u32[]{:S(2)}) %collective-permute-start.8) | collective-permute-done | bytes 131104 | tf_op jit(solution)/shard_map/ppermute | solution.py:52
  25.9 1.5 %collective-permute-done.9 = bf16[4,128,128]{2,1,0:T(8,128)(2,1)S(1)} collective-permute-done((bf16[4,128,128]{2,1,0:T(8,128)(2,1)S(1)}, bf16[4,128,128]{2,1,0:T(8,128)(2,1)S(1)}, u32[]{:S(2)}, u32[]{:S(2)}) %collective-permute-start.9) | collective-permute-done | bytes 131104 | tf_op jit(solution)/shard_map/ppermute | solution.py:52
  27.4 0.1 add_convert_fusion
  27.4 3.7 %collective-permute-start.10 = (bf16[4,128,128]{2,1,0:T(8,128)(2,1)S(1)}, bf16[4,128,128]{2,1,0:T(8,128)(2,1)S(1)}, u32[]{:S(2)}, u32[]{:S(2)}) collective-permute-start(bf16[4,128,128]{2,1,0:T(8,128)(2,1)S(1)} %add_convert_fusion), channel_id=1, source_target_pairs={{0,24},{1,25},{2,26},{3,27},{4,28},{5,29},{6,30},{7,31},{8,16},{9,... | collective-permute-start | bytes 393224 | tf_op jit(solution)/shard_map/ppermute | solution.py:52
  31.2 1.3 %fusion.4 = f32[729,128]{1,0:T(8,128)} fusion(f32[729,128]{1,0:T(8,128)S(1)} %fusion, f32[729,128]{1,0:T(8,128)S(1)} %fusion.2, s32[729]{0:T(1024)S(1)} %reduce, f32[729,128]{1,0:T(8,128)S(1)} %get-tuple-element.28), kind=kOutput, calls=%fused_computation.5 | convolution fusion | flops 137140208 | bytes 1495908 | tf_op jit(solution)/shard_map/dot_general | solution.py:62
  32.5 1.9 %collective-permute-done.10 = bf16[4,128,128]{2,1,0:T(8,128)(2,1)S(1)} collective-permute-done((bf16[4,128,128]{2,1,0:T(8,128)(2,1)S(1)}, bf16[4,128,128]{2,1,0:T(8,128)(2,1)S(1)}, u32[]{:S(2)}, u32[]{:S(2)}) %collective-permute-start.10) | collective-permute-done | bytes 131104 | tf_op jit(solution)/shard_map/ppermute | solution.py:52
  34.3 0.7 %add_multiply_fusion = f32[4,128,128]{2,1,0:T(8,128)} fusion(bf16[4,128,128]{2,1,0:T(8,128)(2,1)S(1)} %collective-permute-done.10, bf16[4,128,128]{2,1,0:T(8,128)(2,1)S(1)} %add_convert_fusion), kind=kLoop, calls=%fused_computation.11 | loop fusion | flops 262144 | bytes 524288 | tf_op jit(solution)/shard_map/mul | solution.py:266
  (5 shorter events, 0.1 us)
Async XLA Ops:
  0.6 6.9 %copy-start = (s32[2,81]{1,0:T(2,128)S(1)}, s32[2,81]{1,0:T(2,128)}, u32[]{:S(2)}) copy-start(s32[2,81]{1,0:T(2,128)} %faces.1) | copy-start | bytes 1948
  3.0 5.6 %collective-permute-start = (bf16[96,128]{1,0:T(8,128)(2,1)S(1)}, bf16[96,128]{1,0:T(8,128)(2,1)S(1)}, u32[]{:S(2)}, u32[]{:S(2)}) collective-permute-start(bf16[96,128]{1,0:T(8,128)(2,1)S(1)} %get-tuple-element.37), channel_id=1, source_target_pairs={{0,2},{1,3},{2,0},{3,1},{4,8},{5,9},{6,10},{7,11},{8,4},{9,5},{10,... | collective-permute-start | bytes 73736 | tf_op jit(solution)/shard_map/ppermute | solution.py:222
  6.0 3.8 %collective-permute-start.1 = (bf16[96,128]{1,0:T(8,128)(2,1)S(1)}, bf16[96,128]{1,0:T(8,128)(2,1)S(1)}, u32[]{:S(2)}, u32[]{:S(2)}) collective-permute-start(bf16[96,128]{1,0:T(8,128)(2,1)S(1)} %get-tuple-element.36), channel_id=1, source_target_pairs={{0,4},{1,5},{2,6},{3,7},{4,0},{5,1},{6,2},{7,3},{8,12},{9,13},{10,... | collective-permute-start | bytes 73736 | tf_op jit(solution)/shard_map/ppermute | solution.py:221
  9.8 5.1 %copy-start.1 = (s32[1,729]{1,0:T(1,128)S(1)}, s32[1,729]{1,0:T(1,128)}, u32[]{:S(2)}) copy-start(s32[1,729]{1,0:T(1,128)} %cell_hbm.1) | copy-start | bytes 8752
  10.1 5.6 %collective-permute-start.5 = (bf16[729,128]{1,0:T(8,128)(2,1)S(1)}, bf16[729,128]{1,0:T(8,128)(2,1)S(1)}, u32[]{:S(2)}, u32[]{:S(2)}) collective-permute-start(bf16[729,128]{1,0:T(8,128)(2,1)S(1)} %get-tuple-element.27.rest_0_), channel_id=1, source_target_pairs={{0,2},{1,3},{2,0},{3,1},{4,6},{5,7},{6,4},{7,5},{8,10},{9,11},{10,... | collective-permute-start | bytes 559880 | tf_op jit(solution)/shard_map/ppermute | solution.py:250
  11.5 4.8 %collective-permute-start.2 = (bf16[96,256]{1,0:T(8,128)(2,1)S(1)}, bf16[96,256]{1,0:T(8,128)(2,1)S(1)}, u32[]{:S(2)}, u32[]{:S(2)}) collective-permute-start(bf16[96,256]{1,0:T(8,128)(2,1)S(1)} %get-tuple-element.33), channel_id=1, source_target_pairs={{0,2},{1,3},{2,0},{3,1},{4,8},{5,9},{6,10},{7,11},{8,4},{9,5},{10,... | collective-permute-start | bytes 147464 | tf_op jit(solution)/shard_map/ppermute | solution.py:222
  12.6 4.5 %collective-permute-start.3 = (bf16[96,256]{1,0:T(8,128)(2,1)S(1)}, bf16[96,256]{1,0:T(8,128)(2,1)S(1)}, u32[]{:S(2)}, u32[]{:S(2)}) collective-permute-start(bf16[96,256]{1,0:T(8,128)(2,1)S(1)} %get-tuple-element.32), channel_id=1, source_target_pairs={{0,4},{1,5},{2,6},{3,7},{4,0},{5,1},{6,2},{7,3},{8,12},{9,13},{10,... | collective-permute-start | bytes 147464 | tf_op jit(solution)/shard_map/ppermute | solution.py:221
  15.0 2.1 %collective-permute-start.4 = (bf16[729,128]{1,0:T(8,128)(2,1)S(1)}, bf16[729,128]{1,0:T(8,128)(2,1)S(1)}, u32[]{:S(2)}, u32[]{:S(2)}) collective-permute-start(bf16[729,128]{1,0:T(8,128)(2,1)S(1)} %get-tuple-element.27.rest_0_), channel_id=1, source_target_pairs={{0,1},{1,0},{2,3},{3,2},{4,5},{5,4},{6,7},{7,6},{8,9},{9,8},{10,11... | collective-permute-start | bytes 559880 | tf_op jit(solution)/shard_map/ppermute | solution.py:250
  15.8 1.4 %collective-permute-start.6 = (bf16[729,128]{1,0:T(8,128)(2,1)S(1)}, bf16[729,128]{1,0:T(8,128)(2,1)S(1)}, u32[]{:S(2)}, u32[]{:S(2)}) collective-permute-start(bf16[729,128]{1,0:T(8,128)(2,1)S(1)} %collective-permute-done.5.rest_2_), channel_id=1, source_target_pairs={{0,1},{1,0},{2,3},{3,2},{4,5},{5,4},{6,7},{7,6},{8,9},{9,8},{10,11... | collective-permute-start | bytes 559880 | tf_op jit(solution)/shard_map/ppermute | solution.py:250
  17.9 7.1 %collective-permute-start.7 = (bf16[4,128,128]{2,1,0:T(8,128)(2,1)S(1)}, bf16[4,128,128]{2,1,0:T(8,128)(2,1)S(1)}, u32[]{:S(2)}, u32[]{:S(2)}) collective-permute-start(bf16[4,128,128]{2,1,0:T(8,128)(2,1)S(1)} %get-tuple-element.29), channel_id=1, source_target_pairs={{0,4},{1,9},{2,6},{3,11},{4,0},{5,13},{6,2},{7,15},{8,12},{9,1},{1... | collective-permute-start | bytes 393224 | tf_op jit(solution)/shard_map/ppermute | solution.py:52
  19.9 6.0 %collective-permute-start.8 = (bf16[4,128,128]{2,1,0:T(8,128)(2,1)S(1)}, bf16[4,128,128]{2,1,0:T(8,128)(2,1)S(1)}, u32[]{:S(2)}, u32[]{:S(2)}) collective-permute-start(bf16[4,128,128]{2,1,0:T(8,128)(2,1)S(1)} %get-tuple-element.29), channel_id=1, source_target_pairs={{0,8},{1,5},{2,10},{3,7},{4,12},{5,1},{6,14},{7,3},{8,0},{9,13},{1... | collective-permute-start | bytes 393224 | tf_op jit(solution)/shard_map/ppermute | solution.py:52
  21.5 5.9 %collective-permute-start.9 = (bf16[4,128,128]{2,1,0:T(8,128)(2,1)S(1)}, bf16[4,128,128]{2,1,0:T(8,128)(2,1)S(1)}, u32[]{:S(2)}, u32[]{:S(2)}) collective-permute-start(bf16[4,128,128]{2,1,0:T(8,128)(2,1)S(1)} %get-tuple-element.29), channel_id=1, source_target_pairs={{0,12},{1,13},{2,14},{3,15},{4,8},{5,9},{6,10},{7,11},{8,4},{9,5},... | collective-permute-start | bytes 393224 | tf_op jit(solution)/shard_map/ppermute | solution.py:52
  27.4 6.9 %collective-permute-start.10 = (bf16[4,128,128]{2,1,0:T(8,128)(2,1)S(1)}, bf16[4,128,128]{2,1,0:T(8,128)(2,1)S(1)}, u32[]{:S(2)}, u32[]{:S(2)}) collective-permute-start(bf16[4,128,128]{2,1,0:T(8,128)(2,1)S(1)} %add_convert_fusion), channel_id=1, source_target_pairs={{0,24},{1,25},{2,26},{3,27},{4,28},{5,29},{6,30},{7,31},{8,16},{9,... | collective-permute-start | bytes 393224 | tf_op jit(solution)/shard_map/ppermute | solution.py:52

commit v8 on v7

--- a/solution.py
+++ b/solution.py
@@ -42,8 +42,9 @@
     steps = [[lambda part, band, m=m: part ^ m[band % 2] for m in step] for step in steps]
     for stride, radix in other:
         steps.append([lambda part, band, d=(stride, radix, by): turn(part, *d) for by in range(1, radix)])
+    kind = BF16 if len(steps) <= 3 else F32
     for step in steps:
-        word = value.astype(BF16)
+        word = value.astype(kind)
         words = [word.astype(F32)]
         for move in step:
             pairs = [
@@ -71,11 +72,12 @@
 
 
 def row_chunks(count):
-    return [(first, min(first + 256, count)) for first in range(0, count, 256)]
-
-
-def tall_dot(rows_of, values):
-    return jnp.concatenate([dot(rows_of(first, last), values) for first, last in row_chunks(values.shape[0])], axis=0)
+    return [(first, min(first + 368, count)) for first in range(0, count, 368)]
+
+
+def tall_dot(rows_of, values, count=None):
+    chunks = row_chunks(count or values.shape[0])
+    return jnp.concatenate([dot(rows_of(first, last), values) for first, last in chunks], axis=0)
 
 
 def first_kernel(waves_hbm, cell_hbm, faces_hbm, ham_hbm, start, local, sums, ham, one, columns, waves, cell, faces, rows, sems):
@@ -133,7 +135,7 @@
 
 def second_kernel(before, after, mine, border, start, keep, result, block):
     halo = 0.5 * jnp.concatenate([before[...], after[...]], axis=0).astype(F32)
-    sums = mine[...] + dot(border[...], halo.astype(BF16))
+    sums = mine[...] + tall_dot(lambda first, last: border[first:last], halo.astype(BF16), border.shape[0])
     result[...] = sums
     block[...] = (sums - start[...].astype(F32) * keep[...]).astype(BF16)
 
@@ -147,7 +149,8 @@
     width = result.shape[1]
     here = jnp.concatenate([before[:, :width], after[:, :width]], axis=0)
     there = jnp.concatenate([before[:, width:], jnp.zeros((after.shape[0], width), BF16)], axis=0)
-    halo = dot(one_t[...], jnp.concatenate([here, there], axis=1))
+    halo_in = jnp.concatenate([here, there], axis=1)
+    halo = tall_dot(lambda first, last: one_t[first:last], halo_in, one_t.shape[0])
     older = start[...].astype(F32)
     whole = result[...] + halo[:, :width]
     filtered[...] = whole - older

time: 35.2 us -> 35.1 us (level)
  no operation moved by 1% of the time
where the time goes in v8:
time: 35.1 us; the launch traced here: 34.9 us
  starting transfers between devices  16.5 us (47%)
  waiting for transfers between devices  10.1 us (29%)
  Pallas kernels  4.39 us (13%)
  matrix products  2.28 us (6%)
  other arithmetic  0.87 us (2%)
  between operations  0.77 us (2%)
    ppermute x4, starting transfers between devices, sum_over_cells(): words.append(lax.ppermute(word, ('cells', 'bands'), pairs).astype(F32))  7.33 us
    ppermute x4, waiting for transfers between devices, sum_over_cells(): words.append(lax.ppermute(word, ('cells', 'bands'), pairs).astype(F32))  6.72 us
    ppermute x2, starting transfers between devices, neighbours(): odd_even = lax.ppermute(jnp.where(odd, high, low), both, pair_swap(1))  4.1 us
    ppermute x2, starting transfers between devices, neighbours(): even_odd = lax.ppermute(jnp.where(odd, low, high), both, pair_swap(0))  3.91 us
    pallas_call x1, Pallas kernels, body(): pl.pallas_call(first_kernel, out_shape=(shape(nodal, BF16), shape(nodal,...  2.31 us
    dot_general x3, matrix products, dot(): return jnp.dot(a, b, preferred_element_type=F32)  2.28 us
    ppermute x2, waiting for transfers between devices, neighbours(): even_odd = lax.ppermute(jnp.where(odd, low, high), both, pair_swap(0))  2.02 us
    ppermute x3, starting transfers between devices, body(): lax.ppermute(blocks[at], 'bands', turned(groups, stride, radix, radix - by))  1.16 us
  transfers between devices with their start and end apart: 11, of which 9 were waited for; matrix products, arithmetic and copies ran while one was open for 7% of the time, Pallas kernels for 4%

profile of v8, /device:TPU:0, one launch (start us, length us, event | category | flops | bytes accessed | tf_op | source)
XLA Modules:
  0.0 34.9 jit_solution(3931887459915744291)
XLA Ops:
  0.6 0.0 copy-start
  0.7 2.3 %shard_map.59 = (bf16[729,128]{1,0:T(8,128)(2,1)S(1)}, f32[729,128]{1,0:T(8,128)S(1)}, bf16[192,128]{1,0:T(8,128)(2,1)S(1)}, bf16[729,729]{1,0:T(8,128)(2,1)S(1)...) custom-call(bf16[729,128]{1,0:T(8,128)(2,1)} %waves_hbm.1, s32[1,729]{1,0:T(1,128)} %cell_hbm.1, s32[2,81]{1,0:T(2,128)} %faces.1, ...), custom_call_target="tpu_custom_call" | custom-call | tf_op jit(solution)/shard_map/pallas_call | solution.py:183
  3.0 3.0 %collective-permute-start = (bf16[96,128]{1,0:T(8,128)(2,1)S(1)}, bf16[96,128]{1,0:T(8,128)(2,1)S(1)}, u32[]{:S(2)}, u32[]{:S(2)}) collective-permute-start(bf16[96,128]{1,0:T(8,128)(2,1)S(1)} %get-tuple-element.37), channel_id=1, source_target_pairs={{0,2},{1,3},{2,0},{3,1},{4,8},{5,9},{6,10},{7,11},{8,4},{9,5},{10,... | collective-permute-start | bytes 73736 | tf_op jit(solution)/shard_map/ppermute | solution.py:225
  6.0 1.5 %collective-permute-start.1 = (bf16[96,128]{1,0:T(8,128)(2,1)S(1)}, bf16[96,128]{1,0:T(8,128)(2,1)S(1)}, u32[]{:S(2)}, u32[]{:S(2)}) collective-permute-start(bf16[96,128]{1,0:T(8,128)(2,1)S(1)} %get-tuple-element.36), channel_id=1, source_target_pairs={{0,4},{1,5},{2,6},{3,7},{4,0},{5,1},{6,2},{7,3},{8,12},{9,13},{10,... | collective-permute-start | bytes 73736 | tf_op jit(solution)/shard_map/ppermute | solution.py:224
  7.5 0.0 copy-done
  7.5 1.0 %shard_map.60 = (bf16[729,192]{1,0:T(8,128)(2,1)S(1)}, f32[729,128]{1,0:T(8,128)S(1)}, f32[729,128]{1,0:T(8,128)S(1)}, bf16[729,192]{1,0:T(8,128)(2,1)S(1)}) custom-call(f32[768,8]{1,0:T(8,128)S(1)} %get-tuple-element.17.columns, s32[2,81]{1,0:T(2,128)S(1)} %copy-done, f32[729,128]{1,0:T(8,128)S(1)} %get-tuple-element.18.local, ...), custom_call_target="tpu_custom_call" | custom-call | tf_op jit(solution)/shard_map/pallas_call | solution.py:229
  8.5 0.0 collective-permute-done
  8.6 1.3 %collective-permute-done.1 = bf16[96,128]{1,0:T(8,128)(2,1)S(1)} collective-permute-done((bf16[96,128]{1,0:T(8,128)(2,1)S(1)}, bf16[96,128]{1,0:T(8,128)(2,1)S(1)}, u32[]{:S(2)}, u32[]{:S(2)}) %collective-permute-start.1) | collective-permute-done | bytes 24608 | tf_op jit(solution)/shard_map/ppermute | solution.py:224
  9.9 0.0 copy-start.1
  9.9 0.3 shard_map.61
  10.1 1.1 %collective-permute-start.5 = (bf16[729,128]{1,0:T(8,128)(2,1)S(1)}, bf16[729,128]{1,0:T(8,128)(2,1)S(1)}, u32[]{:S(2)}, u32[]{:S(2)}) collective-permute-start(bf16[729,128]{1,0:T(8,128)(2,1)S(1)} %get-tuple-element.27.rest_0_), channel_id=1, source_target_pairs={{0,2},{1,3},{2,0},{3,1},{4,6},{5,7},{6,4},{7,5},{8,10},{9,11},{10,... | collective-permute-start | bytes 559880 | tf_op jit(solution)/shard_map/ppermute | solution.py:253
  11.2 0.3 shard_map.62
  11.5 1.1 %collective-permute-start.2 = (bf16[96,256]{1,0:T(8,128)(2,1)S(1)}, bf16[96,256]{1,0:T(8,128)(2,1)S(1)}, u32[]{:S(2)}, u32[]{:S(2)}) collective-permute-start(bf16[96,256]{1,0:T(8,128)(2,1)S(1)} %get-tuple-element.33), channel_id=1, source_target_pairs={{0,2},{1,3},{2,0},{3,1},{4,8},{5,9},{6,10},{7,11},{8,4},{9,5},{10,... | collective-permute-start | bytes 147464 | tf_op jit(solution)/shard_map/ppermute | solution.py:225
  12.6 2.4 %collective-permute-start.3 = (bf16[96,256]{1,0:T(8,128)(2,1)S(1)}, bf16[96,256]{1,0:T(8,128)(2,1)S(1)}, u32[]{:S(2)}, u32[]{:S(2)}) collective-permute-start(bf16[96,256]{1,0:T(8,128)(2,1)S(1)} %get-tuple-element.32), channel_id=1, source_target_pairs={{0,4},{1,5},{2,6},{3,7},{4,0},{5,1},{6,2},{7,3},{8,12},{9,13},{10,... | collective-permute-start | bytes 147464 | tf_op jit(solution)/shard_map/ppermute | solution.py:224
  15.0 0.0 copy-done.1
  15.0 0.1 collective-permute-start.4
  15.1 0.7 %collective-permute-done.5.rest_2_ = bf16[729,128]{1,0:T(8,128)(2,1)S(1)} collective-permute-done((bf16[729,128]{1,0:T(8,128)(2,1)S(1)}, bf16[729,128]{1,0:T(8,128)(2,1)S(1)}, u32[]{:S(2)}, u32[]{:S(2)}) %collective-permute-start.5) | collective-permute-done | bytes 186656 | tf_op jit(solution)/shard_map/ppermute | solution.py:253
  15.8 0.0 collective-permute-start.6
  15.8 0.5 %collective-permute-done.2 = bf16[96,256]{1,0:T(8,128)(2,1)S(1)} collective-permute-done((bf16[96,256]{1,0:T(8,128)(2,1)S(1)}, bf16[96,256]{1,0:T(8,128)(2,1)S(1)}, u32[]{:S(2)}, u32[]{:S(2)}) %collective-permute-start.2) | collective-permute-done | bytes 49184 | tf_op jit(solution)/shard_map/ppermute | solution.py:225
  16.3 0.7 %collective-permute-done.3 = bf16[96,256]{1,0:T(8,128)(2,1)S(1)} collective-permute-done((bf16[96,256]{1,0:T(8,128)(2,1)S(1)}, bf16[96,256]{1,0:T(8,128)(2,1)S(1)}, u32[]{:S(2)}, u32[]{:S(2)}) %collective-permute-start.3) | collective-permute-done | bytes 49184 | tf_op jit(solution)/shard_map/ppermute | solution.py:224
  17.0 0.0 collective-permute-done.4.rest_1_
  17.1 0.2 collective-permute-done.6.rest_3_
  17.2 0.6 %shard_map.63 = (f32[729,128]{1,0:T(8,128)S(1)}, bf16[4,128,128]{2,1,0:T(8,128)(2,1)S(1)}) custom-call(f32[729,128]{1,0:T(8,128)S(1)} %get-tuple-element.24.result, bf16[729,128]{1,0:T(8,128)(2,1)S(1)} %get-tuple-element.22.start, f32[729,128]{1,0:T(8,128)S(1)} %get-tuple-element.23.keep, bf16[96,256]{1,0:T(8,128)(2,1)S(1)} %get-tuple-element.31.before, ...), custom_call_target="tpu_custom_call" | custom-call | tf_op jit(solution)/shard_map/pallas_call | solution.py:262
  17.8 2.0 %collective-permute-start.7 = (bf16[4,128,128]{2,1,0:T(8,128)(2,1)S(1)}, bf16[4,128,128]{2,1,0:T(8,128)(2,1)S(1)}, u32[]{:S(2)}, u32[]{:S(2)}) collective-permute-start(bf16[4,128,128]{2,1,0:T(8,128)(2,1)S(1)} %get-tuple-element.29), channel_id=1, source_target_pairs={{0,4},{1,9},{2,6},{3,11},{4,0},{5,13},{6,2},{7,15},{8,12},{9,1},{1... | collective-permute-start | bytes 393224 | tf_op jit(solution)/shard_map/ppermute | solution.py:53
  19.8 1.6 %collective-permute-start.8 = (bf16[4,128,128]{2,1,0:T(8,128)(2,1)S(1)}, bf16[4,128,128]{2,1,0:T(8,128)(2,1)S(1)}, u32[]{:S(2)}, u32[]{:S(2)}) collective-permute-start(bf16[4,128,128]{2,1,0:T(8,128)(2,1)S(1)} %get-tuple-element.29), channel_id=1, source_target_pairs={{0,8},{1,5},{2,10},{3,7},{4,12},{5,1},{6,14},{7,3},{8,0},{9,13},{1... | collective-permute-start | bytes 393224 | tf_op jit(solution)/shard_map/ppermute | solution.py:53
  21.4 0.0 collective-permute-start.9
  21.4 0.5 %fusion.2 = f32[729,128]{1,0:T(8,128)S(1)} fusion(s32[729]{0:T(1024)S(1)} %reduce, f32[729,128]{1,0:T(8,128)S(1)} %get-tuple-element.28), kind=kOutput, calls=%fused_computation.3 | convolution fusion | flops 137233520 | bytes 749412 | tf_op jit(solution)/shard_map/dot_general | solution.py:63
  21.9 0.5 %fusion = f32[729,128]{1,0:T(8,128)S(1)} fusion(s32[729]{0:T(1024)S(1)} %reduce, f32[729,128]{1,0:T(8,128)S(1)} %get-tuple-element.28), kind=kOutput, calls=%fused_computation.1 | convolution fusion | flops 136673648 | bytes 749412 | tf_op jit(solution)/shard_map/dot_general | solution.py:63
  22.4 2.5 %collective-permute-done.7 = bf16[4,128,128]{2,1,0:T(8,128)(2,1)S(1)} collective-permute-done((bf16[4,128,128]{2,1,0:T(8,128)(2,1)S(1)}, bf16[4,128,128]{2,1,0:T(8,128)(2,1)S(1)}, u32[]{:S(2)}, u32[]{:S(2)}) %collective-permute-start.7) | collective-permute-done | bytes 131104 | tf_op jit(solution)/shard_map/ppermute | solution.py:53
  24.9 0.9 %collective-permute-done.8 = bf16[4,128,128]{2,1,0:T(8,128)(2,1)S(1)} collective-permute-done((bf16[4,128,128]{2,1,0:T(8,128)(2,1)S(1)}, bf16[4,128,128]{2,1,0:T(8,128)(2,1)S(1)}, u32[]{:S(2)}, u32[]{:S(2)}) %collective-permute-start.8) | collective-permute-done | bytes 131104 | tf_op jit(solution)/shard_map/ppermute | solution.py:53
  25.7 1.5 %collective-permute-done.9 = bf16[4,128,128]{2,1,0:T(8,128)(2,1)S(1)} collective-permute-done((bf16[4,128,128]{2,1,0:T(8,128)(2,1)S(1)}, bf16[4,128,128]{2,1,0:T(8,128)(2,1)S(1)}, u32[]{:S(2)}, u32[]{:S(2)}) %collective-permute-start.9) | collective-permute-done | bytes 131104 | tf_op jit(solution)/shard_map/ppermute | solution.py:53
  27.2 0.1 add_convert_fusion
  27.3 3.7 %collective-permute-start.10 = (bf16[4,128,128]{2,1,0:T(8,128)(2,1)S(1)}, bf16[4,128,128]{2,1,0:T(8,128)(2,1)S(1)}, u32[]{:S(2)}, u32[]{:S(2)}) collective-permute-start(bf16[4,128,128]{2,1,0:T(8,128)(2,1)S(1)} %add_convert_fusion), channel_id=1, source_target_pairs={{0,24},{1,25},{2,26},{3,27},{4,28},{5,29},{6,30},{7,31},{8,16},{9,... | collective-permute-start | bytes 393224 | tf_op jit(solution)/shard_map/ppermute | solution.py:53
  31.1 1.3 %fusion.4 = f32[729,128]{1,0:T(8,128)} fusion(f32[729,128]{1,0:T(8,128)S(1)} %fusion, f32[729,128]{1,0:T(8,128)S(1)} %fusion.2, s32[729]{0:T(1024)S(1)} %reduce, f32[729,128]{1,0:T(8,128)S(1)} %get-tuple-element.28), kind=kOutput, calls=%fused_computation.5 | convolution fusion | flops 137140208 | bytes 1495908 | tf_op jit(solution)/shard_map/dot_general | solution.py:63
  32.3 1.9 %collective-permute-done.10 = bf16[4,128,128]{2,1,0:T(8,128)(2,1)S(1)} collective-permute-done((bf16[4,128,128]{2,1,0:T(8,128)(2,1)S(1)}, bf16[4,128,128]{2,1,0:T(8,128)(2,1)S(1)}, u32[]{:S(2)}, u32[]{:S(2)}) %collective-permute-start.10) | collective-permute-done | bytes 131104 | tf_op jit(solution)/shard_map/ppermute | solution.py:53
  34.2 0.7 %add_multiply_fusion = f32[4,128,128]{2,1,0:T(8,128)} fusion(bf16[4,128,128]{2,1,0:T(8,128)(2,1)S(1)} %collective-permute-done.10, bf16[4,128,128]{2,1,0:T(8,128)(2,1)S(1)} %add_convert_fusion), kind=kLoop, calls=%fused_computation.11 | loop fusion | flops 262144 | bytes 524288 | tf_op jit(solution)/shard_map/mul | solution.py:269
  (5 shorter events, 0.1 us)
Async XLA Ops:
  0.6 6.9 %copy-start = (s32[2,81]{1,0:T(2,128)S(1)}, s32[2,81]{1,0:T(2,128)}, u32[]{:S(2)}) copy-start(s32[2,81]{1,0:T(2,128)} %faces.1) | copy-start | bytes 1948
  3.0 5.6 %collective-permute-start = (bf16[96,128]{1,0:T(8,128)(2,1)S(1)}, bf16[96,128]{1,0:T(8,128)(2,1)S(1)}, u32[]{:S(2)}, u32[]{:S(2)}) collective-permute-start(bf16[96,128]{1,0:T(8,128)(2,1)S(1)} %get-tuple-element.37), channel_id=1, source_target_pairs={{0,2},{1,3},{2,0},{3,1},{4,8},{5,9},{6,10},{7,11},{8,4},{9,5},{10,... | collective-permute-start | bytes 73736 | tf_op jit(solution)/shard_map/ppermute | solution.py:225
  6.0 3.8 %collective-permute-start.1 = (bf16[96,128]{1,0:T(8,128)(2,1)S(1)}, bf16[96,128]{1,0:T(8,128)(2,1)S(1)}, u32[]{:S(2)}, u32[]{:S(2)}) collective-permute-start(bf16[96,128]{1,0:T(8,128)(2,1)S(1)} %get-tuple-element.36), channel_id=1, source_target_pairs={{0,4},{1,5},{2,6},{3,7},{4,0},{5,1},{6,2},{7,3},{8,12},{9,13},{10,... | collective-permute-start | bytes 73736 | tf_op jit(solution)/shard_map/ppermute | solution.py:224
  9.9 5.1 %copy-start.1 = (s32[1,729]{1,0:T(1,128)S(1)}, s32[1,729]{1,0:T(1,128)}, u32[]{:S(2)}) copy-start(s32[1,729]{1,0:T(1,128)} %cell_hbm.1) | copy-start | bytes 8752
  10.1 5.6 %collective-permute-start.5 = (bf16[729,128]{1,0:T(8,128)(2,1)S(1)}, bf16[729,128]{1,0:T(8,128)(2,1)S(1)}, u32[]{:S(2)}, u32[]{:S(2)}) collective-permute-start(bf16[729,128]{1,0:T(8,128)(2,1)S(1)} %get-tuple-element.27.rest_0_), channel_id=1, source_target_pairs={{0,2},{1,3},{2,0},{3,1},{4,6},{5,7},{6,4},{7,5},{8,10},{9,11},{10,... | collective-permute-start | bytes 559880 | tf_op jit(solution)/shard_map/ppermute | solution.py:253
  11.5 4.8 %collective-permute-start.2 = (bf16[96,256]{1,0:T(8,128)(2,1)S(1)}, bf16[96,256]{1,0:T(8,128)(2,1)S(1)}, u32[]{:S(2)}, u32[]{:S(2)}) collective-permute-start(bf16[96,256]{1,0:T(8,128)(2,1)S(1)} %get-tuple-element.33), channel_id=1, source_target_pairs={{0,2},{1,3},{2,0},{3,1},{4,8},{5,9},{6,10},{7,11},{8,4},{9,5},{10,... | collective-permute-start | bytes 147464 | tf_op jit(solution)/shard_map/ppermute | solution.py:225
  12.6 4.5 %collective-permute-start.3 = (bf16[96,256]{1,0:T(8,128)(2,1)S(1)}, bf16[96,256]{1,0:T(8,128)(2,1)S(1)}, u32[]{:S(2)}, u32[]{:S(2)}) collective-permute-start(bf16[96,256]{1,0:T(8,128)(2,1)S(1)} %get-tuple-element.32), channel_id=1, source_target_pairs={{0,4},{1,5},{2,6},{3,7},{4,0},{5,1},{6,2},{7,3},{8,12},{9,13},{10,... | collective-permute-start | bytes 147464 | tf_op jit(solution)/shard_map/ppermute | solution.py:224
  15.0 2.1 %collective-permute-start.4 = (bf16[729,128]{1,0:T(8,128)(2,1)S(1)}, bf16[729,128]{1,0:T(8,128)(2,1)S(1)}, u32[]{:S(2)}, u32[]{:S(2)}) collective-permute-start(bf16[729,128]{1,0:T(8,128)(2,1)S(1)} %get-tuple-element.27.rest_0_), channel_id=1, source_target_pairs={{0,1},{1,0},{2,3},{3,2},{4,5},{5,4},{6,7},{7,6},{8,9},{9,8},{10,11... | collective-permute-start | bytes 559880 | tf_op jit(solution)/shard_map/ppermute | solution.py:253
  15.8 1.4 %collective-permute-start.6 = (bf16[729,128]{1,0:T(8,128)(2,1)S(1)}, bf16[729,128]{1,0:T(8,128)(2,1)S(1)}, u32[]{:S(2)}, u32[]{:S(2)}) collective-permute-start(bf16[729,128]{1,0:T(8,128)(2,1)S(1)} %collective-permute-done.5.rest_2_), channel_id=1, source_target_pairs={{0,1},{1,0},{2,3},{3,2},{4,5},{5,4},{6,7},{7,6},{8,9},{9,8},{10,11... | collective-permute-start | bytes 559880 | tf_op jit(solution)/shard_map/ppermute | solution.py:253
  17.8 7.1 %collective-permute-start.7 = (bf16[4,128,128]{2,1,0:T(8,128)(2,1)S(1)}, bf16[4,128,128]{2,1,0:T(8,128)(2,1)S(1)}, u32[]{:S(2)}, u32[]{:S(2)}) collective-permute-start(bf16[4,128,128]{2,1,0:T(8,128)(2,1)S(1)} %get-tuple-element.29), channel_id=1, source_target_pairs={{0,4},{1,9},{2,6},{3,11},{4,0},{5,13},{6,2},{7,15},{8,12},{9,1},{1... | collective-permute-start | bytes 393224 | tf_op jit(solution)/shard_map/ppermute | solution.py:53
  19.8 5.9 %collective-permute-start.8 = (bf16[4,128,128]{2,1,0:T(8,128)(2,1)S(1)}, bf16[4,128,128]{2,1,0:T(8,128)(2,1)S(1)}, u32[]{:S(2)}, u32[]{:S(2)}) collective-permute-start(bf16[4,128,128]{2,1,0:T(8,128)(2,1)S(1)} %get-tuple-element.29), channel_id=1, source_target_pairs={{0,8},{1,5},{2,10},{3,7},{4,12},{5,1},{6,14},{7,3},{8,0},{9,13},{1... | collective-permute-start | bytes 393224 | tf_op jit(solution)/shard_map/ppermute | solution.py:53
  21.4 5.9 %collective-permute-start.9 = (bf16[4,128,128]{2,1,0:T(8,128)(2,1)S(1)}, bf16[4,128,128]{2,1,0:T(8,128)(2,1)S(1)}, u32[]{:S(2)}, u32[]{:S(2)}) collective-permute-start(bf16[4,128,128]{2,1,0:T(8,128)(2,1)S(1)} %get-tuple-element.29), channel_id=1, source_target_pairs={{0,12},{1,13},{2,14},{3,15},{4,8},{5,9},{6,10},{7,11},{8,4},{9,5},... | collective-permute-start | bytes 393224 | tf_op jit(solution)/shard_map/ppermute | solution.py:53
  27.3 6.9 %collective-permute-start.10 = (bf16[4,128,128]{2,1,0:T(8,128)(2,1)S(1)}, bf16[4,128,128]{2,1,0:T(8,128)(2,1)S(1)}, u32[]{:S(2)}, u32[]{:S(2)}) collective-permute-start(bf16[4,128,128]{2,1,0:T(8,128)(2,1)S(1)} %add_convert_fusion), channel_id=1, source_target_pairs={{0,24},{1,25},{2,26},{3,27},{4,28},{5,29},{6,30},{7,31},{8,16},{9,... | collective-permute-start | bytes 393224 | tf_op jit(solution)/shard_map/ppermute | solution.py:53

commit v9 on v8

--- a/solution.py
+++ b/solution.py
@@ -84,9 +84,7 @@
     count = waves.shape[0]
     shared = faces.shape[1]
     padded = one.shape[0] // 2
-    chunks = row_chunks(count)
-    pairs = [(cell_hbm, cell), (faces_hbm, faces), (waves_hbm, waves)]
-    pairs += [(ham_hbm.at[0, first:last], ham.at[first:last]) for first, last in chunks]
+    pairs = ((cell_hbm, cell), (faces_hbm, faces), (waves_hbm, waves), (ham_hbm.at[0], ham))
     copies = [pltpu.make_async_copy(source, target, sems.at[at]) for at, (source, target) in enumerate(pairs)]
     for copy in copies:
         copy.start()
@@ -100,13 +98,12 @@
     columns[...] = turned_rows
     nodes = lax.broadcasted_iota(jnp.int32, (count, count), 1).astype(F32)
     place = one_hot(turned_rows[:count, 0:1] == nodes)
-    pick = one_hot(jnp.concatenate([turned_rows[:padded, 1:2], turned_rows[:padded, 2:3]], axis=0) == row)
-    one[...] = pick
     copies[2].wait()
     begin = tall_dot(lambda first, last: place[first:last], waves[...]).astype(BF16)
     start[...] = begin
-    for copy in copies[3:]:
-        copy.wait()
+    pick = one_hot(jnp.concatenate([turned_rows[:padded, 1:2], turned_rows[:padded, 2:3]], axis=0) == row)
+    one[...] = pick
+    copies[3].wait()
     local[...] = tall_dot(lambda first, last: ham[first:last], begin)
     sums[...] = dot(pick, local[...].astype(BF16)).astype(BF16)
 
@@ -197,7 +194,7 @@
             pltpu.VMEM(connectivity.shape, jnp.int32),
             pltpu.VMEM(face_nodes.shape, jnp.int32),
             pltpu.VMEM((8, lanes), F32),
-            pltpu.SemaphoreType.DMA((3 + len(row_chunks(node_count)),)),
+            pltpu.SemaphoreType.DMA((4,)),
         ],
         compiler_params=params,
     )(*(pltpu.with_memory_space_constraint(x, pltpu.HBM) for x in (wavefunctions, connectivity, face_nodes, hamiltonians)))

time: 35.1 us -> 35 us (level)
  no operation moved by 1% of the time
where the time goes in v9:
time: 35 us; the launch traced here: 34.9 us
  starting transfers between devices  16.5 us (47%)
  waiting for transfers between devices  10.1 us (29%)
  Pallas kernels  4.3 us (12%)
  matrix products  2.27 us (6%)
  other arithmetic  0.87 us (2%)
  between operations  0.77 us (2%)
    ppermute x4, starting transfers between devices, sum_over_cells(): words.append(lax.ppermute(word, ('cells', 'bands'), pairs).astype(F32))  7.33 us
    ppermute x4, waiting for transfers between devices, sum_over_cells(): words.append(lax.ppermute(word, ('cells', 'bands'), pairs).astype(F32))  6.72 us
    ppermute x2, starting transfers between devices, neighbours(): odd_even = lax.ppermute(jnp.where(odd, high, low), both, pair_swap(1))  4.1 us
    ppermute x2, starting transfers between devices, neighbours(): even_odd = lax.ppermute(jnp.where(odd, low, high), both, pair_swap(0))  3.9 us
    dot_general x3, matrix products, dot(): return jnp.dot(a, b, preferred_element_type=F32)  2.27 us
    pallas_call x1, Pallas kernels, body(): pl.pallas_call(first_kernel, out_shape=(shape(nodal, BF16), shape(nodal,...  2.21 us
    ppermute x2, waiting for transfers between devices, neighbours(): even_odd = lax.ppermute(jnp.where(odd, low, high), both, pair_swap(0))  2.02 us
    ppermute x3, starting transfers between devices, body(): lax.ppermute(blocks[at], 'bands', turned(groups, stride, radix, radix - by))  1.16 us
  transfers between devices with their start and end apart: 11, of which 9 were waited for; matrix products, arithmetic and copies ran while one was open for 7% of the time, Pallas kernels for 4%

profile of v9, /device:TPU:0, one launch (start us, length us, event | category | flops | bytes accessed | tf_op | source)
XLA Modules:
  0.0 34.9 jit_solution(6277074604809983788)
XLA Ops:
  0.6 0.0 copy-start
  0.7 2.2 %shard_map.59 = (bf16[729,128]{1,0:T(8,128)(2,1)S(1)}, f32[729,128]{1,0:T(8,128)S(1)}, bf16[192,128]{1,0:T(8,128)(2,1)S(1)}, bf16[729,729]{1,0:T(8,128)(2,1)S(1)...) custom-call(bf16[729,128]{1,0:T(8,128)(2,1)} %waves_hbm.1, s32[1,729]{1,0:T(1,128)} %cell_hbm.1, s32[2,81]{1,0:T(2,128)} %faces.1, ...), custom_call_target="tpu_custom_call" | custom-call | tf_op jit(solution)/shard_map/pallas_call | solution.py:180
  2.9 3.0 %collective-permute-start = (bf16[96,128]{1,0:T(8,128)(2,1)S(1)}, bf16[96,128]{1,0:T(8,128)(2,1)S(1)}, u32[]{:S(2)}, u32[]{:S(2)}) collective-permute-start(bf16[96,128]{1,0:T(8,128)(2,1)S(1)} %get-tuple-element.37), channel_id=1, source_target_pairs={{0,2},{1,3},{2,0},{3,1},{4,8},{5,9},{6,10},{7,11},{8,4},{9,5},{10,... | collective-permute-start | bytes 73736 | tf_op jit(solution)/shard_map/ppermute | solution.py:222
  5.9 1.5 %collective-permute-start.1 = (bf16[96,128]{1,0:T(8,128)(2,1)S(1)}, bf16[96,128]{1,0:T(8,128)(2,1)S(1)}, u32[]{:S(2)}, u32[]{:S(2)}) collective-permute-start(bf16[96,128]{1,0:T(8,128)(2,1)S(1)} %get-tuple-element.36), channel_id=1, source_target_pairs={{0,4},{1,5},{2,6},{3,7},{4,0},{5,1},{6,2},{7,3},{8,12},{9,13},{10,... | collective-permute-start | bytes 73736 | tf_op jit(solution)/shard_map/ppermute | solution.py:221
  7.4 0.0 copy-done
  7.4 1.0 %shard_map.60 = (bf16[729,192]{1,0:T(8,128)(2,1)S(1)}, f32[729,128]{1,0:T(8,128)S(1)}, f32[729,128]{1,0:T(8,128)S(1)}, bf16[729,192]{1,0:T(8,128)(2,1)S(1)}) custom-call(f32[768,8]{1,0:T(8,128)S(1)} %get-tuple-element.17.columns, s32[2,81]{1,0:T(2,128)S(1)} %copy-done, f32[729,128]{1,0:T(8,128)S(1)} %get-tuple-element.18.local, ...), custom_call_target="tpu_custom_call" | custom-call | tf_op jit(solution)/shard_map/pallas_call | solution.py:226
  8.4 0.0 collective-permute-done
  8.5 1.3 %collective-permute-done.1 = bf16[96,128]{1,0:T(8,128)(2,1)S(1)} collective-permute-done((bf16[96,128]{1,0:T(8,128)(2,1)S(1)}, bf16[96,128]{1,0:T(8,128)(2,1)S(1)}, u32[]{:S(2)}, u32[]{:S(2)}) %collective-permute-start.1) | collective-permute-done | bytes 24608 | tf_op jit(solution)/shard_map/ppermute | solution.py:221
  9.8 0.0 copy-start.1
  9.8 0.3 shard_map.61
  10.0 1.1 %collective-permute-start.5 = (bf16[729,128]{1,0:T(8,128)(2,1)S(1)}, bf16[729,128]{1,0:T(8,128)(2,1)S(1)}, u32[]{:S(2)}, u32[]{:S(2)}) collective-permute-start(bf16[729,128]{1,0:T(8,128)(2,1)S(1)} %get-tuple-element.27.rest_0_), channel_id=1, source_target_pairs={{0,2},{1,3},{2,0},{3,1},{4,6},{5,7},{6,4},{7,5},{8,10},{9,11},{10,... | collective-permute-start | bytes 559880 | tf_op jit(solution)/shard_map/ppermute | solution.py:250
  11.1 0.3 shard_map.62
  11.4 1.1 %collective-permute-start.2 = (bf16[96,256]{1,0:T(8,128)(2,1)S(1)}, bf16[96,256]{1,0:T(8,128)(2,1)S(1)}, u32[]{:S(2)}, u32[]{:S(2)}) collective-permute-start(bf16[96,256]{1,0:T(8,128)(2,1)S(1)} %get-tuple-element.33), channel_id=1, source_target_pairs={{0,2},{1,3},{2,0},{3,1},{4,8},{5,9},{6,10},{7,11},{8,4},{9,5},{10,... | collective-permute-start | bytes 147464 | tf_op jit(solution)/shard_map/ppermute | solution.py:222
  12.5 2.4 %collective-permute-start.3 = (bf16[96,256]{1,0:T(8,128)(2,1)S(1)}, bf16[96,256]{1,0:T(8,128)(2,1)S(1)}, u32[]{:S(2)}, u32[]{:S(2)}) collective-permute-start(bf16[96,256]{1,0:T(8,128)(2,1)S(1)} %get-tuple-element.32), channel_id=1, source_target_pairs={{0,4},{1,5},{2,6},{3,7},{4,0},{5,1},{6,2},{7,3},{8,12},{9,13},{10,... | collective-permute-start | bytes 147464 | tf_op jit(solution)/shard_map/ppermute | solution.py:221
  14.9 0.0 copy-done.1
  14.9 0.1 collective-permute-start.4
  15.0 0.7 %collective-permute-done.5.rest_2_ = bf16[729,128]{1,0:T(8,128)(2,1)S(1)} collective-permute-done((bf16[729,128]{1,0:T(8,128)(2,1)S(1)}, bf16[729,128]{1,0:T(8,128)(2,1)S(1)}, u32[]{:S(2)}, u32[]{:S(2)}) %collective-permute-start.5) | collective-permute-done | bytes 186656 | tf_op jit(solution)/shard_map/ppermute | solution.py:250
  15.7 0.0 collective-permute-start.6
  15.7 0.5 %collective-permute-done.2 = bf16[96,256]{1,0:T(8,128)(2,1)S(1)} collective-permute-done((bf16[96,256]{1,0:T(8,128)(2,1)S(1)}, bf16[96,256]{1,0:T(8,128)(2,1)S(1)}, u32[]{:S(2)}, u32[]{:S(2)}) %collective-permute-start.2) | collective-permute-done | bytes 49184 | tf_op jit(solution)/shard_map/ppermute | solution.py:222
  16.2 0.7 %collective-permute-done.3 = bf16[96,256]{1,0:T(8,128)(2,1)S(1)} collective-permute-done((bf16[96,256]{1,0:T(8,128)(2,1)S(1)}, bf16[96,256]{1,0:T(8,128)(2,1)S(1)}, u32[]{:S(2)}, u32[]{:S(2)}) %collective-permute-start.3) | collective-permute-done | bytes 49184 | tf_op jit(solution)/shard_map/ppermute | solution.py:221
  16.9 0.0 collective-permute-done.4.rest_1_
  17.0 0.2 collective-permute-done.6.rest_3_
  17.1 0.6 %shard_map.63 = (f32[729,128]{1,0:T(8,128)S(1)}, bf16[4,128,128]{2,1,0:T(8,128)(2,1)S(1)}) custom-call(f32[729,128]{1,0:T(8,128)S(1)} %get-tuple-element.24.result, bf16[729,128]{1,0:T(8,128)(2,1)S(1)} %get-tuple-element.22.start, f32[729,128]{1,0:T(8,128)S(1)} %get-tuple-element.23.keep, bf16[96,256]{1,0:T(8,128)(2,1)S(1)} %get-tuple-element.31.before, ...), custom_call_target="tpu_custom_call" | custom-call | tf_op jit(solution)/shard_map/pallas_call | solution.py:259
  17.7 2.0 %collective-permute-start.7 = (bf16[4,128,128]{2,1,0:T(8,128)(2,1)S(1)}, bf16[4,128,128]{2,1,0:T(8,128)(2,1)S(1)}, u32[]{:S(2)}, u32[]{:S(2)}) collective-permute-start(bf16[4,128,128]{2,1,0:T(8,128)(2,1)S(1)} %get-tuple-element.29), channel_id=1, source_target_pairs={{0,4},{1,9},{2,6},{3,11},{4,0},{5,13},{6,2},{7,15},{8,12},{9,1},{1... | collective-permute-start | bytes 393224 | tf_op jit(solution)/shard_map/ppermute | solution.py:53
  19.7 1.6 %collective-permute-start.8 = (bf16[4,128,128]{2,1,0:T(8,128)(2,1)S(1)}, bf16[4,128,128]{2,1,0:T(8,128)(2,1)S(1)}, u32[]{:S(2)}, u32[]{:S(2)}) collective-permute-start(bf16[4,128,128]{2,1,0:T(8,128)(2,1)S(1)} %get-tuple-element.29), channel_id=1, source_target_pairs={{0,8},{1,5},{2,10},{3,7},{4,12},{5,1},{6,14},{7,3},{8,0},{9,13},{1... | collective-permute-start | bytes 393224 | tf_op jit(solution)/shard_map/ppermute | solution.py:53
  21.3 0.0 collective-permute-start.9
  21.3 0.5 %fusion.2 = f32[729,128]{1,0:T(8,128)S(1)} fusion(s32[729]{0:T(1024)S(1)} %reduce, f32[729,128]{1,0:T(8,128)S(1)} %get-tuple-element.28), kind=kOutput, calls=%fused_computation.3 | convolution fusion | flops 137233520 | bytes 749412 | tf_op jit(solution)/shard_map/dot_general | solution.py:63
  21.8 0.5 %fusion = f32[729,128]{1,0:T(8,128)S(1)} fusion(s32[729]{0:T(1024)S(1)} %reduce, f32[729,128]{1,0:T(8,128)S(1)} %get-tuple-element.28), kind=kOutput, calls=%fused_computation.1 | convolution fusion | flops 136673648 | bytes 749412 | tf_op jit(solution)/shard_map/dot_general | solution.py:63
  22.3 2.5 %collective-permute-done.7 = bf16[4,128,128]{2,1,0:T(8,128)(2,1)S(1)} collective-permute-done((bf16[4,128,128]{2,1,0:T(8,128)(2,1)S(1)}, bf16[4,128,128]{2,1,0:T(8,128)(2,1)S(1)}, u32[]{:S(2)}, u32[]{:S(2)}) %collective-permute-start.7) | collective-permute-done | bytes 131104 | tf_op jit(solution)/shard_map/ppermute | solution.py:53
  24.8 0.9 %collective-permute-done.8 = bf16[4,128,128]{2,1,0:T(8,128)(2,1)S(1)} collective-permute-done((bf16[4,128,128]{2,1,0:T(8,128)(2,1)S(1)}, bf16[4,128,128]{2,1,0:T(8,128)(2,1)S(1)}, u32[]{:S(2)}, u32[]{:S(2)}) %collective-permute-start.8) | collective-permute-done | bytes 131104 | tf_op jit(solution)/shard_map/ppermute | solution.py:53
  25.6 1.5 %collective-permute-done.9 = bf16[4,128,128]{2,1,0:T(8,128)(2,1)S(1)} collective-permute-done((bf16[4,128,128]{2,1,0:T(8,128)(2,1)S(1)}, bf16[4,128,128]{2,1,0:T(8,128)(2,1)S(1)}, u32[]{:S(2)}, u32[]{:S(2)}) %collective-permute-start.9) | collective-permute-done | bytes 131104 | tf_op jit(solution)/shard_map/ppermute | solution.py:53
  27.1 0.1 add_convert_fusion
  27.2 3.8 %collective-permute-start.10 = (bf16[4,128,128]{2,1,0:T(8,128)(2,1)S(1)}, bf16[4,128,128]{2,1,0:T(8,128)(2,1)S(1)}, u32[]{:S(2)}, u32[]{:S(2)}) collective-permute-start(bf16[4,128,128]{2,1,0:T(8,128)(2,1)S(1)} %add_convert_fusion), channel_id=1, source_target_pairs={{0,24},{1,25},{2,26},{3,27},{4,28},{5,29},{6,30},{7,31},{8,16},{9,... | collective-permute-start | bytes 393224 | tf_op jit(solution)/shard_map/ppermute | solution.py:53
  31.0 1.3 %fusion.4 = f32[729,128]{1,0:T(8,128)} fusion(f32[729,128]{1,0:T(8,128)S(1)} %fusion, f32[729,128]{1,0:T(8,128)S(1)} %fusion.2, s32[729]{0:T(1024)S(1)} %reduce, f32[729,128]{1,0:T(8,128)S(1)} %get-tuple-element.28), kind=kOutput, calls=%fused_computation.5 | convolution fusion | flops 137140208 | bytes 1495908 | tf_op jit(solution)/shard_map/dot_general | solution.py:63
  32.3 1.9 %collective-permute-done.10 = bf16[4,128,128]{2,1,0:T(8,128)(2,1)S(1)} collective-permute-done((bf16[4,128,128]{2,1,0:T(8,128)(2,1)S(1)}, bf16[4,128,128]{2,1,0:T(8,128)(2,1)S(1)}, u32[]{:S(2)}, u32[]{:S(2)}) %collective-permute-start.10) | collective-permute-done | bytes 131104 | tf_op jit(solution)/shard_map/ppermute | solution.py:53
  34.1 0.7 %add_multiply_fusion = f32[4,128,128]{2,1,0:T(8,128)} fusion(bf16[4,128,128]{2,1,0:T(8,128)(2,1)S(1)} %collective-permute-done.10, bf16[4,128,128]{2,1,0:T(8,128)(2,1)S(1)} %add_convert_fusion), kind=kLoop, calls=%fused_computation.11 | loop fusion | flops 262144 | bytes 524288 | tf_op jit(solution)/shard_map/mul | solution.py:266
  (5 shorter events, 0.1 us)
Async XLA Ops:
  0.6 6.8 %copy-start = (s32[2,81]{1,0:T(2,128)S(1)}, s32[2,81]{1,0:T(2,128)}, u32[]{:S(2)}) copy-start(s32[2,81]{1,0:T(2,128)} %faces.1) | copy-start | bytes 1948
  2.9 5.6 %collective-permute-start = (bf16[96,128]{1,0:T(8,128)(2,1)S(1)}, bf16[96,128]{1,0:T(8,128)(2,1)S(1)}, u32[]{:S(2)}, u32[]{:S(2)}) collective-permute-start(bf16[96,128]{1,0:T(8,128)(2,1)S(1)} %get-tuple-element.37), channel_id=1, source_target_pairs={{0,2},{1,3},{2,0},{3,1},{4,8},{5,9},{6,10},{7,11},{8,4},{9,5},{10,... | collective-permute-start | bytes 73736 | tf_op jit(solution)/shard_map/ppermute | solution.py:222
  5.9 3.8 %collective-permute-start.1 = (bf16[96,128]{1,0:T(8,128)(2,1)S(1)}, bf16[96,128]{1,0:T(8,128)(2,1)S(1)}, u32[]{:S(2)}, u32[]{:S(2)}) collective-permute-start(bf16[96,128]{1,0:T(8,128)(2,1)S(1)} %get-tuple-element.36), channel_id=1, source_target_pairs={{0,4},{1,5},{2,6},{3,7},{4,0},{5,1},{6,2},{7,3},{8,12},{9,13},{10,... | collective-permute-start | bytes 73736 | tf_op jit(solution)/shard_map/ppermute | solution.py:221
  9.8 5.1 %copy-start.1 = (s32[1,729]{1,0:T(1,128)S(1)}, s32[1,729]{1,0:T(1,128)}, u32[]{:S(2)}) copy-start(s32[1,729]{1,0:T(1,128)} %cell_hbm.1) | copy-start | bytes 8752
  10.0 5.6 %collective-permute-start.5 = (bf16[729,128]{1,0:T(8,128)(2,1)S(1)}, bf16[729,128]{1,0:T(8,128)(2,1)S(1)}, u32[]{:S(2)}, u32[]{:S(2)}) collective-permute-start(bf16[729,128]{1,0:T(8,128)(2,1)S(1)} %get-tuple-element.27.rest_0_), channel_id=1, source_target_pairs={{0,2},{1,3},{2,0},{3,1},{4,6},{5,7},{6,4},{7,5},{8,10},{9,11},{10,... | collective-permute-start | bytes 559880 | tf_op jit(solution)/shard_map/ppermute | solution.py:250
  11.4 4.8 %collective-permute-start.2 = (bf16[96,256]{1,0:T(8,128)(2,1)S(1)}, bf16[96,256]{1,0:T(8,128)(2,1)S(1)}, u32[]{:S(2)}, u32[]{:S(2)}) collective-permute-start(bf16[96,256]{1,0:T(8,128)(2,1)S(1)} %get-tuple-element.33), channel_id=1, source_target_pairs={{0,2},{1,3},{2,0},{3,1},{4,8},{5,9},{6,10},{7,11},{8,4},{9,5},{10,... | collective-permute-start | bytes 147464 | tf_op jit(solution)/shard_map/ppermute | solution.py:222
  12.5 4.5 %collective-permute-start.3 = (bf16[96,256]{1,0:T(8,128)(2,1)S(1)}, bf16[96,256]{1,0:T(8,128)(2,1)S(1)}, u32[]{:S(2)}, u32[]{:S(2)}) collective-permute-start(bf16[96,256]{1,0:T(8,128)(2,1)S(1)} %get-tuple-element.32), channel_id=1, source_target_pairs={{0,4},{1,5},{2,6},{3,7},{4,0},{5,1},{6,2},{7,3},{8,12},{9,13},{10,... | collective-permute-start | bytes 147464 | tf_op jit(solution)/shard_map/ppermute | solution.py:221
  14.9 2.1 %collective-permute-start.4 = (bf16[729,128]{1,0:T(8,128)(2,1)S(1)}, bf16[729,128]{1,0:T(8,128)(2,1)S(1)}, u32[]{:S(2)}, u32[]{:S(2)}) collective-permute-start(bf16[729,128]{1,0:T(8,128)(2,1)S(1)} %get-tuple-element.27.rest_0_), channel_id=1, source_target_pairs={{0,1},{1,0},{2,3},{3,2},{4,5},{5,4},{6,7},{7,6},{8,9},{9,8},{10,11... | collective-permute-start | bytes 559880 | tf_op jit(solution)/shard_map/ppermute | solution.py:250
  15.7 1.4 %collective-permute-start.6 = (bf16[729,128]{1,0:T(8,128)(2,1)S(1)}, bf16[729,128]{1,0:T(8,128)(2,1)S(1)}, u32[]{:S(2)}, u32[]{:S(2)}) collective-permute-start(bf16[729,128]{1,0:T(8,128)(2,1)S(1)} %collective-permute-done.5.rest_2_), channel_id=1, source_target_pairs={{0,1},{1,0},{2,3},{3,2},{4,5},{5,4},{6,7},{7,6},{8,9},{9,8},{10,11... | collective-permute-start | bytes 559880 | tf_op jit(solution)/shard_map/ppermute | solution.py:250
  17.7 7.1 %collective-permute-start.7 = (bf16[4,128,128]{2,1,0:T(8,128)(2,1)S(1)}, bf16[4,128,128]{2,1,0:T(8,128)(2,1)S(1)}, u32[]{:S(2)}, u32[]{:S(2)}) collective-permute-start(bf16[4,128,128]{2,1,0:T(8,128)(2,1)S(1)} %get-tuple-element.29), channel_id=1, source_target_pairs={{0,4},{1,9},{2,6},{3,11},{4,0},{5,13},{6,2},{7,15},{8,12},{9,1},{1... | collective-permute-start | bytes 393224 | tf_op jit(solution)/shard_map/ppermute | solution.py:53
  19.7 5.9 %collective-permute-start.8 = (bf16[4,128,128]{2,1,0:T(8,128)(2,1)S(1)}, bf16[4,128,128]{2,1,0:T(8,128)(2,1)S(1)}, u32[]{:S(2)}, u32[]{:S(2)}) collective-permute-start(bf16[4,128,128]{2,1,0:T(8,128)(2,1)S(1)} %get-tuple-element.29), channel_id=1, source_target_pairs={{0,8},{1,5},{2,10},{3,7},{4,12},{5,1},{6,14},{7,3},{8,0},{9,13},{1... | collective-permute-start | bytes 393224 | tf_op jit(solution)/shard_map/ppermute | solution.py:53
  21.3 5.9 %collective-permute-start.9 = (bf16[4,128,128]{2,1,0:T(8,128)(2,1)S(1)}, bf16[4,128,128]{2,1,0:T(8,128)(2,1)S(1)}, u32[]{:S(2)}, u32[]{:S(2)}) collective-permute-start(bf16[4,128,128]{2,1,0:T(8,128)(2,1)S(1)} %get-tuple-element.29), channel_id=1, source_target_pairs={{0,12},{1,13},{2,14},{3,15},{4,8},{5,9},{6,10},{7,11},{8,4},{9,5},... | collective-permute-start | bytes 393224 | tf_op jit(solution)/shard_map/ppermute | solution.py:53
  27.2 6.9 %collective-permute-start.10 = (bf16[4,128,128]{2,1,0:T(8,128)(2,1)S(1)}, bf16[4,128,128]{2,1,0:T(8,128)(2,1)S(1)}, u32[]{:S(2)}, u32[]{:S(2)}) collective-permute-start(bf16[4,128,128]{2,1,0:T(8,128)(2,1)S(1)} %add_convert_fusion), channel_id=1, source_target_pairs={{0,24},{1,25},{2,26},{3,27},{4,28},{5,29},{6,30},{7,31},{8,16},{9,... | collective-permute-start | bytes 393224 | tf_op jit(solution)/shard_map/ppermute | solution.py:53

commit v10 on v9

--- a/solution.py
+++ b/solution.py
@@ -200,9 +200,9 @@
     )(*(pltpu.with_memory_space_constraint(x, pltpu.HBM) for x in (wavefunctions, connectivity, face_nodes, hamiltonians)))
 
     both = ("cells", "bands")
-    chip = digits(groups)[-1] if groups > 1 else (1, 1)
-
-    def pair_swap(first):
+    core, chip = (digits(groups)[0], digits(groups)[-1]) if groups > 1 else ((1, 1), (1, 1))
+
+    def pair_swap(first, spare):
         pairs = []
         for part in range(parts):
             other = first + ((part - first) ^ 1)
@@ -210,19 +210,19 @@
                 if part >= first and other < parts:
                     pairs.append((part * groups + band, other * groups + band))
                 else:
-                    pairs.append((part * groups + band, part * groups + turn(band, *chip, 1)))
+                    pairs.append((part * groups + band, part * groups + turn(band, *spare, 1)))
         return pairs
 
     odd = place % 2 == 1
     even = place % 2 == 0
 
-    def neighbours(sums):
+    def neighbours(sums, spare):
         low, high = sums[:padded], sums[padded:]
-        even_odd = lax.ppermute(jnp.where(odd, low, high), both, pair_swap(0))
-        odd_even = lax.ppermute(jnp.where(odd, high, low), both, pair_swap(1))
+        even_odd = lax.ppermute(jnp.where(odd, low, high), both, pair_swap(0, spare))
+        odd_even = lax.ppermute(jnp.where(odd, high, low), both, pair_swap(1, spare))
         return jnp.where(even, odd_even, even_odd), jnp.where(even, even_odd, odd_even)
 
-    before, after = neighbours(sums)
+    before, after = neighbours(sums, core)
     one_t, keep, mine, border = pl.pallas_call(
         middle_kernel,
         out_shape=(
@@ -255,7 +255,7 @@
         out_specs=vmem(1)[0],
         compiler_params=params,
     )(result, start, one)
-    before, after = neighbours(sums)
+    before, after = neighbours(sums, chip)
     filtered, gram = pl.pallas_call(
         third_kernel,
         out_shape=(shape(nodal, F32), shape((groups, width, width), BF16)),

time: 35 us -> 35 us (level)
  starting transfers between devices: 16.5 us -> 17 us
  waiting for transfers between devices: 10.1 us -> 9.65 us
    ppermute x3, starting transfers between devices: 1.16 us -> 1.68 us  [body(): lax.ppermute(blocks[at], 'bands', turned(groups, stride, radix, radix - by))]
    ppermute x3, waiting for transfers between devices: 0.88 us -> 0.48 us  [body(): lax.ppermute(blocks[at], 'bands', turned(groups, stride, radix, radix - by))]
  transfers between devices with their start and end apart: 11 -> 11, of which waited for: 9 -> 8; matrix products, arithmetic and copies ran while one was open for 7% -> 7% of each run, Pallas kernels for 4% -> 4%
where the time goes in v10:
time: 35 us; the launch traced here: 34.8 us
  starting transfers between devices  17 us (49%)
  waiting for transfers between devices  9.65 us (28%)
  Pallas kernels  4.31 us (12%)
  matrix products  2.27 us (6%)
  other arithmetic  0.87 us (2%)
  between operations  0.78 us (2%)
    ppermute x4, starting transfers between devices, sum_over_cells(): words.append(lax.ppermute(word, ('cells', 'bands'), pairs).astype(F32))  7.27 us
    ppermute x2, starting transfers between devices, neighbours(): lax.ppermute(jnp.where(odd, low, high), both, pair_swap(0, spare))  6.92 us
    ppermute x4, waiting for transfers between devices, sum_over_cells(): words.append(lax.ppermute(word, ('cells', 'bands'), pairs).astype(F32))  6.91 us
    dot_general x3, matrix products, dot(): return jnp.dot(a, b, preferred_element_type=F32)  2.27 us
    pallas_call x1, Pallas kernels, body(): pl.pallas_call(first_kernel, out_shape=(shape(nodal, BF16), shape(nodal,...  2.21 us
    ppermute x2, waiting for transfers between devices, neighbours(): lax.ppermute(jnp.where(odd, low, high), both, pair_swap(0, spare))  1.76 us
    ppermute x3, starting transfers between devices, body(): lax.ppermute(blocks[at], 'bands', turned(groups, stride, radix, radix - by))  1.68 us
    ppermute x2, starting transfers between devices, neighbours(): lax.ppermute(jnp.where(odd, high, low), both, pair_swap(1, spare))  1.09 us
  transfers between devices with their start and end apart: 11, of which 8 were waited for; matrix products, arithmetic and copies ran while one was open for 7% of the time, Pallas kernels for 4%

profile of v10, /device:TPU:0, one launch (start us, length us, event | category | flops | bytes accessed | tf_op | source)
XLA Modules:
  0.0 34.8 jit_solution(10299623549713394466)
XLA Ops:
  0.6 0.0 copy-start
  0.7 2.2 %shard_map.59 = (bf16[729,128]{1,0:T(8,128)(2,1)S(1)}, f32[729,128]{1,0:T(8,128)S(1)}, bf16[192,128]{1,0:T(8,128)(2,1)S(1)}, bf16[729,729]{1,0:T(8,128)(2,1)S(1)...) custom-call(bf16[729,128]{1,0:T(8,128)(2,1)} %waves_hbm.1, s32[1,729]{1,0:T(1,128)} %cell_hbm.1, s32[2,81]{1,0:T(2,128)} %faces.1, ...), custom_call_target="tpu_custom_call" | custom-call | tf_op jit(solution)/shard_map/pallas_call | solution.py:180
  2.9 0.5 %collective-permute-start = (bf16[96,128]{1,0:T(8,128)(2,1)S(1)}, bf16[96,128]{1,0:T(8,128)(2,1)S(1)}, u32[]{:S(2)}, u32[]{:S(2)}) collective-permute-start(bf16[96,128]{1,0:T(8,128)(2,1)S(1)} %get-tuple-element.37), channel_id=1, source_target_pairs={{0,1},{1,0},{2,3},{3,2},{4,8},{5,9},{6,10},{7,11},{8,4},{9,5},{10,... | collective-permute-start | bytes 73736 | tf_op jit(solution)/shard_map/ppermute | solution.py:222
  3.4 4.0 %collective-permute-start.1 = (bf16[96,128]{1,0:T(8,128)(2,1)S(1)}, bf16[96,128]{1,0:T(8,128)(2,1)S(1)}, u32[]{:S(2)}, u32[]{:S(2)}) collective-permute-start(bf16[96,128]{1,0:T(8,128)(2,1)S(1)} %get-tuple-element.36), channel_id=1, source_target_pairs={{0,4},{1,5},{2,6},{3,7},{4,0},{5,1},{6,2},{7,3},{8,12},{9,13},{10,... | collective-permute-start | bytes 73736 | tf_op jit(solution)/shard_map/ppermute | solution.py:221
  7.4 0.0 copy-done
  7.4 1.0 %shard_map.60 = (bf16[729,192]{1,0:T(8,128)(2,1)S(1)}, f32[729,128]{1,0:T(8,128)S(1)}, f32[729,128]{1,0:T(8,128)S(1)}, bf16[729,192]{1,0:T(8,128)(2,1)S(1)}) custom-call(f32[768,8]{1,0:T(8,128)S(1)} %get-tuple-element.17.columns, s32[2,81]{1,0:T(2,128)S(1)} %copy-done, f32[729,128]{1,0:T(8,128)S(1)} %get-tuple-element.18.local, ...), custom_call_target="tpu_custom_call" | custom-call | tf_op jit(solution)/shard_map/pallas_call | solution.py:226
  8.4 0.0 collective-permute-done
  8.5 0.8 %collective-permute-done.1 = bf16[96,128]{1,0:T(8,128)(2,1)S(1)} collective-permute-done((bf16[96,128]{1,0:T(8,128)(2,1)S(1)}, bf16[96,128]{1,0:T(8,128)(2,1)S(1)}, u32[]{:S(2)}, u32[]{:S(2)}) %collective-permute-start.1) | collective-permute-done | bytes 24608 | tf_op jit(solution)/shard_map/ppermute | solution.py:221
  9.3 0.0 copy-start.1
  9.3 0.3 shard_map.61
  9.5 1.6 %collective-permute-start.5 = (bf16[729,128]{1,0:T(8,128)(2,1)S(1)}, bf16[729,128]{1,0:T(8,128)(2,1)S(1)}, u32[]{:S(2)}, u32[]{:S(2)}) collective-permute-start(bf16[729,128]{1,0:T(8,128)(2,1)S(1)} %get-tuple-element.27.rest_0_), channel_id=1, source_target_pairs={{0,2},{1,3},{2,0},{3,1},{4,6},{5,7},{6,4},{7,5},{8,10},{9,11},{10,... | collective-permute-start | bytes 559880 | tf_op jit(solution)/shard_map/ppermute | solution.py:250
  11.1 0.3 shard_map.62
  11.4 0.6 %collective-permute-start.2 = (bf16[96,256]{1,0:T(8,128)(2,1)S(1)}, bf16[96,256]{1,0:T(8,128)(2,1)S(1)}, u32[]{:S(2)}, u32[]{:S(2)}) collective-permute-start(bf16[96,256]{1,0:T(8,128)(2,1)S(1)} %get-tuple-element.33), channel_id=1, source_target_pairs={{0,2},{1,3},{2,0},{3,1},{4,8},{5,9},{6,10},{7,11},{8,4},{9,5},{10,... | collective-permute-start | bytes 147464 | tf_op jit(solution)/shard_map/ppermute | solution.py:222
  12.0 2.9 %collective-permute-start.3 = (bf16[96,256]{1,0:T(8,128)(2,1)S(1)}, bf16[96,256]{1,0:T(8,128)(2,1)S(1)}, u32[]{:S(2)}, u32[]{:S(2)}) collective-permute-start(bf16[96,256]{1,0:T(8,128)(2,1)S(1)} %get-tuple-element.32), channel_id=1, source_target_pairs={{0,4},{1,5},{2,6},{3,7},{4,0},{5,1},{6,2},{7,3},{8,12},{9,13},{10,... | collective-permute-start | bytes 147464 | tf_op jit(solution)/shard_map/ppermute | solution.py:221
  14.9 0.0 copy-done.1
  14.9 0.1 collective-permute-start.4
  15.0 0.5 %collective-permute-done.5.rest_2_ = bf16[729,128]{1,0:T(8,128)(2,1)S(1)} collective-permute-done((bf16[729,128]{1,0:T(8,128)(2,1)S(1)}, bf16[729,128]{1,0:T(8,128)(2,1)S(1)}, u32[]{:S(2)}, u32[]{:S(2)}) %collective-permute-start.5) | collective-permute-done | bytes 186656 | tf_op jit(solution)/shard_map/ppermute | solution.py:250
  15.4 0.0 collective-permute-start.6
  15.5 0.5 %collective-permute-done.2 = bf16[96,256]{1,0:T(8,128)(2,1)S(1)} collective-permute-done((bf16[96,256]{1,0:T(8,128)(2,1)S(1)}, bf16[96,256]{1,0:T(8,128)(2,1)S(1)}, u32[]{:S(2)}, u32[]{:S(2)}) %collective-permute-start.2) | collective-permute-done | bytes 49184 | tf_op jit(solution)/shard_map/ppermute | solution.py:222
  16.0 1.0 %collective-permute-done.3 = bf16[96,256]{1,0:T(8,128)(2,1)S(1)} collective-permute-done((bf16[96,256]{1,0:T(8,128)(2,1)S(1)}, bf16[96,256]{1,0:T(8,128)(2,1)S(1)}, u32[]{:S(2)}, u32[]{:S(2)}) %collective-permute-start.3) | collective-permute-done | bytes 49184 | tf_op jit(solution)/shard_map/ppermute | solution.py:221
  16.9 0.0 collective-permute-done.4.rest_1_
  17.0 0.0 collective-permute-done.6.rest_3_
  17.0 0.6 %shard_map.63 = (f32[729,128]{1,0:T(8,128)S(1)}, bf16[4,128,128]{2,1,0:T(8,128)(2,1)S(1)}) custom-call(f32[729,128]{1,0:T(8,128)S(1)} %get-tuple-element.24.result, bf16[729,128]{1,0:T(8,128)(2,1)S(1)} %get-tuple-element.22.start, f32[729,128]{1,0:T(8,128)S(1)} %get-tuple-element.23.keep, bf16[96,256]{1,0:T(8,128)(2,1)S(1)} %get-tuple-element.31.before, ...), custom_call_target="tpu_custom_call" | custom-call | tf_op jit(solution)/shard_map/pallas_call | solution.py:259
  17.6 2.1 %collective-permute-start.7 = (bf16[4,128,128]{2,1,0:T(8,128)(2,1)S(1)}, bf16[4,128,128]{2,1,0:T(8,128)(2,1)S(1)}, u32[]{:S(2)}, u32[]{:S(2)}) collective-permute-start(bf16[4,128,128]{2,1,0:T(8,128)(2,1)S(1)} %get-tuple-element.29), channel_id=1, source_target_pairs={{0,4},{1,9},{2,6},{3,11},{4,0},{5,13},{6,2},{7,15},{8,12},{9,1},{1... | collective-permute-start | bytes 393224 | tf_op jit(solution)/shard_map/ppermute | solution.py:53
  19.7 1.6 %collective-permute-start.8 = (bf16[4,128,128]{2,1,0:T(8,128)(2,1)S(1)}, bf16[4,128,128]{2,1,0:T(8,128)(2,1)S(1)}, u32[]{:S(2)}, u32[]{:S(2)}) collective-permute-start(bf16[4,128,128]{2,1,0:T(8,128)(2,1)S(1)} %get-tuple-element.29), channel_id=1, source_target_pairs={{0,8},{1,5},{2,10},{3,7},{4,12},{5,1},{6,14},{7,3},{8,0},{9,13},{1... | collective-permute-start | bytes 393224 | tf_op jit(solution)/shard_map/ppermute | solution.py:53
  21.3 0.0 collective-permute-start.9
  21.3 0.5 %fusion.2 = f32[729,128]{1,0:T(8,128)S(1)} fusion(s32[729]{0:T(1024)S(1)} %reduce, f32[729,128]{1,0:T(8,128)S(1)} %get-tuple-element.28), kind=kOutput, calls=%fused_computation.3 | convolution fusion | flops 137233520 | bytes 749412 | tf_op jit(solution)/shard_map/dot_general | solution.py:63
  21.8 0.5 %fusion = f32[729,128]{1,0:T(8,128)S(1)} fusion(s32[729]{0:T(1024)S(1)} %reduce, f32[729,128]{1,0:T(8,128)S(1)} %get-tuple-element.28), kind=kOutput, calls=%fused_computation.1 | convolution fusion | flops 136673648 | bytes 749412 | tf_op jit(solution)/shard_map/dot_general | solution.py:63
  22.3 2.5 %collective-permute-done.7 = bf16[4,128,128]{2,1,0:T(8,128)(2,1)S(1)} collective-permute-done((bf16[4,128,128]{2,1,0:T(8,128)(2,1)S(1)}, bf16[4,128,128]{2,1,0:T(8,128)(2,1)S(1)}, u32[]{:S(2)}, u32[]{:S(2)}) %collective-permute-start.7) | collective-permute-done | bytes 131104 | tf_op jit(solution)/shard_map/ppermute | solution.py:53
  24.8 0.9 %collective-permute-done.8 = bf16[4,128,128]{2,1,0:T(8,128)(2,1)S(1)} collective-permute-done((bf16[4,128,128]{2,1,0:T(8,128)(2,1)S(1)}, bf16[4,128,128]{2,1,0:T(8,128)(2,1)S(1)}, u32[]{:S(2)}, u32[]{:S(2)}) %collective-permute-start.8) | collective-permute-done | bytes 131104 | tf_op jit(solution)/shard_map/ppermute | solution.py:53
  25.6 1.5 %collective-permute-done.9 = bf16[4,128,128]{2,1,0:T(8,128)(2,1)S(1)} collective-permute-done((bf16[4,128,128]{2,1,0:T(8,128)(2,1)S(1)}, bf16[4,128,128]{2,1,0:T(8,128)(2,1)S(1)}, u32[]{:S(2)}, u32[]{:S(2)}) %collective-permute-start.9) | collective-permute-done | bytes 131104 | tf_op jit(solution)/shard_map/ppermute | solution.py:53
  27.1 0.1 add_convert_fusion
  27.2 3.6 %collective-permute-start.10 = (bf16[4,128,128]{2,1,0:T(8,128)(2,1)S(1)}, bf16[4,128,128]{2,1,0:T(8,128)(2,1)S(1)}, u32[]{:S(2)}, u32[]{:S(2)}) collective-permute-start(bf16[4,128,128]{2,1,0:T(8,128)(2,1)S(1)} %add_convert_fusion), channel_id=1, source_target_pairs={{0,24},{1,25},{2,26},{3,27},{4,28},{5,29},{6,30},{7,31},{8,16},{9,... | collective-permute-start | bytes 393224 | tf_op jit(solution)/shard_map/ppermute | solution.py:53
  30.8 1.3 %fusion.4 = f32[729,128]{1,0:T(8,128)} fusion(f32[729,128]{1,0:T(8,128)S(1)} %fusion, f32[729,128]{1,0:T(8,128)S(1)} %fusion.2, s32[729]{0:T(1024)S(1)} %reduce, f32[729,128]{1,0:T(8,128)S(1)} %get-tuple-element.28), kind=kOutput, calls=%fused_computation.5 | convolution fusion | flops 137140208 | bytes 1495908 | tf_op jit(solution)/shard_map/dot_general | solution.py:63
  32.1 2.0 %collective-permute-done.10 = bf16[4,128,128]{2,1,0:T(8,128)(2,1)S(1)} collective-permute-done((bf16[4,128,128]{2,1,0:T(8,128)(2,1)S(1)}, bf16[4,128,128]{2,1,0:T(8,128)(2,1)S(1)}, u32[]{:S(2)}, u32[]{:S(2)}) %collective-permute-start.10) | collective-permute-done | bytes 131104 | tf_op jit(solution)/shard_map/ppermute | solution.py:53
  34.1 0.7 %add_multiply_fusion = f32[4,128,128]{2,1,0:T(8,128)} fusion(bf16[4,128,128]{2,1,0:T(8,128)(2,1)S(1)} %collective-permute-done.10, bf16[4,128,128]{2,1,0:T(8,128)(2,1)S(1)} %add_convert_fusion), kind=kLoop, calls=%fused_computation.11 | loop fusion | flops 262144 | bytes 524288 | tf_op jit(solution)/shard_map/mul | solution.py:266
  (5 shorter events, 0.1 us)
Async XLA Ops:
  0.6 6.8 %copy-start = (s32[2,81]{1,0:T(2,128)S(1)}, s32[2,81]{1,0:T(2,128)}, u32[]{:S(2)}) copy-start(s32[2,81]{1,0:T(2,128)} %faces.1) | copy-start | bytes 1948
  2.9 5.6 %collective-permute-start = (bf16[96,128]{1,0:T(8,128)(2,1)S(1)}, bf16[96,128]{1,0:T(8,128)(2,1)S(1)}, u32[]{:S(2)}, u32[]{:S(2)}) collective-permute-start(bf16[96,128]{1,0:T(8,128)(2,1)S(1)} %get-tuple-element.37), channel_id=1, source_target_pairs={{0,1},{1,0},{2,3},{3,2},{4,8},{5,9},{6,10},{7,11},{8,4},{9,5},{10,... | collective-permute-start | bytes 73736 | tf_op jit(solution)/shard_map/ppermute | solution.py:222
  3.4 5.8 %collective-permute-start.1 = (bf16[96,128]{1,0:T(8,128)(2,1)S(1)}, bf16[96,128]{1,0:T(8,128)(2,1)S(1)}, u32[]{:S(2)}, u32[]{:S(2)}) collective-permute-start(bf16[96,128]{1,0:T(8,128)(2,1)S(1)} %get-tuple-element.36), channel_id=1, source_target_pairs={{0,4},{1,5},{2,6},{3,7},{4,0},{5,1},{6,2},{7,3},{8,12},{9,13},{10,... | collective-permute-start | bytes 73736 | tf_op jit(solution)/shard_map/ppermute | solution.py:221
  9.3 5.6 %copy-start.1 = (s32[1,729]{1,0:T(1,128)S(1)}, s32[1,729]{1,0:T(1,128)}, u32[]{:S(2)}) copy-start(s32[1,729]{1,0:T(1,128)} %cell_hbm.1) | copy-start | bytes 8752
  9.5 5.9 %collective-permute-start.5 = (bf16[729,128]{1,0:T(8,128)(2,1)S(1)}, bf16[729,128]{1,0:T(8,128)(2,1)S(1)}, u32[]{:S(2)}, u32[]{:S(2)}) collective-permute-start(bf16[729,128]{1,0:T(8,128)(2,1)S(1)} %get-tuple-element.27.rest_0_), channel_id=1, source_target_pairs={{0,2},{1,3},{2,0},{3,1},{4,6},{5,7},{6,4},{7,5},{8,10},{9,11},{10,... | collective-permute-start | bytes 559880 | tf_op jit(solution)/shard_map/ppermute | solution.py:250
  11.4 4.6 %collective-permute-start.2 = (bf16[96,256]{1,0:T(8,128)(2,1)S(1)}, bf16[96,256]{1,0:T(8,128)(2,1)S(1)}, u32[]{:S(2)}, u32[]{:S(2)}) collective-permute-start(bf16[96,256]{1,0:T(8,128)(2,1)S(1)} %get-tuple-element.33), channel_id=1, source_target_pairs={{0,2},{1,3},{2,0},{3,1},{4,8},{5,9},{6,10},{7,11},{8,4},{9,5},{10,... | collective-permute-start | bytes 147464 | tf_op jit(solution)/shard_map/ppermute | solution.py:222
  12.0 5.0 %collective-permute-start.3 = (bf16[96,256]{1,0:T(8,128)(2,1)S(1)}, bf16[96,256]{1,0:T(8,128)(2,1)S(1)}, u32[]{:S(2)}, u32[]{:S(2)}) collective-permute-start(bf16[96,256]{1,0:T(8,128)(2,1)S(1)} %get-tuple-element.32), channel_id=1, source_target_pairs={{0,4},{1,5},{2,6},{3,7},{4,0},{5,1},{6,2},{7,3},{8,12},{9,13},{10,... | collective-permute-start | bytes 147464 | tf_op jit(solution)/shard_map/ppermute | solution.py:221
  14.9 2.1 %collective-permute-start.4 = (bf16[729,128]{1,0:T(8,128)(2,1)S(1)}, bf16[729,128]{1,0:T(8,128)(2,1)S(1)}, u32[]{:S(2)}, u32[]{:S(2)}) collective-permute-start(bf16[729,128]{1,0:T(8,128)(2,1)S(1)} %get-tuple-element.27.rest_0_), channel_id=1, source_target_pairs={{0,1},{1,0},{2,3},{3,2},{4,5},{5,4},{6,7},{7,6},{8,9},{9,8},{10,11... | collective-permute-start | bytes 559880 | tf_op jit(solution)/shard_map/ppermute | solution.py:250
  15.4 1.5 %collective-permute-start.6 = (bf16[729,128]{1,0:T(8,128)(2,1)S(1)}, bf16[729,128]{1,0:T(8,128)(2,1)S(1)}, u32[]{:S(2)}, u32[]{:S(2)}) collective-permute-start(bf16[729,128]{1,0:T(8,128)(2,1)S(1)} %collective-permute-done.5.rest_2_), channel_id=1, source_target_pairs={{0,1},{1,0},{2,3},{3,2},{4,5},{5,4},{6,7},{7,6},{8,9},{9,8},{10,11... | collective-permute-start | bytes 559880 | tf_op jit(solution)/shard_map/ppermute | solution.py:250
  17.6 7.2 %collective-permute-start.7 = (bf16[4,128,128]{2,1,0:T(8,128)(2,1)S(1)}, bf16[4,128,128]{2,1,0:T(8,128)(2,1)S(1)}, u32[]{:S(2)}, u32[]{:S(2)}) collective-permute-start(bf16[4,128,128]{2,1,0:T(8,128)(2,1)S(1)} %get-tuple-element.29), channel_id=1, source_target_pairs={{0,4},{1,9},{2,6},{3,11},{4,0},{5,13},{6,2},{7,15},{8,12},{9,1},{1... | collective-permute-start | bytes 393224 | tf_op jit(solution)/shard_map/ppermute | solution.py:53
  19.7 5.9 %collective-permute-start.8 = (bf16[4,128,128]{2,1,0:T(8,128)(2,1)S(1)}, bf16[4,128,128]{2,1,0:T(8,128)(2,1)S(1)}, u32[]{:S(2)}, u32[]{:S(2)}) collective-permute-start(bf16[4,128,128]{2,1,0:T(8,128)(2,1)S(1)} %get-tuple-element.29), channel_id=1, source_target_pairs={{0,8},{1,5},{2,10},{3,7},{4,12},{5,1},{6,14},{7,3},{8,0},{9,13},{1... | collective-permute-start | bytes 393224 | tf_op jit(solution)/shard_map/ppermute | solution.py:53
  21.3 5.9 %collective-permute-start.9 = (bf16[4,128,128]{2,1,0:T(8,128)(2,1)S(1)}, bf16[4,128,128]{2,1,0:T(8,128)(2,1)S(1)}, u32[]{:S(2)}, u32[]{:S(2)}) collective-permute-start(bf16[4,128,128]{2,1,0:T(8,128)(2,1)S(1)} %get-tuple-element.29), channel_id=1, source_target_pairs={{0,12},{1,13},{2,14},{3,15},{4,8},{5,9},{6,10},{7,11},{8,4},{9,5},... | collective-permute-start | bytes 393224 | tf_op jit(solution)/shard_map/ppermute | solution.py:53
  27.2 6.9 %collective-permute-start.10 = (bf16[4,128,128]{2,1,0:T(8,128)(2,1)S(1)}, bf16[4,128,128]{2,1,0:T(8,128)(2,1)S(1)}, u32[]{:S(2)}, u32[]{:S(2)}) collective-permute-start(bf16[4,128,128]{2,1,0:T(8,128)(2,1)S(1)} %add_convert_fusion), channel_id=1, source_target_pairs={{0,24},{1,25},{2,26},{3,27},{4,28},{5,29},{6,30},{7,31},{8,16},{9,... | collective-permute-start | bytes 393224 | tf_op jit(solution)/shard_map/ppermute | solution.py:53

commit v11 on v9

--- a/solution.py
+++ b/solution.py
@@ -152,13 +152,13 @@
     whole = result[...] + halo[:, :width]
     filtered[...] = whole - older
     right = (whole - older * keep[...] - halo[:, width:]).astype(BF16)
-    product = dot_t(right, jnp.concatenate([block[...] for block in blocks], axis=1))
+    left = [jnp.transpose(block[...].astype(F32)).astype(BF16) for block in blocks]
     group = lax.axis_index("bands")
     for at in range(len(blocks)):
         target = 0
         for stride, radix in digits(len(blocks)):
             target = target + (group // stride + at // stride) % radix * stride
-        gram[target] = jnp.transpose(product[:, at * width : (at + 1) * width]).astype(BF16)
+        gram[target] = dot(left[at], right).astype(BF16)
 
 
 def vmem(count):

time: 35 us -> 35 us (level)
  no operation moved by 1% of the time
where the time goes in v11:
time: 35 us; the launch traced here: 34.8 us
  starting transfers between devices  16.5 us (47%)
  waiting for transfers between devices  10.1 us (29%)
  Pallas kernels  4.31 us (12%)
  matrix products  2.28 us (7%)
  other arithmetic  0.87 us (2%)
  between operations  0.76 us (2%)
    ppermute x4, starting transfers between devices, sum_over_cells(): words.append(lax.ppermute(word, ('cells', 'bands'), pairs).astype(F32))  7.33 us
    ppermute x4, waiting for transfers between devices, sum_over_cells(): words.append(lax.ppermute(word, ('cells', 'bands'), pairs).astype(F32))  6.7 us
    ppermute x2, starting transfers between devices, neighbours(): odd_even = lax.ppermute(jnp.where(odd, high, low), both, pair_swap(1))  4.1 us
    ppermute x2, starting transfers between devices, neighbours(): even_odd = lax.ppermute(jnp.where(odd, low, high), both, pair_swap(0))  3.9 us
    dot_general x3, matrix products, dot(): return jnp.dot(a, b, preferred_element_type=F32)  2.28 us
    pallas_call x1, Pallas kernels, body(): pl.pallas_call(first_kernel, out_shape=(shape(nodal, BF16), shape(nodal,...  2.21 us
    ppermute x2, waiting for transfers between devices, neighbours(): even_odd = lax.ppermute(jnp.where(odd, low, high), both, pair_swap(0))  2.02 us
    ppermute x3, starting transfers between devices, body(): lax.ppermute(blocks[at], 'bands', turned(groups, stride, radix, radix - by))  1.16 us
  transfers between devices with their start and end apart: 11, of which 9 were waited for; matrix products, arithmetic and copies ran while one was open for 7% of the time, Pallas kernels for 4%

profile of v11, /device:TPU:0, one launch (start us, length us, event | category | flops | bytes accessed | tf_op | source)
XLA Modules:
  0.0 34.8 jit_solution(10915534350743142277)
XLA Ops:
  0.6 0.0 copy-start
  0.7 2.2 %shard_map.59 = (bf16[729,128]{1,0:T(8,128)(2,1)S(1)}, f32[729,128]{1,0:T(8,128)S(1)}, bf16[192,128]{1,0:T(8,128)(2,1)S(1)}, bf16[729,729]{1,0:T(8,128)(2,1)S(1)...) custom-call(bf16[729,128]{1,0:T(8,128)(2,1)} %waves_hbm.1, s32[1,729]{1,0:T(1,128)} %cell_hbm.1, s32[2,81]{1,0:T(2,128)} %faces.1, ...), custom_call_target="tpu_custom_call" | custom-call | tf_op jit(solution)/shard_map/pallas_call | solution.py:180
  2.9 3.0 %collective-permute-start = (bf16[96,128]{1,0:T(8,128)(2,1)S(1)}, bf16[96,128]{1,0:T(8,128)(2,1)S(1)}, u32[]{:S(2)}, u32[]{:S(2)}) collective-permute-start(bf16[96,128]{1,0:T(8,128)(2,1)S(1)} %get-tuple-element.37), channel_id=1, source_target_pairs={{0,2},{1,3},{2,0},{3,1},{4,8},{5,9},{6,10},{7,11},{8,4},{9,5},{10,... | collective-permute-start | bytes 73736 | tf_op jit(solution)/shard_map/ppermute | solution.py:222
  5.9 1.5 %collective-permute-start.1 = (bf16[96,128]{1,0:T(8,128)(2,1)S(1)}, bf16[96,128]{1,0:T(8,128)(2,1)S(1)}, u32[]{:S(2)}, u32[]{:S(2)}) collective-permute-start(bf16[96,128]{1,0:T(8,128)(2,1)S(1)} %get-tuple-element.36), channel_id=1, source_target_pairs={{0,4},{1,5},{2,6},{3,7},{4,0},{5,1},{6,2},{7,3},{8,12},{9,13},{10,... | collective-permute-start | bytes 73736 | tf_op jit(solution)/shard_map/ppermute | solution.py:221
  7.4 0.0 copy-done
  7.4 1.0 %shard_map.60 = (bf16[729,192]{1,0:T(8,128)(2,1)S(1)}, f32[729,128]{1,0:T(8,128)S(1)}, f32[729,128]{1,0:T(8,128)S(1)}, bf16[729,192]{1,0:T(8,128)(2,1)S(1)}) custom-call(f32[768,8]{1,0:T(8,128)S(1)} %get-tuple-element.17.columns, s32[2,81]{1,0:T(2,128)S(1)} %copy-done, f32[729,128]{1,0:T(8,128)S(1)} %get-tuple-element.18.local, ...), custom_call_target="tpu_custom_call" | custom-call | tf_op jit(solution)/shard_map/pallas_call | solution.py:226
  8.4 0.0 collective-permute-done
  8.5 1.3 %collective-permute-done.1 = bf16[96,128]{1,0:T(8,128)(2,1)S(1)} collective-permute-done((bf16[96,128]{1,0:T(8,128)(2,1)S(1)}, bf16[96,128]{1,0:T(8,128)(2,1)S(1)}, u32[]{:S(2)}, u32[]{:S(2)}) %collective-permute-start.1) | collective-permute-done | bytes 24608 | tf_op jit(solution)/shard_map/ppermute | solution.py:221
  9.8 0.0 copy-start.1
  9.8 0.3 shard_map.61
  10.0 1.1 %collective-permute-start.5 = (bf16[729,128]{1,0:T(8,128)(2,1)S(1)}, bf16[729,128]{1,0:T(8,128)(2,1)S(1)}, u32[]{:S(2)}, u32[]{:S(2)}) collective-permute-start(bf16[729,128]{1,0:T(8,128)(2,1)S(1)} %get-tuple-element.27.rest_0_), channel_id=1, source_target_pairs={{0,2},{1,3},{2,0},{3,1},{4,6},{5,7},{6,4},{7,5},{8,10},{9,11},{10,... | collective-permute-start | bytes 559880 | tf_op jit(solution)/shard_map/ppermute | solution.py:250
  11.1 0.3 shard_map.62
  11.4 1.1 %collective-permute-start.2 = (bf16[96,256]{1,0:T(8,128)(2,1)S(1)}, bf16[96,256]{1,0:T(8,128)(2,1)S(1)}, u32[]{:S(2)}, u32[]{:S(2)}) collective-permute-start(bf16[96,256]{1,0:T(8,128)(2,1)S(1)} %get-tuple-element.33), channel_id=1, source_target_pairs={{0,2},{1,3},{2,0},{3,1},{4,8},{5,9},{6,10},{7,11},{8,4},{9,5},{10,... | collective-permute-start | bytes 147464 | tf_op jit(solution)/shard_map/ppermute | solution.py:222
  12.5 2.4 %collective-permute-start.3 = (bf16[96,256]{1,0:T(8,128)(2,1)S(1)}, bf16[96,256]{1,0:T(8,128)(2,1)S(1)}, u32[]{:S(2)}, u32[]{:S(2)}) collective-permute-start(bf16[96,256]{1,0:T(8,128)(2,1)S(1)} %get-tuple-element.32), channel_id=1, source_target_pairs={{0,4},{1,5},{2,6},{3,7},{4,0},{5,1},{6,2},{7,3},{8,12},{9,13},{10,... | collective-permute-start | bytes 147464 | tf_op jit(solution)/shard_map/ppermute | solution.py:221
  14.9 0.0 copy-done.1
  14.9 0.1 collective-permute-start.4
  15.0 0.7 %collective-permute-done.5.rest_2_ = bf16[729,128]{1,0:T(8,128)(2,1)S(1)} collective-permute-done((bf16[729,128]{1,0:T(8,128)(2,1)S(1)}, bf16[729,128]{1,0:T(8,128)(2,1)S(1)}, u32[]{:S(2)}, u32[]{:S(2)}) %collective-permute-start.5) | collective-permute-done | bytes 186656 | tf_op jit(solution)/shard_map/ppermute | solution.py:250
  15.7 0.0 collective-permute-start.6
  15.7 0.5 %collective-permute-done.2 = bf16[96,256]{1,0:T(8,128)(2,1)S(1)} collective-permute-done((bf16[96,256]{1,0:T(8,128)(2,1)S(1)}, bf16[96,256]{1,0:T(8,128)(2,1)S(1)}, u32[]{:S(2)}, u32[]{:S(2)}) %collective-permute-start.2) | collective-permute-done | bytes 49184 | tf_op jit(solution)/shard_map/ppermute | solution.py:222
  16.2 0.7 %collective-permute-done.3 = bf16[96,256]{1,0:T(8,128)(2,1)S(1)} collective-permute-done((bf16[96,256]{1,0:T(8,128)(2,1)S(1)}, bf16[96,256]{1,0:T(8,128)(2,1)S(1)}, u32[]{:S(2)}, u32[]{:S(2)}) %collective-permute-start.3) | collective-permute-done | bytes 49184 | tf_op jit(solution)/shard_map/ppermute | solution.py:221
  16.9 0.0 collective-permute-done.4.rest_1_
  17.0 0.2 collective-permute-done.6.rest_3_
  17.1 0.6 %shard_map.63 = (f32[729,128]{1,0:T(8,128)S(1)}, bf16[4,128,128]{2,1,0:T(8,128)(2,1)S(1)}) custom-call(f32[729,128]{1,0:T(8,128)S(1)} %get-tuple-element.24.result, bf16[729,128]{1,0:T(8,128)(2,1)S(1)} %get-tuple-element.22.start, f32[729,128]{1,0:T(8,128)S(1)} %get-tuple-element.23.keep, bf16[96,256]{1,0:T(8,128)(2,1)S(1)} %get-tuple-element.31.before, ...), custom_call_target="tpu_custom_call" | custom-call | tf_op jit(solution)/shard_map/pallas_call | solution.py:259
  17.7 2.0 %collective-permute-start.7 = (bf16[4,128,128]{2,1,0:T(8,128)(2,1)S(1)}, bf16[4,128,128]{2,1,0:T(8,128)(2,1)S(1)}, u32[]{:S(2)}, u32[]{:S(2)}) collective-permute-start(bf16[4,128,128]{2,1,0:T(8,128)(2,1)S(1)} %get-tuple-element.29), channel_id=1, source_target_pairs={{0,4},{1,9},{2,6},{3,11},{4,0},{5,13},{6,2},{7,15},{8,12},{9,1},{1... | collective-permute-start | bytes 393224 | tf_op jit(solution)/shard_map/ppermute | solution.py:53
  19.7 1.6 %collective-permute-start.8 = (bf16[4,128,128]{2,1,0:T(8,128)(2,1)S(1)}, bf16[4,128,128]{2,1,0:T(8,128)(2,1)S(1)}, u32[]{:S(2)}, u32[]{:S(2)}) collective-permute-start(bf16[4,128,128]{2,1,0:T(8,128)(2,1)S(1)} %get-tuple-element.29), channel_id=1, source_target_pairs={{0,8},{1,5},{2,10},{3,7},{4,12},{5,1},{6,14},{7,3},{8,0},{9,13},{1... | collective-permute-start | bytes 393224 | tf_op jit(solution)/shard_map/ppermute | solution.py:53
  21.3 0.0 collective-permute-start.9
  21.3 0.5 %fusion.2 = f32[729,128]{1,0:T(8,128)S(1)} fusion(s32[729]{0:T(1024)S(1)} %reduce, f32[729,128]{1,0:T(8,128)S(1)} %get-tuple-element.28), kind=kOutput, calls=%fused_computation.3 | convolution fusion | flops 137233520 | bytes 749412 | tf_op jit(solution)/shard_map/dot_general | solution.py:63
  21.8 0.5 %fusion = f32[729,128]{1,0:T(8,128)S(1)} fusion(s32[729]{0:T(1024)S(1)} %reduce, f32[729,128]{1,0:T(8,128)S(1)} %get-tuple-element.28), kind=kOutput, calls=%fused_computation.1 | convolution fusion | flops 136673648 | bytes 749412 | tf_op jit(solution)/shard_map/dot_general | solution.py:63
  22.3 2.5 %collective-permute-done.7 = bf16[4,128,128]{2,1,0:T(8,128)(2,1)S(1)} collective-permute-done((bf16[4,128,128]{2,1,0:T(8,128)(2,1)S(1)}, bf16[4,128,128]{2,1,0:T(8,128)(2,1)S(1)}, u32[]{:S(2)}, u32[]{:S(2)}) %collective-permute-start.7) | collective-permute-done | bytes 131104 | tf_op jit(solution)/shard_map/ppermute | solution.py:53
  24.8 0.9 %collective-permute-done.8 = bf16[4,128,128]{2,1,0:T(8,128)(2,1)S(1)} collective-permute-done((bf16[4,128,128]{2,1,0:T(8,128)(2,1)S(1)}, bf16[4,128,128]{2,1,0:T(8,128)(2,1)S(1)}, u32[]{:S(2)}, u32[]{:S(2)}) %collective-permute-start.8) | collective-permute-done | bytes 131104 | tf_op jit(solution)/shard_map/ppermute | solution.py:53
  25.6 1.5 %collective-permute-done.9 = bf16[4,128,128]{2,1,0:T(8,128)(2,1)S(1)} collective-permute-done((bf16[4,128,128]{2,1,0:T(8,128)(2,1)S(1)}, bf16[4,128,128]{2,1,0:T(8,128)(2,1)S(1)}, u32[]{:S(2)}, u32[]{:S(2)}) %collective-permute-start.9) | collective-permute-done | bytes 131104 | tf_op jit(solution)/shard_map/ppermute | solution.py:53
  27.1 0.1 add_convert_fusion
  27.2 3.8 %collective-permute-start.10 = (bf16[4,128,128]{2,1,0:T(8,128)(2,1)S(1)}, bf16[4,128,128]{2,1,0:T(8,128)(2,1)S(1)}, u32[]{:S(2)}, u32[]{:S(2)}) collective-permute-start(bf16[4,128,128]{2,1,0:T(8,128)(2,1)S(1)} %add_convert_fusion), channel_id=1, source_target_pairs={{0,24},{1,25},{2,26},{3,27},{4,28},{5,29},{6,30},{7,31},{8,16},{9,... | collective-permute-start | bytes 393224 | tf_op jit(solution)/shard_map/ppermute | solution.py:53
  31.0 1.3 %fusion.4 = f32[729,128]{1,0:T(8,128)} fusion(f32[729,128]{1,0:T(8,128)S(1)} %fusion, f32[729,128]{1,0:T(8,128)S(1)} %fusion.2, s32[729]{0:T(1024)S(1)} %reduce, f32[729,128]{1,0:T(8,128)S(1)} %get-tuple-element.28), kind=kOutput, calls=%fused_computation.5 | convolution fusion | flops 137140208 | bytes 1495908 | tf_op jit(solution)/shard_map/dot_general | solution.py:63
  32.3 1.8 %collective-permute-done.10 = bf16[4,128,128]{2,1,0:T(8,128)(2,1)S(1)} collective-permute-done((bf16[4,128,128]{2,1,0:T(8,128)(2,1)S(1)}, bf16[4,128,128]{2,1,0:T(8,128)(2,1)S(1)}, u32[]{:S(2)}, u32[]{:S(2)}) %collective-permute-start.10) | collective-permute-done | bytes 131104 | tf_op jit(solution)/shard_map/ppermute | solution.py:53
  34.1 0.7 %add_multiply_fusion = f32[4,128,128]{2,1,0:T(8,128)} fusion(bf16[4,128,128]{2,1,0:T(8,128)(2,1)S(1)} %collective-permute-done.10, bf16[4,128,128]{2,1,0:T(8,128)(2,1)S(1)} %add_convert_fusion), kind=kLoop, calls=%fused_computation.11 | loop fusion | flops 262144 | bytes 524288 | tf_op jit(solution)/shard_map/mul | solution.py:266
  (5 shorter events, 0.1 us)
Async XLA Ops:
  0.6 6.8 %copy-start = (s32[2,81]{1,0:T(2,128)S(1)}, s32[2,81]{1,0:T(2,128)}, u32[]{:S(2)}) copy-start(s32[2,81]{1,0:T(2,128)} %faces.1) | copy-start | bytes 1948
  2.9 5.6 %collective-permute-start = (bf16[96,128]{1,0:T(8,128)(2,1)S(1)}, bf16[96,128]{1,0:T(8,128)(2,1)S(1)}, u32[]{:S(2)}, u32[]{:S(2)}) collective-permute-start(bf16[96,128]{1,0:T(8,128)(2,1)S(1)} %get-tuple-element.37), channel_id=1, source_target_pairs={{0,2},{1,3},{2,0},{3,1},{4,8},{5,9},{6,10},{7,11},{8,4},{9,5},{10,... | collective-permute-start | bytes 73736 | tf_op jit(solution)/shard_map/ppermute | solution.py:222
  5.9 3.8 %collective-permute-start.1 = (bf16[96,128]{1,0:T(8,128)(2,1)S(1)}, bf16[96,128]{1,0:T(8,128)(2,1)S(1)}, u32[]{:S(2)}, u32[]{:S(2)}) collective-permute-start(bf16[96,128]{1,0:T(8,128)(2,1)S(1)} %get-tuple-element.36), channel_id=1, source_target_pairs={{0,4},{1,5},{2,6},{3,7},{4,0},{5,1},{6,2},{7,3},{8,12},{9,13},{10,... | collective-permute-start | bytes 73736 | tf_op jit(solution)/shard_map/ppermute | solution.py:221
  9.8 5.1 %copy-start.1 = (s32[1,729]{1,0:T(1,128)S(1)}, s32[1,729]{1,0:T(1,128)}, u32[]{:S(2)}) copy-start(s32[1,729]{1,0:T(1,128)} %cell_hbm.1) | copy-start | bytes 8752
  10.0 5.6 %collective-permute-start.5 = (bf16[729,128]{1,0:T(8,128)(2,1)S(1)}, bf16[729,128]{1,0:T(8,128)(2,1)S(1)}, u32[]{:S(2)}, u32[]{:S(2)}) collective-permute-start(bf16[729,128]{1,0:T(8,128)(2,1)S(1)} %get-tuple-element.27.rest_0_), channel_id=1, source_target_pairs={{0,2},{1,3},{2,0},{3,1},{4,6},{5,7},{6,4},{7,5},{8,10},{9,11},{10,... | collective-permute-start | bytes 559880 | tf_op jit(solution)/shard_map/ppermute | solution.py:250
  11.4 4.8 %collective-permute-start.2 = (bf16[96,256]{1,0:T(8,128)(2,1)S(1)}, bf16[96,256]{1,0:T(8,128)(2,1)S(1)}, u32[]{:S(2)}, u32[]{:S(2)}) collective-permute-start(bf16[96,256]{1,0:T(8,128)(2,1)S(1)} %get-tuple-element.33), channel_id=1, source_target_pairs={{0,2},{1,3},{2,0},{3,1},{4,8},{5,9},{6,10},{7,11},{8,4},{9,5},{10,... | collective-permute-start | bytes 147464 | tf_op jit(solution)/shard_map/ppermute | solution.py:222
  12.5 4.5 %collective-permute-start.3 = (bf16[96,256]{1,0:T(8,128)(2,1)S(1)}, bf16[96,256]{1,0:T(8,128)(2,1)S(1)}, u32[]{:S(2)}, u32[]{:S(2)}) collective-permute-start(bf16[96,256]{1,0:T(8,128)(2,1)S(1)} %get-tuple-element.32), channel_id=1, source_target_pairs={{0,4},{1,5},{2,6},{3,7},{4,0},{5,1},{6,2},{7,3},{8,12},{9,13},{10,... | collective-permute-start | bytes 147464 | tf_op jit(solution)/shard_map/ppermute | solution.py:221
  14.9 2.1 %collective-permute-start.4 = (bf16[729,128]{1,0:T(8,128)(2,1)S(1)}, bf16[729,128]{1,0:T(8,128)(2,1)S(1)}, u32[]{:S(2)}, u32[]{:S(2)}) collective-permute-start(bf16[729,128]{1,0:T(8,128)(2,1)S(1)} %get-tuple-element.27.rest_0_), channel_id=1, source_target_pairs={{0,1},{1,0},{2,3},{3,2},{4,5},{5,4},{6,7},{7,6},{8,9},{9,8},{10,11... | collective-permute-start | bytes 559880 | tf_op jit(solution)/shard_map/ppermute | solution.py:250
  15.7 1.4 %collective-permute-start.6 = (bf16[729,128]{1,0:T(8,128)(2,1)S(1)}, bf16[729,128]{1,0:T(8,128)(2,1)S(1)}, u32[]{:S(2)}, u32[]{:S(2)}) collective-permute-start(bf16[729,128]{1,0:T(8,128)(2,1)S(1)} %collective-permute-done.5.rest_2_), channel_id=1, source_target_pairs={{0,1},{1,0},{2,3},{3,2},{4,5},{5,4},{6,7},{7,6},{8,9},{9,8},{10,11... | collective-permute-start | bytes 559880 | tf_op jit(solution)/shard_map/ppermute | solution.py:250
  17.7 7.1 %collective-permute-start.7 = (bf16[4,128,128]{2,1,0:T(8,128)(2,1)S(1)}, bf16[4,128,128]{2,1,0:T(8,128)(2,1)S(1)}, u32[]{:S(2)}, u32[]{:S(2)}) collective-permute-start(bf16[4,128,128]{2,1,0:T(8,128)(2,1)S(1)} %get-tuple-element.29), channel_id=1, source_target_pairs={{0,4},{1,9},{2,6},{3,11},{4,0},{5,13},{6,2},{7,15},{8,12},{9,1},{1... | collective-permute-start | bytes 393224 | tf_op jit(solution)/shard_map/ppermute | solution.py:53
  19.7 5.9 %collective-permute-start.8 = (bf16[4,128,128]{2,1,0:T(8,128)(2,1)S(1)}, bf16[4,128,128]{2,1,0:T(8,128)(2,1)S(1)}, u32[]{:S(2)}, u32[]{:S(2)}) collective-permute-start(bf16[4,128,128]{2,1,0:T(8,128)(2,1)S(1)} %get-tuple-element.29), channel_id=1, source_target_pairs={{0,8},{1,5},{2,10},{3,7},{4,12},{5,1},{6,14},{7,3},{8,0},{9,13},{1... | collective-permute-start | bytes 393224 | tf_op jit(solution)/shard_map/ppermute | solution.py:53
  21.3 5.9 %collective-permute-start.9 = (bf16[4,128,128]{2,1,0:T(8,128)(2,1)S(1)}, bf16[4,128,128]{2,1,0:T(8,128)(2,1)S(1)}, u32[]{:S(2)}, u32[]{:S(2)}) collective-permute-start(bf16[4,128,128]{2,1,0:T(8,128)(2,1)S(1)} %get-tuple-element.29), channel_id=1, source_target_pairs={{0,12},{1,13},{2,14},{3,15},{4,8},{5,9},{6,10},{7,11},{8,4},{9,5},... | collective-permute-start | bytes 393224 | tf_op jit(solution)/shard_map/ppermute | solution.py:53
  27.2 6.9 %collective-permute-start.10 = (bf16[4,128,128]{2,1,0:T(8,128)(2,1)S(1)}, bf16[4,128,128]{2,1,0:T(8,128)(2,1)S(1)}, u32[]{:S(2)}, u32[]{:S(2)}) collective-permute-start(bf16[4,128,128]{2,1,0:T(8,128)(2,1)S(1)} %add_convert_fusion), channel_id=1, source_target_pairs={{0,24},{1,25},{2,26},{3,27},{4,28},{5,29},{6,30},{7,31},{8,16},{9,... | collective-permute-start | bytes 393224 | tf_op jit(solution)/shard_map/ppermute | solution.py:53

commit v12 on v10

--- a/solution.py
+++ b/solution.py
@@ -130,28 +130,27 @@
     border[...] = both[:, width:].astype(BF16)
 
 
-def second_kernel(before, after, mine, border, start, keep, result, block):
+def second_kernel(before, after, mine, border, start, keep, result, counted, block):
     halo = 0.5 * jnp.concatenate([before[...], after[...]], axis=0).astype(F32)
     sums = mine[...] + tall_dot(lambda first, last: border[first:last], halo.astype(BF16), border.shape[0])
     result[...] = sums
-    block[...] = (sums - start[...].astype(F32) * keep[...]).astype(BF16)
+    here = sums - start[...].astype(F32) * keep[...]
+    counted[...] = here
+    block[...] = here.astype(BF16)
 
 
 def face_kernel(result, start, one, sums):
     sums[...] = dot(one[...], jnp.concatenate([result[...].astype(BF16), start[...]], axis=1)).astype(BF16)
 
 
-def third_kernel(result, start, keep, before, after, one_t, *rest):
-    blocks, (filtered, gram) = rest[:-2], rest[-2:]
-    width = result.shape[1]
+def third_kernel(counted, before, after, one_t, *rest):
+    blocks, gram = rest[:-1], rest[-1]
+    width = counted.shape[1]
     here = jnp.concatenate([before[:, :width], after[:, :width]], axis=0)
     there = jnp.concatenate([before[:, width:], jnp.zeros((after.shape[0], width), BF16)], axis=0)
     halo_in = jnp.concatenate([here, there], axis=1)
     halo = tall_dot(lambda first, last: one_t[first:last], halo_in, one_t.shape[0])
-    older = start[...].astype(F32)
-    whole = result[...] + halo[:, :width]
-    filtered[...] = whole - older
-    right = (whole - older * keep[...] - halo[:, width:]).astype(BF16)
+    right = (counted[...] + (halo[:, :width] - halo[:, width:])).astype(BF16)
     product = dot_t(right, jnp.concatenate([block[...] for block in blocks], axis=1))
     group = lax.axis_index("bands")
     for at in range(len(blocks)):
@@ -235,11 +234,11 @@
         out_specs=tuple(vmem(4)),
         compiler_params=params,
     )(columns, face_nodes, local, ham)
-    result, block = pl.pallas_call(
+    result, counted, block = pl.pallas_call(
         second_kernel,
-        out_shape=(shape(nodal, F32), shape(nodal, BF16)),
+        out_shape=(shape(nodal, F32), shape(nodal, F32), shape(nodal, BF16)),
         in_specs=vmem(6),
-        out_specs=tuple(vmem(2)),
+        out_specs=tuple(vmem(3)),
         compiler_params=params,
     )(before, after, mine, border, start, keep)
 
@@ -256,13 +255,15 @@
         compiler_params=params,
     )(result, start, one)
     before, after = neighbours(sums, chip)
-    filtered, gram = pl.pallas_call(
+    gram = pl.pallas_call(
         third_kernel,
-        out_shape=(shape(nodal, F32), shape((groups, width, width), BF16)),
-        in_specs=vmem(6 + groups),
-        out_specs=tuple(vmem(2)),
-        compiler_params=params,
-    )(result, start, keep, before, after, one_t, *(blocks[at] for at in range(groups)))
+        out_shape=shape((groups, width, width), BF16),
+        in_specs=vmem(4 + groups),
+        out_specs=vmem(1)[0],
+        compiler_params=params,
+    )(counted, before, after, one_t, *(blocks[at] for at in range(groups)))
+    gram, late_before, late_after = lax.optimization_barrier((gram, before[:, :width], after[:, :width]))
+    filtered = result + dot(one_t, jnp.concatenate([late_before, late_after])) - start.astype(F32)
     total = sum_over_cells(gram) * (1.0 / (parts * node_count))
     correlation = total.reshape(groups * width, width)
 

time: 35 us -> 35 us (level)
    dot_general x3 -> x4, matrix products: 2.27 us -> 2.54 us  [dot(): return jnp.dot(a, b, preferred_element_type=F32)]
where the time goes in v12:
time: 35 us; the launch traced here: 34.9 us
  starting transfers between devices  16.9 us (48%)
  waiting for transfers between devices  9.42 us (27%)
  Pallas kernels  4.3 us (12%)
  matrix products  2.54 us (7%)
  other arithmetic  0.87 us (2%)
  between operations  0.8 us (2%)
    ppermute x4, starting transfers between devices, sum_over_cells(): words.append(lax.ppermute(word, ('cells', 'bands'), pairs).astype(F32))  7.25 us
    ppermute x2, starting transfers between devices, neighbours(): lax.ppermute(jnp.where(odd, low, high), both, pair_swap(0, spare))  6.92 us
    ppermute x4, waiting for transfers between devices, sum_over_cells(): words.append(lax.ppermute(word, ('cells', 'bands'), pairs).astype(F32))  6.67 us
    dot_general x4, matrix products, dot(): return jnp.dot(a, b, preferred_element_type=F32)  2.54 us
    pallas_call x1, Pallas kernels, body(): pl.pallas_call(first_kernel, out_shape=(shape(nodal, BF16), shape(nodal,...  2.21 us
    ppermute x2, waiting for transfers between devices, neighbours(): lax.ppermute(jnp.where(odd, low, high), both, pair_swap(0, spare))  1.76 us
    ppermute x3, starting transfers between devices, body(): lax.ppermute(blocks[at], 'bands', turned(groups, stride, radix, radix - by))  1.68 us
    ppermute x2, starting transfers between devices, neighbours(): lax.ppermute(jnp.where(odd, high, low), both, pair_swap(1, spare))  1.08 us
  transfers between devices with their start and end apart: 11, of which 8 were waited for; matrix products, arithmetic and copies ran while one was open for 7% of the time, Pallas kernels for 4%

profile of v12, /device:TPU:0, one launch (start us, length us, event | category | flops | bytes accessed | tf_op | source)
XLA Modules:
  0.0 34.9 jit_solution(17357051166677436902)
XLA Ops:
  0.6 0.0 copy-start
  0.7 2.2 %shard_map.59 = (bf16[729,128]{1,0:T(8,128)(2,1)S(1)}, f32[729,128]{1,0:T(8,128)S(1)}, bf16[192,128]{1,0:T(8,128)(2,1)S(1)}, bf16[729,729]{1,0:T(8,128)(2,1)S(1)...) custom-call(bf16[729,128]{1,0:T(8,128)(2,1)} %waves_hbm.1, s32[1,729]{1,0:T(1,128)} %cell_hbm.1, s32[2,81]{1,0:T(2,128)} %faces.1, ...), custom_call_target="tpu_custom_call" | custom-call | tf_op jit(solution)/shard_map/pallas_call | solution.py:179
  2.9 0.5 %collective-permute-start = (bf16[96,128]{1,0:T(8,128)(2,1)S(1)}, bf16[96,128]{1,0:T(8,128)(2,1)S(1)}, u32[]{:S(2)}, u32[]{:S(2)}) collective-permute-start(bf16[96,128]{1,0:T(8,128)(2,1)S(1)} %get-tuple-element.41), channel_id=1, source_target_pairs={{0,1},{1,0},{2,3},{3,2},{4,8},{5,9},{6,10},{7,11},{8,4},{9,5},{10,... | collective-permute-start | bytes 73736 | tf_op jit(solution)/shard_map/ppermute | solution.py:221
  3.4 4.0 %collective-permute-start.1 = (bf16[96,128]{1,0:T(8,128)(2,1)S(1)}, bf16[96,128]{1,0:T(8,128)(2,1)S(1)}, u32[]{:S(2)}, u32[]{:S(2)}) collective-permute-start(bf16[96,128]{1,0:T(8,128)(2,1)S(1)} %get-tuple-element.40), channel_id=1, source_target_pairs={{0,4},{1,5},{2,6},{3,7},{4,0},{5,1},{6,2},{7,3},{8,12},{9,13},{10,... | collective-permute-start | bytes 73736 | tf_op jit(solution)/shard_map/ppermute | solution.py:220
  7.4 0.0 copy-done
  7.4 1.0 %shard_map.60 = (bf16[729,192]{1,0:T(8,128)(2,1)S(1)}, f32[729,128]{1,0:T(8,128)S(1)}, f32[729,128]{1,0:T(8,128)S(1)}, bf16[729,192]{1,0:T(8,128)(2,1)S(1)}) custom-call(f32[768,8]{1,0:T(8,128)S(1)} %get-tuple-element.19.columns, s32[2,81]{1,0:T(2,128)S(1)} %copy-done, f32[729,128]{1,0:T(8,128)S(1)} %get-tuple-element.20.local, ...), custom_call_target="tpu_custom_call" | custom-call | tf_op jit(solution)/shard_map/pallas_call | solution.py:225
  8.4 0.0 collective-permute-done
  8.4 0.8 %collective-permute-done.1 = bf16[96,128]{1,0:T(8,128)(2,1)S(1)} collective-permute-done((bf16[96,128]{1,0:T(8,128)(2,1)S(1)}, bf16[96,128]{1,0:T(8,128)(2,1)S(1)}, u32[]{:S(2)}, u32[]{:S(2)}) %collective-permute-start.1) | collective-permute-done | bytes 24608 | tf_op jit(solution)/shard_map/ppermute | solution.py:220
  9.3 0.0 copy-start.1
  9.3 0.3 shard_map.61
  9.5 1.6 %collective-permute-start.5 = (bf16[729,128]{1,0:T(8,128)(2,1)S(1)}, bf16[729,128]{1,0:T(8,128)(2,1)S(1)}, u32[]{:S(2)}, u32[]{:S(2)}) collective-permute-start(bf16[729,128]{1,0:T(8,128)(2,1)S(1)} %get-tuple-element.30.rest_0_), channel_id=1, source_target_pairs={{0,2},{1,3},{2,0},{3,1},{4,6},{5,7},{6,4},{7,5},{8,10},{9,11},{10,... | collective-permute-start | bytes 559880 | tf_op jit(solution)/shard_map/ppermute | solution.py:249
  11.1 0.3 shard_map.62
  11.4 0.6 %collective-permute-start.2 = (bf16[96,256]{1,0:T(8,128)(2,1)S(1)}, bf16[96,256]{1,0:T(8,128)(2,1)S(1)}, u32[]{:S(2)}, u32[]{:S(2)}) collective-permute-start(bf16[96,256]{1,0:T(8,128)(2,1)S(1)} %get-tuple-element.37), channel_id=1, source_target_pairs={{0,2},{1,3},{2,0},{3,1},{4,8},{5,9},{6,10},{7,11},{8,4},{9,5},{10,... | collective-permute-start | bytes 147464 | tf_op jit(solution)/shard_map/ppermute | solution.py:221
  12.0 2.9 %collective-permute-start.3 = (bf16[96,256]{1,0:T(8,128)(2,1)S(1)}, bf16[96,256]{1,0:T(8,128)(2,1)S(1)}, u32[]{:S(2)}, u32[]{:S(2)}) collective-permute-start(bf16[96,256]{1,0:T(8,128)(2,1)S(1)} %get-tuple-element.36), channel_id=1, source_target_pairs={{0,4},{1,5},{2,6},{3,7},{4,0},{5,1},{6,2},{7,3},{8,12},{9,13},{10,... | collective-permute-start | bytes 147464 | tf_op jit(solution)/shard_map/ppermute | solution.py:220
  14.9 0.0 copy-done.1
  14.9 0.1 collective-permute-start.4
  15.0 0.5 %collective-permute-done.5.rest_2_ = bf16[729,128]{1,0:T(8,128)(2,1)S(1)} collective-permute-done((bf16[729,128]{1,0:T(8,128)(2,1)S(1)}, bf16[729,128]{1,0:T(8,128)(2,1)S(1)}, u32[]{:S(2)}, u32[]{:S(2)}) %collective-permute-start.5) | collective-permute-done | bytes 186656 | tf_op jit(solution)/shard_map/ppermute | solution.py:249
  15.4 0.0 collective-permute-start.6
  15.5 0.5 %collective-permute-done.2 = bf16[96,256]{1,0:T(8,128)(2,1)S(1)} collective-permute-done((bf16[96,256]{1,0:T(8,128)(2,1)S(1)}, bf16[96,256]{1,0:T(8,128)(2,1)S(1)}, u32[]{:S(2)}, u32[]{:S(2)}) %collective-permute-start.2) | collective-permute-done | bytes 49184 | tf_op jit(solution)/shard_map/ppermute | solution.py:221
  16.0 1.0 %collective-permute-done.3 = bf16[96,256]{1,0:T(8,128)(2,1)S(1)} collective-permute-done((bf16[96,256]{1,0:T(8,128)(2,1)S(1)}, bf16[96,256]{1,0:T(8,128)(2,1)S(1)}, u32[]{:S(2)}, u32[]{:S(2)}) %collective-permute-start.3) | collective-permute-done | bytes 49184 | tf_op jit(solution)/shard_map/ppermute | solution.py:220
  17.0 0.0 collective-permute-done.4.rest_1_
  17.0 0.0 collective-permute-done.6.rest_3_
  17.0 0.6 %shard_map.63 = bf16[4,128,128]{2,1,0:T(8,128)(2,1)S(1)} custom-call(f32[729,128]{1,0:T(8,128)S(1)} %get-tuple-element.28.counted, bf16[96,256]{1,0:T(8,128)(2,1)S(1)} %get-tuple-element.35.before, bf16[96,256]{1,0:T(8,128)(2,1)S(1)} %get-tuple-element.34.after, bf16[729,192]{1,0:T(8,128)(2,1)S(1)} %get-tuple-element.27.one_t, ...), custom_call_target="tpu_custom_call" | custom-call | tf_op jit(solution)/shard_map/pallas_call | solution.py:258
  17.6 2.1 %collective-permute-start.7 = (bf16[4,128,128]{2,1,0:T(8,128)(2,1)S(1)}, bf16[4,128,128]{2,1,0:T(8,128)(2,1)S(1)}, u32[]{:S(2)}, u32[]{:S(2)}) collective-permute-start(bf16[4,128,128]{2,1,0:T(8,128)(2,1)S(1)} %shard_map.63), channel_id=1, source_target_pairs={{0,4},{1,9},{2,6},{3,11},{4,0},{5,13},{6,2},{7,15},{8,12},{9,1},{1... | collective-permute-start | bytes 393224 | tf_op jit(solution)/shard_map/ppermute | solution.py:53
  19.7 1.6 %collective-permute-start.8 = (bf16[4,128,128]{2,1,0:T(8,128)(2,1)S(1)}, bf16[4,128,128]{2,1,0:T(8,128)(2,1)S(1)}, u32[]{:S(2)}, u32[]{:S(2)}) collective-permute-start(bf16[4,128,128]{2,1,0:T(8,128)(2,1)S(1)} %shard_map.63), channel_id=1, source_target_pairs={{0,8},{1,5},{2,10},{3,7},{4,12},{5,1},{6,14},{7,3},{8,0},{9,13},{1... | collective-permute-start | bytes 393224 | tf_op jit(solution)/shard_map/ppermute | solution.py:53
  21.3 0.0 collective-permute-start.9
  21.3 0.2 fusion.5
  21.6 0.5 %fusion.1 = f32[729,128]{1,0:T(8,128)S(1)} fusion(s32[729]{0:T(1024)S(1)} %reduce, f32[729,128]{1,0:T(8,128)S(1)} %fusion.5), kind=kOutput, calls=%fused_computation.2 | convolution fusion | flops 136953584 | bytes 749412 | tf_op jit(solution)/shard_map/dot_general | solution.py:63
  22.0 0.5 %fusion.3 = f32[729,128]{1,0:T(8,128)S(1)} fusion(f32[729,128]{1,0:T(8,128)S(1)} %fusion.1, s32[729]{0:T(1024)S(1)} %reduce, f32[729,128]{1,0:T(8,128)S(1)} %fusion.5), kind=kOutput, calls=%fused_computation.5 | convolution fusion | flops 137326832 | bytes 1122660 | tf_op jit(solution)/shard_map/dot_general | solution.py:63
  22.6 2.4 %collective-permute-done.7 = bf16[4,128,128]{2,1,0:T(8,128)(2,1)S(1)} collective-permute-done((bf16[4,128,128]{2,1,0:T(8,128)(2,1)S(1)}, bf16[4,128,128]{2,1,0:T(8,128)(2,1)S(1)}, u32[]{:S(2)}, u32[]{:S(2)}) %collective-permute-start.7) | collective-permute-done | bytes 131104 | tf_op jit(solution)/shard_map/ppermute | solution.py:53
  24.9 0.7 %collective-permute-done.8 = bf16[4,128,128]{2,1,0:T(8,128)(2,1)S(1)} collective-permute-done((bf16[4,128,128]{2,1,0:T(8,128)(2,1)S(1)}, bf16[4,128,128]{2,1,0:T(8,128)(2,1)S(1)}, u32[]{:S(2)}, u32[]{:S(2)}) %collective-permute-start.8) | collective-permute-done | bytes 131104 | tf_op jit(solution)/shard_map/ppermute | solution.py:53
  25.6 1.5 %collective-permute-done.9 = bf16[4,128,128]{2,1,0:T(8,128)(2,1)S(1)} collective-permute-done((bf16[4,128,128]{2,1,0:T(8,128)(2,1)S(1)}, bf16[4,128,128]{2,1,0:T(8,128)(2,1)S(1)}, u32[]{:S(2)}, u32[]{:S(2)}) %collective-permute-start.9) | collective-permute-done | bytes 131104 | tf_op jit(solution)/shard_map/ppermute | solution.py:53
  27.2 0.1 add_convert_fusion
  27.2 3.5 %collective-permute-start.10 = (bf16[4,128,128]{2,1,0:T(8,128)(2,1)S(1)}, bf16[4,128,128]{2,1,0:T(8,128)(2,1)S(1)}, u32[]{:S(2)}, u32[]{:S(2)}) collective-permute-start(bf16[4,128,128]{2,1,0:T(8,128)(2,1)S(1)} %add_convert_fusion), channel_id=1, source_target_pairs={{0,24},{1,25},{2,26},{3,27},{4,28},{5,29},{6,30},{7,31},{8,16},{9,... | collective-permute-start | bytes 393224 | tf_op jit(solution)/shard_map/ppermute | solution.py:53
  30.8 1.3 %fusion.4 = f32[729,128]{1,0:T(8,128)} fusion(f32[729,128]{1,0:T(8,128)S(1)} %fusion.3, s32[729]{0:T(1024)S(1)} %reduce, f32[729,128]{1,0:T(8,128)S(1)} %fusion.5), kind=kOutput, calls=%fused_computation.6 | convolution fusion | flops 136766960 | bytes 1122660 | tf_op jit(solution)/shard_map/dot_general | solution.py:63
  32.0 2.1 %collective-permute-done.10 = bf16[4,128,128]{2,1,0:T(8,128)(2,1)S(1)} collective-permute-done((bf16[4,128,128]{2,1,0:T(8,128)(2,1)S(1)}, bf16[4,128,128]{2,1,0:T(8,128)(2,1)S(1)}, u32[]{:S(2)}, u32[]{:S(2)}) %collective-permute-start.10) | collective-permute-done | bytes 131104 | tf_op jit(solution)/shard_map/ppermute | solution.py:53
  34.1 0.7 %add_multiply_fusion = f32[4,128,128]{2,1,0:T(8,128)} fusion(bf16[4,128,128]{2,1,0:T(8,128)(2,1)S(1)} %collective-permute-done.10, bf16[4,128,128]{2,1,0:T(8,128)(2,1)S(1)} %add_convert_fusion), kind=kLoop, calls=%fused_computation.13 | loop fusion | flops 262144 | bytes 524288 | tf_op jit(solution)/shard_map/mul | solution.py:267
  (7 shorter events, 0.1 us)
Async XLA Ops:
  0.6 6.8 %copy-start = (s32[2,81]{1,0:T(2,128)S(1)}, s32[2,81]{1,0:T(2,128)}, u32[]{:S(2)}) copy-start(s32[2,81]{1,0:T(2,128)} %faces.1) | copy-start | bytes 1948
  2.9 5.6 %collective-permute-start = (bf16[96,128]{1,0:T(8,128)(2,1)S(1)}, bf16[96,128]{1,0:T(8,128)(2,1)S(1)}, u32[]{:S(2)}, u32[]{:S(2)}) collective-permute-start(bf16[96,128]{1,0:T(8,128)(2,1)S(1)} %get-tuple-element.41), channel_id=1, source_target_pairs={{0,1},{1,0},{2,3},{3,2},{4,8},{5,9},{6,10},{7,11},{8,4},{9,5},{10,... | collective-permute-start | bytes 73736 | tf_op jit(solution)/shard_map/ppermute | solution.py:221
  3.4 5.8 %collective-permute-start.1 = (bf16[96,128]{1,0:T(8,128)(2,1)S(1)}, bf16[96,128]{1,0:T(8,128)(2,1)S(1)}, u32[]{:S(2)}, u32[]{:S(2)}) collective-permute-start(bf16[96,128]{1,0:T(8,128)(2,1)S(1)} %get-tuple-element.40), channel_id=1, source_target_pairs={{0,4},{1,5},{2,6},{3,7},{4,0},{5,1},{6,2},{7,3},{8,12},{9,13},{10,... | collective-permute-start | bytes 73736 | tf_op jit(solution)/shard_map/ppermute | solution.py:220
  9.3 5.6 %copy-start.1 = (s32[1,729]{1,0:T(1,128)S(1)}, s32[1,729]{1,0:T(1,128)}, u32[]{:S(2)}) copy-start(s32[1,729]{1,0:T(1,128)} %cell_hbm.1) | copy-start | bytes 8752
  9.5 5.9 %collective-permute-start.5 = (bf16[729,128]{1,0:T(8,128)(2,1)S(1)}, bf16[729,128]{1,0:T(8,128)(2,1)S(1)}, u32[]{:S(2)}, u32[]{:S(2)}) collective-permute-start(bf16[729,128]{1,0:T(8,128)(2,1)S(1)} %get-tuple-element.30.rest_0_), channel_id=1, source_target_pairs={{0,2},{1,3},{2,0},{3,1},{4,6},{5,7},{6,4},{7,5},{8,10},{9,11},{10,... | collective-permute-start | bytes 559880 | tf_op jit(solution)/shard_map/ppermute | solution.py:249
  11.4 4.6 %collective-permute-start.2 = (bf16[96,256]{1,0:T(8,128)(2,1)S(1)}, bf16[96,256]{1,0:T(8,128)(2,1)S(1)}, u32[]{:S(2)}, u32[]{:S(2)}) collective-permute-start(bf16[96,256]{1,0:T(8,128)(2,1)S(1)} %get-tuple-element.37), channel_id=1, source_target_pairs={{0,2},{1,3},{2,0},{3,1},{4,8},{5,9},{6,10},{7,11},{8,4},{9,5},{10,... | collective-permute-start | bytes 147464 | tf_op jit(solution)/shard_map/ppermute | solution.py:221
  12.0 4.9 %collective-permute-start.3 = (bf16[96,256]{1,0:T(8,128)(2,1)S(1)}, bf16[96,256]{1,0:T(8,128)(2,1)S(1)}, u32[]{:S(2)}, u32[]{:S(2)}) collective-permute-start(bf16[96,256]{1,0:T(8,128)(2,1)S(1)} %get-tuple-element.36), channel_id=1, source_target_pairs={{0,4},{1,5},{2,6},{3,7},{4,0},{5,1},{6,2},{7,3},{8,12},{9,13},{10,... | collective-permute-start | bytes 147464 | tf_op jit(solution)/shard_map/ppermute | solution.py:220
  14.9 2.1 %collective-permute-start.4 = (bf16[729,128]{1,0:T(8,128)(2,1)S(1)}, bf16[729,128]{1,0:T(8,128)(2,1)S(1)}, u32[]{:S(2)}, u32[]{:S(2)}) collective-permute-start(bf16[729,128]{1,0:T(8,128)(2,1)S(1)} %get-tuple-element.30.rest_0_), channel_id=1, source_target_pairs={{0,1},{1,0},{2,3},{3,2},{4,5},{5,4},{6,7},{7,6},{8,9},{9,8},{10,11... | collective-permute-start | bytes 559880 | tf_op jit(solution)/shard_map/ppermute | solution.py:249
  15.4 1.5 %collective-permute-start.6 = (bf16[729,128]{1,0:T(8,128)(2,1)S(1)}, bf16[729,128]{1,0:T(8,128)(2,1)S(1)}, u32[]{:S(2)}, u32[]{:S(2)}) collective-permute-start(bf16[729,128]{1,0:T(8,128)(2,1)S(1)} %collective-permute-done.5.rest_2_), channel_id=1, source_target_pairs={{0,1},{1,0},{2,3},{3,2},{4,5},{5,4},{6,7},{7,6},{8,9},{9,8},{10,11... | collective-permute-start | bytes 559880 | tf_op jit(solution)/shard_map/ppermute | solution.py:249
  17.6 7.4 %collective-permute-start.7 = (bf16[4,128,128]{2,1,0:T(8,128)(2,1)S(1)}, bf16[4,128,128]{2,1,0:T(8,128)(2,1)S(1)}, u32[]{:S(2)}, u32[]{:S(2)}) collective-permute-start(bf16[4,128,128]{2,1,0:T(8,128)(2,1)S(1)} %shard_map.63), channel_id=1, source_target_pairs={{0,4},{1,9},{2,6},{3,11},{4,0},{5,13},{6,2},{7,15},{8,12},{9,1},{1... | collective-permute-start | bytes 393224 | tf_op jit(solution)/shard_map/ppermute | solution.py:53
  19.7 5.9 %collective-permute-start.8 = (bf16[4,128,128]{2,1,0:T(8,128)(2,1)S(1)}, bf16[4,128,128]{2,1,0:T(8,128)(2,1)S(1)}, u32[]{:S(2)}, u32[]{:S(2)}) collective-permute-start(bf16[4,128,128]{2,1,0:T(8,128)(2,1)S(1)} %shard_map.63), channel_id=1, source_target_pairs={{0,8},{1,5},{2,10},{3,7},{4,12},{5,1},{6,14},{7,3},{8,0},{9,13},{1... | collective-permute-start | bytes 393224 | tf_op jit(solution)/shard_map/ppermute | solution.py:53
  21.3 5.9 %collective-permute-start.9 = (bf16[4,128,128]{2,1,0:T(8,128)(2,1)S(1)}, bf16[4,128,128]{2,1,0:T(8,128)(2,1)S(1)}, u32[]{:S(2)}, u32[]{:S(2)}) collective-permute-start(bf16[4,128,128]{2,1,0:T(8,128)(2,1)S(1)} %shard_map.63), channel_id=1, source_target_pairs={{0,12},{1,13},{2,14},{3,15},{4,8},{5,9},{6,10},{7,11},{8,4},{9,5},... | collective-permute-start | bytes 393224 | tf_op jit(solution)/shard_map/ppermute | solution.py:53
  27.2 6.9 %collective-permute-start.10 = (bf16[4,128,128]{2,1,0:T(8,128)(2,1)S(1)}, bf16[4,128,128]{2,1,0:T(8,128)(2,1)S(1)}, u32[]{:S(2)}, u32[]{:S(2)}) collective-permute-start(bf16[4,128,128]{2,1,0:T(8,128)(2,1)S(1)} %add_convert_fusion), channel_id=1, source_target_pairs={{0,24},{1,25},{2,26},{3,27},{4,28},{5,29},{6,30},{7,31},{8,16},{9,... | collective-permute-start | bytes 393224 | tf_op jit(solution)/shard_map/ppermute | solution.py:53

commit v13 on v9

--- a/solution.py
+++ b/solution.py
@@ -36,7 +36,7 @@
     steps = []
     if len(masks) >= 2:
         first, second = masks[:2]
-        steps.append([(first, second), (second, first), (first ^ second, first ^ second)])
+        steps.append([(first, first ^ second), (second, first), (first ^ second, second)])
         masks = masks[2:]
     steps += [[(mask, mask)] for mask in masks]
     steps = [[lambda part, band, m=m: part ^ m[band % 2] for m in step] for step in steps]

time: 35 us -> 35.1 us (level)
  no operation moved by 1% of the time
where the time goes in v13:
time: 35.1 us; the launch traced here: 34.9 us
  starting transfers between devices  16.3 us (46%)
  waiting for transfers between devices  10.4 us (30%)
  Pallas kernels  4.3 us (12%)
  matrix products  2.27 us (6%)
  other arithmetic  0.87 us (2%)
  between operations  0.77 us (2%)
    ppermute x4, starting transfers between devices, sum_over_cells(): words.append(lax.ppermute(word, ('cells', 'bands'), pairs).astype(F32))  7.13 us
    ppermute x4, waiting for transfers between devices, sum_over_cells(): words.append(lax.ppermute(word, ('cells', 'bands'), pairs).astype(F32))  6.96 us
    ppermute x2, starting transfers between devices, neighbours(): odd_even = lax.ppermute(jnp.where(odd, high, low), both, pair_swap(1))  4.1 us
    ppermute x2, starting transfers between devices, neighbours(): even_odd = lax.ppermute(jnp.where(odd, low, high), both, pair_swap(0))  3.9 us
    dot_general x3, matrix products, dot(): return jnp.dot(a, b, preferred_element_type=F32)  2.27 us
    pallas_call x1, Pallas kernels, body(): pl.pallas_call(first_kernel, out_shape=(shape(nodal, BF16), shape(nodal,...  2.21 us
    ppermute x2, waiting for transfers between devices, neighbours(): even_odd = lax.ppermute(jnp.where(odd, low, high), both, pair_swap(0))  2.02 us
    ppermute x3, starting transfers between devices, body(): lax.ppermute(blocks[at], 'bands', turned(groups, stride, radix, radix - by))  1.16 us
  transfers between devices with their start and end apart: 11, of which 9 were waited for; matrix products, arithmetic and copies ran while one was open for 7% of the time, Pallas kernels for 4%

profile of v13, /device:TPU:0, one launch (start us, length us, event | category | flops | bytes accessed | tf_op | source)
XLA Modules:
  0.0 34.9 jit_solution(18286506408944349977)
XLA Ops:
  0.6 0.0 copy-start
  0.7 2.2 %shard_map.59 = (bf16[729,128]{1,0:T(8,128)(2,1)S(1)}, f32[729,128]{1,0:T(8,128)S(1)}, bf16[192,128]{1,0:T(8,128)(2,1)S(1)}, bf16[729,729]{1,0:T(8,128)(2,1)S(1)...) custom-call(bf16[729,128]{1,0:T(8,128)(2,1)} %waves_hbm.1, s32[1,729]{1,0:T(1,128)} %cell_hbm.1, s32[2,81]{1,0:T(2,128)} %faces.1, ...), custom_call_target="tpu_custom_call" | custom-call | tf_op jit(solution)/shard_map/pallas_call | solution.py:180
  2.9 3.0 %collective-permute-start = (bf16[96,128]{1,0:T(8,128)(2,1)S(1)}, bf16[96,128]{1,0:T(8,128)(2,1)S(1)}, u32[]{:S(2)}, u32[]{:S(2)}) collective-permute-start(bf16[96,128]{1,0:T(8,128)(2,1)S(1)} %get-tuple-element.37), channel_id=1, source_target_pairs={{0,2},{1,3},{2,0},{3,1},{4,8},{5,9},{6,10},{7,11},{8,4},{9,5},{10,... | collective-permute-start | bytes 73736 | tf_op jit(solution)/shard_map/ppermute | solution.py:222
  5.9 1.5 %collective-permute-start.1 = (bf16[96,128]{1,0:T(8,128)(2,1)S(1)}, bf16[96,128]{1,0:T(8,128)(2,1)S(1)}, u32[]{:S(2)}, u32[]{:S(2)}) collective-permute-start(bf16[96,128]{1,0:T(8,128)(2,1)S(1)} %get-tuple-element.36), channel_id=1, source_target_pairs={{0,4},{1,5},{2,6},{3,7},{4,0},{5,1},{6,2},{7,3},{8,12},{9,13},{10,... | collective-permute-start | bytes 73736 | tf_op jit(solution)/shard_map/ppermute | solution.py:221
  7.4 0.0 copy-done
  7.4 1.0 %shard_map.60 = (bf16[729,192]{1,0:T(8,128)(2,1)S(1)}, f32[729,128]{1,0:T(8,128)S(1)}, f32[729,128]{1,0:T(8,128)S(1)}, bf16[729,192]{1,0:T(8,128)(2,1)S(1)}) custom-call(f32[768,8]{1,0:T(8,128)S(1)} %get-tuple-element.17.columns, s32[2,81]{1,0:T(2,128)S(1)} %copy-done, f32[729,128]{1,0:T(8,128)S(1)} %get-tuple-element.18.local, ...), custom_call_target="tpu_custom_call" | custom-call | tf_op jit(solution)/shard_map/pallas_call | solution.py:226
  8.4 0.0 collective-permute-done
  8.5 1.3 %collective-permute-done.1 = bf16[96,128]{1,0:T(8,128)(2,1)S(1)} collective-permute-done((bf16[96,128]{1,0:T(8,128)(2,1)S(1)}, bf16[96,128]{1,0:T(8,128)(2,1)S(1)}, u32[]{:S(2)}, u32[]{:S(2)}) %collective-permute-start.1) | collective-permute-done | bytes 24608 | tf_op jit(solution)/shard_map/ppermute | solution.py:221
  9.8 0.0 copy-start.1
  9.8 0.3 shard_map.61
  10.0 1.1 %collective-permute-start.5 = (bf16[729,128]{1,0:T(8,128)(2,1)S(1)}, bf16[729,128]{1,0:T(8,128)(2,1)S(1)}, u32[]{:S(2)}, u32[]{:S(2)}) collective-permute-start(bf16[729,128]{1,0:T(8,128)(2,1)S(1)} %get-tuple-element.27.rest_0_), channel_id=1, source_target_pairs={{0,2},{1,3},{2,0},{3,1},{4,6},{5,7},{6,4},{7,5},{8,10},{9,11},{10,... | collective-permute-start | bytes 559880 | tf_op jit(solution)/shard_map/ppermute | solution.py:250
  11.1 0.3 shard_map.62
  11.4 1.1 %collective-permute-start.2 = (bf16[96,256]{1,0:T(8,128)(2,1)S(1)}, bf16[96,256]{1,0:T(8,128)(2,1)S(1)}, u32[]{:S(2)}, u32[]{:S(2)}) collective-permute-start(bf16[96,256]{1,0:T(8,128)(2,1)S(1)} %get-tuple-element.33), channel_id=1, source_target_pairs={{0,2},{1,3},{2,0},{3,1},{4,8},{5,9},{6,10},{7,11},{8,4},{9,5},{10,... | collective-permute-start | bytes 147464 | tf_op jit(solution)/shard_map/ppermute | solution.py:222
  12.5 2.4 %collective-permute-start.3 = (bf16[96,256]{1,0:T(8,128)(2,1)S(1)}, bf16[96,256]{1,0:T(8,128)(2,1)S(1)}, u32[]{:S(2)}, u32[]{:S(2)}) collective-permute-start(bf16[96,256]{1,0:T(8,128)(2,1)S(1)} %get-tuple-element.32), channel_id=1, source_target_pairs={{0,4},{1,5},{2,6},{3,7},{4,0},{5,1},{6,2},{7,3},{8,12},{9,13},{10,... | collective-permute-start | bytes 147464 | tf_op jit(solution)/shard_map/ppermute | solution.py:221
  14.9 0.0 copy-done.1
  14.9 0.1 collective-permute-start.4
  15.0 0.7 %collective-permute-done.5.rest_2_ = bf16[729,128]{1,0:T(8,128)(2,1)S(1)} collective-permute-done((bf16[729,128]{1,0:T(8,128)(2,1)S(1)}, bf16[729,128]{1,0:T(8,128)(2,1)S(1)}, u32[]{:S(2)}, u32[]{:S(2)}) %collective-permute-start.5) | collective-permute-done | bytes 186656 | tf_op jit(solution)/shard_map/ppermute | solution.py:250
  15.7 0.0 collective-permute-start.6
  15.7 0.5 %collective-permute-done.2 = bf16[96,256]{1,0:T(8,128)(2,1)S(1)} collective-permute-done((bf16[96,256]{1,0:T(8,128)(2,1)S(1)}, bf16[96,256]{1,0:T(8,128)(2,1)S(1)}, u32[]{:S(2)}, u32[]{:S(2)}) %collective-permute-start.2) | collective-permute-done | bytes 49184 | tf_op jit(solution)/shard_map/ppermute | solution.py:222
  16.2 0.7 %collective-permute-done.3 = bf16[96,256]{1,0:T(8,128)(2,1)S(1)} collective-permute-done((bf16[96,256]{1,0:T(8,128)(2,1)S(1)}, bf16[96,256]{1,0:T(8,128)(2,1)S(1)}, u32[]{:S(2)}, u32[]{:S(2)}) %collective-permute-start.3) | collective-permute-done | bytes 49184 | tf_op jit(solution)/shard_map/ppermute | solution.py:221
  16.9 0.0 collective-permute-done.4.rest_1_
  17.0 0.2 collective-permute-done.6.rest_3_
  17.1 0.6 %shard_map.63 = (f32[729,128]{1,0:T(8,128)S(1)}, bf16[4,128,128]{2,1,0:T(8,128)(2,1)S(1)}) custom-call(f32[729,128]{1,0:T(8,128)S(1)} %get-tuple-element.24.result, bf16[729,128]{1,0:T(8,128)(2,1)S(1)} %get-tuple-element.22.start, f32[729,128]{1,0:T(8,128)S(1)} %get-tuple-element.23.keep, bf16[96,256]{1,0:T(8,128)(2,1)S(1)} %get-tuple-element.31.before, ...), custom_call_target="tpu_custom_call" | custom-call | tf_op jit(solution)/shard_map/pallas_call | solution.py:259
  17.7 2.0 %collective-permute-start.7 = (bf16[4,128,128]{2,1,0:T(8,128)(2,1)S(1)}, bf16[4,128,128]{2,1,0:T(8,128)(2,1)S(1)}, u32[]{:S(2)}, u32[]{:S(2)}) collective-permute-start(bf16[4,128,128]{2,1,0:T(8,128)(2,1)S(1)} %get-tuple-element.29), channel_id=1, source_target_pairs={{0,4},{1,13},{2,6},{3,15},{4,0},{5,9},{6,2},{7,11},{8,12},{9,5},{1... | collective-permute-start | bytes 393224 | tf_op jit(solution)/shard_map/ppermute | solution.py:53
  19.7 1.6 %collective-permute-start.8 = (bf16[4,128,128]{2,1,0:T(8,128)(2,1)S(1)}, bf16[4,128,128]{2,1,0:T(8,128)(2,1)S(1)}, u32[]{:S(2)}, u32[]{:S(2)}) collective-permute-start(bf16[4,128,128]{2,1,0:T(8,128)(2,1)S(1)} %get-tuple-element.29), channel_id=1, source_target_pairs={{0,8},{1,5},{2,10},{3,7},{4,12},{5,1},{6,14},{7,3},{8,0},{9,13},{1... | collective-permute-start | bytes 393224 | tf_op jit(solution)/shard_map/ppermute | solution.py:53
  21.3 0.0 collective-permute-start.9
  21.3 0.5 %fusion.2 = f32[729,128]{1,0:T(8,128)S(1)} fusion(s32[729]{0:T(1024)S(1)} %reduce, f32[729,128]{1,0:T(8,128)S(1)} %get-tuple-element.28), kind=kOutput, calls=%fused_computation.3 | convolution fusion | flops 137233520 | bytes 749412 | tf_op jit(solution)/shard_map/dot_general | solution.py:63
  21.8 0.5 %fusion = f32[729,128]{1,0:T(8,128)S(1)} fusion(s32[729]{0:T(1024)S(1)} %reduce, f32[729,128]{1,0:T(8,128)S(1)} %get-tuple-element.28), kind=kOutput, calls=%fused_computation.1 | convolution fusion | flops 136673648 | bytes 749412 | tf_op jit(solution)/shard_map/dot_general | solution.py:63
  22.3 3.1 %collective-permute-done.7 = bf16[4,128,128]{2,1,0:T(8,128)(2,1)S(1)} collective-permute-done((bf16[4,128,128]{2,1,0:T(8,128)(2,1)S(1)}, bf16[4,128,128]{2,1,0:T(8,128)(2,1)S(1)}, u32[]{:S(2)}, u32[]{:S(2)}) %collective-permute-start.7) | collective-permute-done | bytes 131104 | tf_op jit(solution)/shard_map/ppermute | solution.py:53
  25.4 0.3 collective-permute-done.8
  25.7 1.5 %collective-permute-done.9 = bf16[4,128,128]{2,1,0:T(8,128)(2,1)S(1)} collective-permute-done((bf16[4,128,128]{2,1,0:T(8,128)(2,1)S(1)}, bf16[4,128,128]{2,1,0:T(8,128)(2,1)S(1)}, u32[]{:S(2)}, u32[]{:S(2)}) %collective-permute-start.9) | collective-permute-done | bytes 131104 | tf_op jit(solution)/shard_map/ppermute | solution.py:53
  27.1 0.1 add_convert_fusion
  27.2 3.6 %collective-permute-start.10 = (bf16[4,128,128]{2,1,0:T(8,128)(2,1)S(1)}, bf16[4,128,128]{2,1,0:T(8,128)(2,1)S(1)}, u32[]{:S(2)}, u32[]{:S(2)}) collective-permute-start(bf16[4,128,128]{2,1,0:T(8,128)(2,1)S(1)} %add_convert_fusion), channel_id=1, source_target_pairs={{0,24},{1,25},{2,26},{3,27},{4,28},{5,29},{6,30},{7,31},{8,16},{9,... | collective-permute-start | bytes 393224 | tf_op jit(solution)/shard_map/ppermute | solution.py:53
  30.8 1.3 %fusion.4 = f32[729,128]{1,0:T(8,128)} fusion(f32[729,128]{1,0:T(8,128)S(1)} %fusion, f32[729,128]{1,0:T(8,128)S(1)} %fusion.2, s32[729]{0:T(1024)S(1)} %reduce, f32[729,128]{1,0:T(8,128)S(1)} %get-tuple-element.28), kind=kOutput, calls=%fused_computation.5 | convolution fusion | flops 137140208 | bytes 1495908 | tf_op jit(solution)/shard_map/dot_general | solution.py:63
  32.1 2.1 %collective-permute-done.10 = bf16[4,128,128]{2,1,0:T(8,128)(2,1)S(1)} collective-permute-done((bf16[4,128,128]{2,1,0:T(8,128)(2,1)S(1)}, bf16[4,128,128]{2,1,0:T(8,128)(2,1)S(1)}, u32[]{:S(2)}, u32[]{:S(2)}) %collective-permute-start.10) | collective-permute-done | bytes 131104 | tf_op jit(solution)/shard_map/ppermute | solution.py:53
  34.2 0.7 %add_multiply_fusion = f32[4,128,128]{2,1,0:T(8,128)} fusion(bf16[4,128,128]{2,1,0:T(8,128)(2,1)S(1)} %collective-permute-done.10, bf16[4,128,128]{2,1,0:T(8,128)(2,1)S(1)} %add_convert_fusion), kind=kLoop, calls=%fused_computation.11 | loop fusion | flops 262144 | bytes 524288 | tf_op jit(solution)/shard_map/mul | solution.py:266
  (5 shorter events, 0.1 us)
Async XLA Ops:
  0.6 6.8 %copy-start = (s32[2,81]{1,0:T(2,128)S(1)}, s32[2,81]{1,0:T(2,128)}, u32[]{:S(2)}) copy-start(s32[2,81]{1,0:T(2,128)} %faces.1) | copy-start | bytes 1948
  2.9 5.6 %collective-permute-start = (bf16[96,128]{1,0:T(8,128)(2,1)S(1)}, bf16[96,128]{1,0:T(8,128)(2,1)S(1)}, u32[]{:S(2)}, u32[]{:S(2)}) collective-permute-start(bf16[96,128]{1,0:T(8,128)(2,1)S(1)} %get-tuple-element.37), channel_id=1, source_target_pairs={{0,2},{1,3},{2,0},{3,1},{4,8},{5,9},{6,10},{7,11},{8,4},{9,5},{10,... | collective-permute-start | bytes 73736 | tf_op jit(solution)/shard_map/ppermute | solution.py:222
  5.9 3.8 %collective-permute-start.1 = (bf16[96,128]{1,0:T(8,128)(2,1)S(1)}, bf16[96,128]{1,0:T(8,128)(2,1)S(1)}, u32[]{:S(2)}, u32[]{:S(2)}) collective-permute-start(bf16[96,128]{1,0:T(8,128)(2,1)S(1)} %get-tuple-element.36), channel_id=1, source_target_pairs={{0,4},{1,5},{2,6},{3,7},{4,0},{5,1},{6,2},{7,3},{8,12},{9,13},{10,... | collective-permute-start | bytes 73736 | tf_op jit(solution)/shard_map/ppermute | solution.py:221
  9.8 5.1 %copy-start.1 = (s32[1,729]{1,0:T(1,128)S(1)}, s32[1,729]{1,0:T(1,128)}, u32[]{:S(2)}) copy-start(s32[1,729]{1,0:T(1,128)} %cell_hbm.1) | copy-start | bytes 8752
  10.0 5.6 %collective-permute-start.5 = (bf16[729,128]{1,0:T(8,128)(2,1)S(1)}, bf16[729,128]{1,0:T(8,128)(2,1)S(1)}, u32[]{:S(2)}, u32[]{:S(2)}) collective-permute-start(bf16[729,128]{1,0:T(8,128)(2,1)S(1)} %get-tuple-element.27.rest_0_), channel_id=1, source_target_pairs={{0,2},{1,3},{2,0},{3,1},{4,6},{5,7},{6,4},{7,5},{8,10},{9,11},{10,... | collective-permute-start | bytes 559880 | tf_op jit(solution)/shard_map/ppermute | solution.py:250
  11.4 4.8 %collective-permute-start.2 = (bf16[96,256]{1,0:T(8,128)(2,1)S(1)}, bf16[96,256]{1,0:T(8,128)(2,1)S(1)}, u32[]{:S(2)}, u32[]{:S(2)}) collective-permute-start(bf16[96,256]{1,0:T(8,128)(2,1)S(1)} %get-tuple-element.33), channel_id=1, source_target_pairs={{0,2},{1,3},{2,0},{3,1},{4,8},{5,9},{6,10},{7,11},{8,4},{9,5},{10,... | collective-permute-start | bytes 147464 | tf_op jit(solution)/shard_map/ppermute | solution.py:222
  12.5 4.5 %collective-permute-start.3 = (bf16[96,256]{1,0:T(8,128)(2,1)S(1)}, bf16[96,256]{1,0:T(8,128)(2,1)S(1)}, u32[]{:S(2)}, u32[]{:S(2)}) collective-permute-start(bf16[96,256]{1,0:T(8,128)(2,1)S(1)} %get-tuple-element.32), channel_id=1, source_target_pairs={{0,4},{1,5},{2,6},{3,7},{4,0},{5,1},{6,2},{7,3},{8,12},{9,13},{10,... | collective-permute-start | bytes 147464 | tf_op jit(solution)/shard_map/ppermute | solution.py:221
  14.9 2.1 %collective-permute-start.4 = (bf16[729,128]{1,0:T(8,128)(2,1)S(1)}, bf16[729,128]{1,0:T(8,128)(2,1)S(1)}, u32[]{:S(2)}, u32[]{:S(2)}) collective-permute-start(bf16[729,128]{1,0:T(8,128)(2,1)S(1)} %get-tuple-element.27.rest_0_), channel_id=1, source_target_pairs={{0,1},{1,0},{2,3},{3,2},{4,5},{5,4},{6,7},{7,6},{8,9},{9,8},{10,11... | collective-permute-start | bytes 559880 | tf_op jit(solution)/shard_map/ppermute | solution.py:250
  15.7 1.4 %collective-permute-start.6 = (bf16[729,128]{1,0:T(8,128)(2,1)S(1)}, bf16[729,128]{1,0:T(8,128)(2,1)S(1)}, u32[]{:S(2)}, u32[]{:S(2)}) collective-permute-start(bf16[729,128]{1,0:T(8,128)(2,1)S(1)} %collective-permute-done.5.rest_2_), channel_id=1, source_target_pairs={{0,1},{1,0},{2,3},{3,2},{4,5},{5,4},{6,7},{7,6},{8,9},{9,8},{10,11... | collective-permute-start | bytes 559880 | tf_op jit(solution)/shard_map/ppermute | solution.py:250
  17.7 7.7 %collective-permute-start.7 = (bf16[4,128,128]{2,1,0:T(8,128)(2,1)S(1)}, bf16[4,128,128]{2,1,0:T(8,128)(2,1)S(1)}, u32[]{:S(2)}, u32[]{:S(2)}) collective-permute-start(bf16[4,128,128]{2,1,0:T(8,128)(2,1)S(1)} %get-tuple-element.29), channel_id=1, source_target_pairs={{0,4},{1,13},{2,6},{3,15},{4,0},{5,9},{6,2},{7,11},{8,12},{9,5},{1... | collective-permute-start | bytes 393224 | tf_op jit(solution)/shard_map/ppermute | solution.py:53
  19.7 6.0 %collective-permute-start.8 = (bf16[4,128,128]{2,1,0:T(8,128)(2,1)S(1)}, bf16[4,128,128]{2,1,0:T(8,128)(2,1)S(1)}, u32[]{:S(2)}, u32[]{:S(2)}) collective-permute-start(bf16[4,128,128]{2,1,0:T(8,128)(2,1)S(1)} %get-tuple-element.29), channel_id=1, source_target_pairs={{0,8},{1,5},{2,10},{3,7},{4,12},{5,1},{6,14},{7,3},{8,0},{9,13},{1... | collective-permute-start | bytes 393224 | tf_op jit(solution)/shard_map/ppermute | solution.py:53
  21.3 5.9 %collective-permute-start.9 = (bf16[4,128,128]{2,1,0:T(8,128)(2,1)S(1)}, bf16[4,128,128]{2,1,0:T(8,128)(2,1)S(1)}, u32[]{:S(2)}, u32[]{:S(2)}) collective-permute-start(bf16[4,128,128]{2,1,0:T(8,128)(2,1)S(1)} %get-tuple-element.29), channel_id=1, source_target_pairs={{0,12},{1,9},{2,14},{3,11},{4,8},{5,13},{6,10},{7,15},{8,4},{9,1},... | collective-permute-start | bytes 393224 | tf_op jit(solution)/shard_map/ppermute | solution.py:53
  27.2 6.9 %collective-permute-start.10 = (bf16[4,128,128]{2,1,0:T(8,128)(2,1)S(1)}, bf16[4,128,128]{2,1,0:T(8,128)(2,1)S(1)}, u32[]{:S(2)}, u32[]{:S(2)}) collective-permute-start(bf16[4,128,128]{2,1,0:T(8,128)(2,1)S(1)} %add_convert_fusion), channel_id=1, source_target_pairs={{0,24},{1,25},{2,26},{3,27},{4,28},{5,29},{6,30},{7,31},{8,16},{9,... | collective-permute-start | bytes 393224 | tf_op jit(solution)/shard_map/ppermute | solution.py:53
